TPU v7x, 32 devices: a whole 2x2x4 slice. The times are simulated.
32 devices in a mesh: band: 8 (over y, x, core), spec: 4 (over z).
Axes of the slice: x: 2, y: 2, z: 4, core: 2. Of those that a mesh axis runs over, the one named last changes fastest.
Arguments:
- spectra: float32 [1296, 16, 512], P(None, 'band', 'spec'), may hold values from 0.05 to 2
- sea_mask: int32 [16, 512], P('band', 'spec'), may hold values 0 or 1
- wind: float32 [2, 16, 512], P(None, None, ('spec', 'band')), may hold values from -30 to 30
- current: float32 [2, 16, 512], P(None, None, ('spec', 'band')), may hold values from -0.2 to 0.2
Outputs:
- spectra_next: float32 [1296, 16, 512], P(None, 'band', 'spec')
All inputs are finite; a program needn't handle non-finite values. No bound on the sum of `sea_mask` on one device may be relied on, other than what follows from the above.
Results may differ from a plain program's by a relative error of at most 0.0003.
Values sent between devices are 32-bit elements; how exact they have to be, the bound alone decides.
No kernel may reach another device: no remote copies, remote signals or barrier semaphores. Data moves between devices by JAX's collectives and lax.ppermute only.
A program may use at most 128 MiB of HBM per device.

v0:
```python
import math

import jax
import jax.numpy as jnp
from jax import lax
from jax.sharding import PartitionSpec as P

NF = 36
ND = 36


LAT_SOUTH = 30.0
LAT_NORTH = 55.0
SPEED_TOP = 0.35
FREQ_STEP = 1.1
TURNING = 1.5
GROWTH = 0.05
WIND_COUPLING = 0.04


def padded(block, sides, width, periodic):
    for axis, dim in sides:
        count = lax.axis_size(axis)
        forward = [(i, i + 1) for i in range(count - 1)]
        if periodic:
            forward.append((count - 1, 0))
        backward = [(target, source) for source, target in forward]
        low = lax.ppermute(
            lax.slice_in_dim(block, block.shape[dim] - width, None, axis=dim), axis, forward
        )
        high = lax.ppermute(lax.slice_in_dim(block, 0, width, axis=dim), axis, backward)
        block = jnp.concatenate([low, block, high], axis=dim)
    return block


def latitude(position, total_rows):
    return (LAT_SOUTH + (LAT_NORTH - LAT_SOUTH) * position / total_rows) * (math.pi / 180.0)


def face_flux(behind, center, ahead, beyond, courant):
    forward = courant >= 0.0
    upwind = jnp.where(forward, behind, beyond)
    source_cell = jnp.where(forward, center, ahead)
    target_cell = jnp.where(forward, ahead, center)
    magnitude = jnp.abs(courant)
    face_value = (
        0.5 * (source_cell + target_cell)
        - 0.5 * magnitude * (target_cell - source_cell)
        - (1.0 - courant * courant) / 6.0 * (target_cell - 2.0 * source_cell + upwind)
    )
    return courant * face_value


def axis_fluxes(extended, cell_courant, along_axis):
    cell_count = extended.shape[along_axis] - 4

    def take_slice(values, offset):
        return lax.slice_in_dim(values, offset, offset + cell_count + 1, axis=along_axis)

    face_courant = 0.5 * (take_slice(cell_courant, 1) + take_slice(cell_courant, 2))
    return face_flux(
        take_slice(extended, 0),
        take_slice(extended, 1),
        take_slice(extended, 2),
        take_slice(extended, 3),
        face_courant,
    )


def component_tables(comp_index):
    freq_index = (comp_index // ND).astype(jnp.float32)
    direction = (comp_index % ND).astype(jnp.float32) * (2.0 * math.pi / ND)
    group_speed = SPEED_TOP * jnp.power(jnp.float32(FREQ_STEP), -freq_index)
    return (group_speed, jnp.cos(direction), jnp.sin(direction))


def propagate(spec_wide, spec_tall, current_wide, current_tall, comp_index, row_start, total_rows):
    group_speed, cos_dir, sin_dir = component_tables(comp_index)
    row_count = spec_wide.shape[1]
    cell_rows = (row_start + jnp.arange(row_count, dtype=jnp.int32)).astype(jnp.float32) + 0.5
    face_rows = (row_start + jnp.arange(row_count + 1, dtype=jnp.int32)).astype(jnp.float32)
    cell_cos = jnp.cos(latitude(cell_rows, total_rows))
    face_cos = jnp.cos(latitude(face_rows, total_rows))
    east_speed = (group_speed * cos_dir)[:, None, None] / cell_cos[None, :, None] + current_wide[0][
        None
    ]
    north_speed = (group_speed * sin_dir)[:, None, None] + current_tall[1][None]
    east_flux = axis_fluxes(spec_wide, east_speed, 2)
    north_flux = axis_fluxes(spec_tall, north_speed, 1) * face_cos[None, :, None]
    center_cells = spec_tall[:, 2:-2, :]
    return (
        center_cells
        - (east_flux[:, :, 1:] - east_flux[:, :, :-1])
        - (north_flux[:, 1:, :] - north_flux[:, :-1, :]) / cell_cos[None, :, None]
    )


def point_step(propagated, wind_rows, sea_rows, row_start, total_rows):
    row_count = propagated.shape[2]
    freq_index = jnp.arange(NF, dtype=jnp.int32).astype(jnp.float32)
    direction = jnp.arange(ND, dtype=jnp.int32).astype(jnp.float32) * (2.0 * math.pi / ND)
    group_speed = SPEED_TOP * jnp.power(jnp.float32(FREQ_STEP), -freq_index)
    cell_rows = (row_start + jnp.arange(row_count, dtype=jnp.int32)).astype(jnp.float32) + 0.5
    tangent = jnp.tan(latitude(cell_rows, total_rows))
    turn_rate = (
        -TURNING
        * group_speed[:, None, None]
        * jnp.cos(direction)[None, :, None]
        * tangent[None, None, :]
    )
    turn_wide = jnp.concatenate([turn_rate[:, -2:], turn_rate, turn_rate[:, :2]], axis=1)[..., None]
    spec_wide = jnp.concatenate([propagated[:, -2:], propagated, propagated[:, :2]], axis=1)
    turn_flux = axis_fluxes(spec_wide, turn_wide, 1)
    turned = propagated - (turn_flux[:, 1:] - turn_flux[:, :-1])
    wind_along = (
        wind_rows[0][None] * jnp.cos(direction)[:, None, None]
        + wind_rows[1][None] * jnp.sin(direction)[:, None, None]
    )
    coupling = WIND_COUPLING * jnp.power(jnp.float32(FREQ_STEP), freq_index)
    growth = GROWTH * jnp.maximum(wind_along[None] * coupling[:, None, None, None] - 1.0, 0.0)
    freq_weight = (freq_index + 1.0) / NF
    steepness = jnp.sum(freq_weight[:, None, None, None] * turned * turned, axis=(0, 1)) * (
        2.0 / (NF * ND)
    )
    damping = 1.0 + freq_weight[:, None, None, None] * steepness[None, None]
    return sea_rows[None, None] * turned * (1.0 + growth) / damping


def per_device(spectra, sea_mask, wind, current):
    comp_count, row_count, col_count = spectra.shape
    total_rows = row_count * lax.axis_size("band")
    band_index = lax.axis_index("band")
    row_start = band_index * row_count
    forcing = jnp.concatenate([wind, current], axis=0)
    relaid = lax.all_to_all(forcing, "band", split_axis=1, concat_axis=2, tiled=True)
    wind_here = relaid[:2]
    current_here = relaid[2:]
    sea_float = sea_mask.astype(jnp.float32)
    masked = spectra * sea_float[None]
    stacked = jnp.concatenate([masked, current_here], axis=0)
    cells_wide = padded(stacked, (("spec", 2),), 2, True)
    cells_tall = padded(stacked, (("band", 1),), 2, False)
    comp_index = jnp.arange(comp_count, dtype=jnp.int32)
    propagated = propagate(
        cells_wide[:comp_count],
        cells_tall[:comp_count],
        cells_wide[comp_count:],
        cells_tall[comp_count:],
        comp_index,
        row_start,
        total_rows,
    )
    shaped = propagated.reshape(NF, ND, row_count, col_count)
    result = point_step(shaped, wind_here, sea_float, row_start, total_rows)
    return result.reshape(comp_count, row_count, col_count)


def solution(mesh):
    placed = (
        P(None, "band", "spec"),
        P("band", "spec"),
        P(None, None, ("spec", "band")),
        P(None, None, ("spec", "band")),
    )
    return jax.shard_map(
        per_device, mesh=mesh, in_specs=placed, out_specs=P(None, "band", "spec"), check_vma=False
    )
```

profile of v0, /device:TPU:0, one launch (start us, length us, event | category | flops | bytes accessed | tf_op | source)
XLA Modules:
  0.0 92.1 jit_solution(15808783464643001035)
XLA Ops:
  0.0 0.7 copy.18
  0.7 0.7 copy.17
  1.5 0.7 reshape.170
  2.2 5.2 %all-to-all-start = ((f32[8,1,128]{2,1,0:T(1,128)}), f32[8,1,128]{2,1,0:T(1,128)S(1)}, u32[]{:S(2)}, u32[]{:S(2)}) async-start(f32[8,1,128]{2,1,0:T(1,128)} %reshape.170), calls=%async_computation | async-start | bytes 8192 | tf_op jit(solution)/shard_map/all_to_all | solution.py:135
  7.4 0.1 fusion.39
  7.5 0.1 fusion.38
  7.7 0.1 broadcast_multiply_fusion.2
  7.8 0.1 broadcast_multiply_fusion.1
  7.9 0.1 fusion.50
  8.0 0.1 maximum_bitcast_fusion
  8.1 0.1 multiply_bitcast_fusion.1
  8.4 0.7 convert_element_type.80
  9.1 1.4 %broadcast_multiply_fusion = f32[324,8,128]{2,1,0:T(8,128)S(1)} fusion(f32[324,8,128]{2,1,0:T(8,128)} %bitcast.40, f32[8,128]{1,0:T(8,128)S(1)} %bitcast.45), kind=kLoop, calls=%fused_computation.49 | loop fusion | flops 331776 | bytes 2658304 | tf_op jit(solution)/shard_map/mul | solution.py:139
  10.5 1.1 %broadcast_divide_fusion = f32[1296,2]{1,0:T(8,128)} fusion(f32[2]{0:T(128)S(1)} %fusion.46, f32[1296]{0:T(1024)S(1)} %fusion.38), kind=kLoop, calls=%fused_computation.50 | loop fusion | flops 2592 | bytes 15560 | tf_op jit(solution)/shard_map/div | solution.py:84
  11.6 1.1 %copy.27 = pred[36,37,2]{2,1,0:T(8,128)(4,1)} copy(pred[36,37,2]{1,2,0:T(4,128)(4,1)S(1)} %compare_bitcast_fusion) | data formatting | bytes 5328 | tf_op jit(solution)/shard_map/jit(_where)/broadcast_in_dim | solution.py:43
  12.6 0.4 copy.29
  13.0 1.2 %copy.28 = f32[36,37,2]{2,1,0:T(8,128)} copy(f32[36,37,2]{1,2,0:T(2,128)S(1)} %get-tuple-element.7) | data formatting | bytes 21312 | tf_op jit(solution)/shard_map/mul | solution.py:48
  14.2 1.2 %copy.26 = f32[36,37,2]{2,1,0:T(8,128)} copy(f32[36,37,2]{1,2,0:T(2,128)S(1)} %bitcast.41) | data formatting | bytes 21312 | tf_op jit(solution)/shard_map/mul | solution.py:51
  15.5 0.0 all-to-all-done
  15.5 0.6 broadcast.339
  16.1 0.6 reduce
  16.7 0.1 reshape.171
  16.8 0.1 slice.144
  16.9 2.9 %pad_maximum_fusion.2 = f32[1298,2,128]{2,1,0:T(2,128)} fusion(f32[2,2,128]{2,1,0:T(2,128)S(1)} %slice.144, f32[1296,2,128]{2,1,0:T(2,128)S(1)} %bitcast.31), kind=kLoop, calls=%fused_computation.23 | loop fusion | flops 332288 | bytes 2658304 | tf_op jit(solution)/shard_map/concatenate | solution.py:140
  19.8 3.5 %collective-permute-start.2 = (f32[1298,2,128]{2,1,0:T(2,128)}, f32[1298,2,128]{2,1,0:T(2,128)}, u32[]{:S(2)}, u32[]{:S(2)}) collective-permute-start(f32[1298,2,128]{2,1,0:T(2,128)} %pad_maximum_fusion.2), channel_id=1, source_target_pairs={{0,4},{4,8},{8,12},{12,16},{16,20},{20,24},{24,28},{1,5},{5,9},{9,... | collective-permute-start | bytes 3987464 | tf_op jit(solution)/shard_map/ppermute | solution.py:28
  23.3 1.3 %collective-permute-start.3 = (f32[1298,2,128]{2,1,0:T(2,128)}, f32[1298,2,128]{2,1,0:T(2,128)}, u32[]{:S(2)}, u32[]{:S(2)}) collective-permute-start(f32[1298,2,128]{2,1,0:T(2,128)} %pad_maximum_fusion.2), channel_id=1, source_target_pairs={{4,0},{8,4},{12,8},{16,12},{20,16},{24,20},{28,24},{5,1},{9,5},{13... | collective-permute-start | bytes 3987464 | tf_op jit(solution)/shard_map/ppermute | solution.py:31
  24.6 3.8 %fusion.18 = (f32[1298,2,2]{2,1,0:T(2,128)}, f32[1298,2,2]{2,1,0:T(2,128)S(1)}) fusion(f32[2,2,128]{2,1,0:T(2,128)S(1)} %slice.144, f32[1296,2,128]{2,1,0:T(2,128)S(1)} %bitcast.32), kind=kLoop, calls=%fused_computation.38 | loop fusion | flops 10384 | bytes 1370688 | tf_op jit(solution)/shard_map/concatenate | solution.py:140
  28.4 2.4 %copy.20 = f32[1298,2,2]{0,2,1:T(2,128)S(1)} copy(f32[1298,2,2]{2,1,0:T(2,128)} %get-tuple-element.11) | data formatting | bytes 41536 | tf_op jit(solution)/shard_map/slice | solution.py:29
  30.8 1.6 %collective-permute-start = (f32[1298,2,2]{0,2,1:T(2,128)S(1)}, f32[1298,2,2]{0,2,1:T(2,128)S(1)}, u32[]{:S(2)}, u32[]{:S(2)}) collective-permute-start(f32[1298,2,2]{0,2,1:T(2,128)S(1)} %copy.20), channel_id=1, source_target_pairs={{0,1},{1,2},{2,3},{3,0},{4,5},{5,6},{6,7},{7,4},{8,9},{9,10},{10,1... | collective-permute-start | bytes 62312 | tf_op jit(solution)/shard_map/ppermute | solution.py:28
  32.4 1.2 %copy.21 = f32[1298,2,2]{0,2,1:T(2,128)S(1)} copy(f32[1298,2,2]{2,1,0:T(2,128)S(1)} %get-tuple-element.12) | data formatting | bytes 41536 | tf_op jit(solution)/shard_map/slice | solution.py:31
  33.6 2.5 %collective-permute-start.1 = (f32[1298,2,2]{0,2,1:T(2,128)S(1)}, f32[1298,2,2]{0,2,1:T(2,128)}, u32[]{:S(2)}, u32[]{:S(2)}) collective-permute-start(f32[1298,2,2]{0,2,1:T(2,128)S(1)} %copy.21), channel_id=1, source_target_pairs={{1,0},{2,1},{3,2},{0,3},{5,4},{6,5},{7,6},{4,7},{9,8},{10,9},{11,1... | collective-permute-start | bytes 62312 | tf_op jit(solution)/shard_map/ppermute | solution.py:31
  36.1 0.1 mul.440
  36.2 0.1 mul.436
  36.3 0.1 multiply_add_fusion.1
  36.4 0.0 collective-permute-done
  36.4 1.5 %copy.22 = f32[1298,2,2]{2,1,0:T(2,128)S(1)} copy(f32[1298,2,2]{0,2,1:T(2,128)S(1)} %collective-permute-done) | data formatting | bytes 41536 | tf_op jit(solution)/shard_map/ppermute | solution.py:28
  37.9 0.1 collective-permute-done.1
  38.0 2.7 %copy.23 = f32[1298,2,2]{2,1,0:T(2,128)} copy(f32[1298,2,2]{0,2,1:T(2,128)} %collective-permute-done.1) | data formatting | bytes 41536 | tf_op jit(solution)/shard_map/ppermute | solution.py:31
  40.6 8.4 %maximum_maximum_fusion = (f32[1298,2,130]{2,1,0:T(2,128)S(1)}, f32[1298,2,130]{2,1,0:T(2,128)S(1)}) fusion(f32[2,2,128]{2,1,0:T(2,128)S(1)} %slice.144, f32[1296,2,128]{2,1,0:T(2,128)S(1)} %bitcast.33, f32[1298,2,2]{2,1,0:T(2,128)S(1)} %copy.22, f32[1298,2,2]{2,1,0:T(2,128)} %copy.23), kind=kLoop, calls=%fused_computation | loop fusion | flops 1349920 | bytes 4070528 | tf_op jit(solution)/shard_map/concatenate | solution.py:32
  49.1 0.0 copy-done
  49.1 0.0 copy-start.4
  49.1 0.1 fusion.42
  49.2 1.0 %copy-done.4 = f32[1296,2]{1,0:T(8,128)S(1)} copy-done((f32[1296,2]{1,0:T(8,128)S(1)}, f32[1296,2]{1,0:T(8,128)}, u32[]{:S(2)}) %copy-start.4) | copy-done | bytes 10392
  50.2 1.6 %broadcast_add_fusion.1 = f32[1296,2,132]{2,1,0:T(2,128)S(1)} fusion(f32[2,132]{1,0:T(2,128)S(1)} %fusion.42, f32[1296,2]{1,0:T(8,128)S(1)} %copy-done.4), kind=kLoop, calls=%fused_computation.48 | loop fusion | flops 342144 | bytes 1380000 | tf_op jit(solution)/shard_map/add | solution.py:84
  51.8 11.6 %fusion.9 = f32[1296,2,129]{2,1,0:T(2,128)S(1)} fusion(f32[1298,2,130]{2,1,0:T(2,128)S(1)} %get-tuple-element.10, f32[1298,2,130]{2,1,0:T(2,128)S(1)} %get-tuple-element.9, f32[1296,2,132]{2,1,0:T(2,128)S(1)} %broadcast_add_fusion.1), kind=kLoop, calls=%fused_computation.16 | loop fusion | flops 7356096 | bytes 9362304 | tf_op jit(solution)/shard_map/mul | solution.py:51
  63.4 0.0 collective-permute-done.2
  63.4 0.0 collective-permute-done.3
  63.4 0.7 fusion.41
  64.1 3.5 %broadcast_add_fusion = f32[1296,6,128]{2,1,0:T(8,128)S(1)} fusion(f32[6,128]{1,0:T(8,128)S(1)} %fusion.41, f32[1296]{0:T(1024)S(1)} %fusion.39), kind=kLoop, calls=%fused_computation.19 | loop fusion | flops 995328 | bytes 3989568 | tf_op jit(solution)/shard_map/add | solution.py:87
  67.6 4.9 %maximum_maximum_fusion.1 = (f32[1298,4,128]{2,1,0:T(4,128)S(1)}, f32[1298,4,128]{2,1,0:T(4,128)S(1)}) fusion(f32[2,2,128]{2,1,0:T(2,128)S(1)} %slice.144, f32[1296,2,128]{2,1,0:T(2,128)S(1)} %bitcast.36, f32[1298,2,128]{2,1,0:T(2,128)} %collective-permute-done.2, f32[1298,2,128]{2,1,0:T(2,128)} %collective-permute-done.3), kind=kLoop, calls=%fused_computation.2 | loop fusion | flops 2658304 | bytes 9304064 | tf_op jit(solution)/shard_map/concatenate | solution.py:32
  72.6 0.0 copy-start.1
  72.6 5.4 %fusion.4 = f32[1296,3,128]{2,1,0:T(4,128)S(1)} fusion(f32[1298,4,128]{2,1,0:T(4,128)S(1)} %get-tuple-element.14, f32[1298,4,128]{2,1,0:T(4,128)S(1)} %get-tuple-element.13, f32[1296,6,128]{2,1,0:T(8,128)S(1)} %broadcast_add_fusion, f32[3]{0:T(128)S(1)} %multiply_cosine_fusion), kind=kLoop, calls=%fused_computation.9 | loop fusion | flops 11446272 | bytes 13934604 | tf_op jit(solution)/shard_map/mul | solution.py:89
  77.9 0.0 copy-done.1
  78.0 0.0 copy-start.2
  78.0 0.0 copy-start.3
  78.0 0.0 copy-start.5
  78.0 1.9 %divide_subtract_fusion = f32[1296,2,128]{2,1,0:T(2,128)S(1)} fusion(f32[1296,3,128]{2,1,0:T(4,128)S(1)} %fusion.4, f32[1296,2,129]{2,1,0:T(2,128)S(1)} %fusion.9, f32[2]{0:T(128)S(1)} %fusion.46, f32[1296,2,128]{2,1,0:T(2,128)S(1)} %copy-done.1, f32[2,128]{1,0:T(2,128)S(1)} %convert_element_type.80), kind=kLoop, calls=%fused_computation.40 | loop fusion | flops 1990656 | bytes 7963656 | tf_op jit(solution)/shard_map/sub | solution.py:92
  79.9 0.0 copy-done.2
  80.0 0.0 copy-done.3
  80.0 0.0 copy-done.5
  80.0 7.3 %fusion.17 = f32[36,37,2,128]{3,2,1,0:T(2,128)S(1)} fusion(f32[36,2,2,128]{3,2,1,0:T(2,128)S(1)} %get-tuple-element.16, f32[36,36,2,128]{3,2,1,0:T(2,128)S(1)} %bitcast.38, f32[36,2,2,128]{3,2,1,0:T(2,128)S(1)} %get-tuple-element.15, pred[36,37,2]{2,1,0:T(8,128)(4,1)S(1)} %copy-done.5, f32[36,37,2]{2,1,0:T(8,128)S(1)} %copy.29, ...), kind=kLoop, calls=%fused_computation.37 | loop fusion | flops 6137856 | bytes 2873160 | tf_op jit(solution)/shard_map/mul | solution.py:51
  87.3 2.0 %fusion.20 = (f32[2,128]{1,0:T(2,128)S(1)}, f32[36,36,2,128]{3,2,1,0:T(2,128)S(1)}) fusion(f32[36]{0:T(128)S(1)} %add_multiply_fusion, f32[36,36,2,128]{3,2,1,0:T(2,128)S(1)} %bitcast.39, f32[36,37,2,128]{3,2,1,0:T(2,128)S(1)} %fusion.17), kind=kLoop, calls=%fused_computation.41 | loop fusion | flops 1658624 | bytes 5309584 | tf_op jit(solution)/shard_map/reduce_sum | solution.py:122
  89.3 0.1 multiply_add_fusion
  89.4 2.7 %multiply_divide_fusion = f32[36,36,2,128]{3,2,1,0:T(2,128)} fusion(f32[36,36,2,128]{3,2,1,0:T(2,128)S(1)} %get-tuple-element.6, f32[36,2,128]{2,1,0:T(2,128)S(1)} %multiply_add_fusion, f32[36,2,128]{2,1,0:T(2,128)S(1)} %multiply_add_fusion.1, f32[2,128]{1,0:T(2,128)S(1)} %convert_element_type.80, f32[36]{0:T(128)S(1)} %power_multiply_fusion), kind=kLoop, calls=%fused_computation.47 | loop fusion | flops 2654208 | bytes 2729104 | tf_op jit(solution)/shard_map/div | solution.py:126
  (17 shorter events, 0.4 us)
Async XLA Ops:
  2.2 13.3 %all-to-all-start = ((f32[8,1,128]{2,1,0:T(1,128)}), f32[8,1,128]{2,1,0:T(1,128)S(1)}, u32[]{:S(2)}, u32[]{:S(2)}) async-start(f32[8,1,128]{2,1,0:T(1,128)} %reshape.170), calls=%async_computation | async-start | bytes 8192 | tf_op jit(solution)/shard_map/all_to_all | solution.py:135
  19.8 43.5 %collective-permute-start.2 = (f32[1298,2,128]{2,1,0:T(2,128)}, f32[1298,2,128]{2,1,0:T(2,128)}, u32[]{:S(2)}, u32[]{:S(2)}) collective-permute-start(f32[1298,2,128]{2,1,0:T(2,128)} %pad_maximum_fusion.2), channel_id=1, source_target_pairs={{0,4},{4,8},{8,12},{12,16},{16,20},{20,24},{24,28},{1,5},{5,9},{9,... | collective-permute-start | bytes 3987464 | tf_op jit(solution)/shard_map/ppermute | solution.py:28
  23.3 40.1 %collective-permute-start.3 = (f32[1298,2,128]{2,1,0:T(2,128)}, f32[1298,2,128]{2,1,0:T(2,128)}, u32[]{:S(2)}, u32[]{:S(2)}) collective-permute-start(f32[1298,2,128]{2,1,0:T(2,128)} %pad_maximum_fusion.2), channel_id=1, source_target_pairs={{4,0},{8,4},{12,8},{16,12},{20,16},{24,20},{28,24},{5,1},{9,5},{13... | collective-permute-start | bytes 3987464 | tf_op jit(solution)/shard_map/ppermute | solution.py:31
  30.8 5.7 %collective-permute-start = (f32[1298,2,2]{0,2,1:T(2,128)S(1)}, f32[1298,2,2]{0,2,1:T(2,128)S(1)}, u32[]{:S(2)}, u32[]{:S(2)}) collective-permute-start(f32[1298,2,2]{0,2,1:T(2,128)S(1)} %copy.20), channel_id=1, source_target_pairs={{0,1},{1,2},{2,3},{3,0},{4,5},{5,6},{6,7},{7,4},{8,9},{9,10},{10,1... | collective-permute-start | bytes 62312 | tf_op jit(solution)/shard_map/ppermute | solution.py:28
  33.6 4.3 %collective-permute-start.1 = (f32[1298,2,2]{0,2,1:T(2,128)S(1)}, f32[1298,2,2]{0,2,1:T(2,128)}, u32[]{:S(2)}, u32[]{:S(2)}) collective-permute-start(f32[1298,2,2]{0,2,1:T(2,128)S(1)} %copy.21), channel_id=1, source_target_pairs={{1,0},{2,1},{3,2},{0,3},{5,4},{6,5},{7,6},{4,7},{9,8},{10,9},{11,1... | collective-permute-start | bytes 62312 | tf_op jit(solution)/shard_map/ppermute | solution.py:31
  40.6 8.4 %copy-start = (f32[1298,2,2]{2,1,0:T(2,128)S(1)}, f32[1298,2,2]{2,1,0:T(2,128)}, u32[]{:S(2)}) copy-start(f32[1298,2,2]{2,1,0:T(2,128)} %copy.23) | copy-start | bytes 62308
  49.1 1.1 %copy-start.4 = (f32[1296,2]{1,0:T(8,128)S(1)}, f32[1296,2]{1,0:T(8,128)}, u32[]{:S(2)}) copy-start(f32[1296,2]{1,0:T(8,128)} %broadcast_divide_fusion) | copy-start | bytes 31108
  72.6 5.4 %copy-start.1 = (f32[1296,2,128]{2,1,0:T(2,128)S(1)}, f32[1296,2,128]{2,1,0:T(2,128)}, u32[]{:S(2)}) copy-start(f32[1296,2,128]{2,1,0:T(2,128)} %param.4) | copy-start | bytes 3981316
  78.0 2.0 %copy-start.2 = (f32[36,37,2]{2,1,0:T(8,128)S(1)}, f32[36,37,2]{2,1,0:T(8,128)}, u32[]{:S(2)}) copy-start(f32[36,37,2]{2,1,0:T(8,128)} %copy.28) | copy-start | bytes 31972
  78.0 2.0 %copy-start.3 = (f32[36,37,2]{2,1,0:T(8,128)S(1)}, f32[36,37,2]{2,1,0:T(8,128)}, u32[]{:S(2)}) copy-start(f32[36,37,2]{2,1,0:T(8,128)} %copy.26) | copy-start | bytes 31972
  78.0 2.0 %copy-start.5 = (pred[36,37,2]{2,1,0:T(8,128)(4,1)S(1)}, pred[36,37,2]{2,1,0:T(8,128)(4,1)}, u32[]{:S(2)}) copy-start(pred[36,37,2]{2,1,0:T(8,128)(4,1)} %copy.27) | copy-start | bytes 7996
where the time goes:
time: 93.7 us; the launch traced here: 92.1 us
  other arithmetic  61.8 us (66%)
  local copies, waits for them, and re-layouts  15.9 us (17%)
  starting transfers between devices  14 us (15%)
    mul x2, other arithmetic, face_flux(): return courant * face_value  18.9 us
    concatenate x2, other arithmetic, padded(): block = jnp.concatenate([low, block, high], axis=dim)  13.3 us
    concatenate x2, other arithmetic, per_device(): stacked = jnp.concatenate([masked, current_here], axis=0)  6.71 us
    mul x1, other arithmetic, propagate(): axis_fluxes(spec_tall, north_speed, 1) * face_cos[None, :, None]  5.37 us
    all_to_all x1, starting transfers between devices, per_device(): lax.all_to_all(forcing, 'band', split_axis=1, concat_axis=2, tiled=True)  5.17 us
    ppermute x2, starting transfers between devices, padded(): lax.ppermute(lax.slice_in_dim(block, block.shape[dim] - width, None, axis...  5.11 us
    add x2, other arithmetic, propagate(): north_speed = (group_speed * sin_dir)[:, None, None] + current_tall[1][None]  4.24 us
    ppermute x2, starting transfers between devices, padded(): lax.ppermute(lax.slice_in_dim(block, 0, width, axis=dim), axis, backward)  3.76 us
  transfers between devices with their start and end apart: 5, of which 1 were waited for; matrix products, arithmetic and copies ran while one was open for 45% of the time, Pallas kernels for 0%

commit v1 on v0

v1 whole, which is shorter than its diff:
```python
import functools
import math

import jax
import jax.numpy as jnp
import numpy as np
from jax import lax
from jax.experimental import pallas as pl
from jax.experimental.pallas import tpu as pltpu
from jax.sharding import PartitionSpec as P

NF = 36
ND = 36
HALF = ND // 2
LAT_SOUTH = 30.0
LAT_NORTH = 55.0
SPEED_TOP = 0.35
FREQ_STEP = 1.1
TURNING = 1.5
GROWTH = 0.05
WIND_COUPLING = 0.04

GF = 4
GROUPS = NF // GF
GROUP_ROWS = GF * ND * 2
DIRECT_GROUPS = 5
LANES = 128
ROWS = NF * ND * 2
WIDE = -(-(ROWS + 2) // LANES) * LANES

COS = [math.cos(2.0 * math.pi * d / ND) for d in range(HALF + 1)]
SIN = [math.sin(2.0 * math.pi * d / ND) for d in range(HALF + 1)]

(
    CUR_A,
    CUR_M,
    CUR_B,
    CX_A,
    CX_B,
    W0_A,
    W0_B,
    W1_A,
    W1_B,
    SEA_A,
    SEA_B,
    SEA_A1,
    SEA_A2,
    SEA_B1,
    SEA_B2,
    TAU,
    ICOS_A,
    ICOS_B,
    KAP_A,
    MU_A,
    MU_B,
    KAP_B,
    TAN_A,
    TAN_B,
    ICOS_0,
    ICOS_1,
) = range(26)
PAR_ROWS = 32


def flux(lo2, lo1, hi1, hi2, c):
    forward = c >= 0.0
    source = jnp.where(forward, lo1, hi1)
    upwind = jnp.where(forward, lo2, hi2)
    both = lo1 + hi1
    bend = both - 3.0 * source + upwind
    w = (1.0 / 6.0) - (c * c) * (1.0 / 6.0)
    return c * (0.5 * (both - c * (hi1 - lo1)) - w * bend)


def group_speed():
    k = lax.broadcasted_iota(jnp.int32, (8, LANES), 0)
    speed = jnp.zeros((8, LANES), jnp.float32)
    for i in range(GF):
        for h in range(2):
            value = SPEED_TOP * FREQ_STEP**-i * (1.0 - 2.0 * h)
            speed = jnp.where(k == 2 * i + h, value, speed)
    return speed


def freq_weight():
    k = lax.broadcasted_iota(jnp.int32, (8, LANES), 0)
    weight = jnp.zeros((8, LANES), jnp.float32)
    for i in range(GF):
        weight = jnp.where(lax.div(k, 2) == i, (i + 1.0) / NF, weight)
    return weight


def swap_halves(v):
    k = lax.broadcasted_iota(jnp.int32, (8, LANES), 0)
    return jnp.where(lax.rem(k, 2) == 0, pltpu.roll(v, 7, 0), pltpu.roll(v, 1, 0))


def wide_row(par, index):
    return jnp.broadcast_to(par[index : index + 1, :], (8, LANES))


def pack_kernel(bands, wind, current, sea, out, line):
    me = lax.axis_index("band")
    rows, strip = wind.shape[1], wind.shape[2]

    def placed(ref, part):
        empty = jnp.zeros((rows, LANES - strip), jnp.float32)
        return pltpu.roll(jnp.concatenate([ref[part], empty], axis=1), me * strip, 1)

    empty = jnp.zeros((8, LANES), jnp.float32)
    line[0, 0:8, :] = empty
    line[0, 8 + rows : 16 + rows, :] = empty
    line[0, 8 : 8 + rows, :] = placed(current, 1)
    line[1, 8 : 8 + rows, :] = placed(current, 0)
    line[2, 8 : 8 + rows, :] = placed(wind, 0)
    line[3, 8 : 8 + rows, :] = placed(wind, 1)
    seas = sea[...].astype(jnp.float32)
    for t in range(bands):
        at = 8 + 2 * t
        out[t, 0:4, :] = line[0, at - 1 : at + 3, :]
        for part in range(1, 4):
            out[t, 2 + 2 * part : 4 + 2 * part, :] = line[part, at : at + 2, :]
        out[t, 10:12, :] = seas
        out[t, 12:16, :] = jnp.zeros((4, LANES), jnp.float32)


def edge_kernel(bands, geometry, relaid, spectra, sea, par, west, east, line):
    me = lax.axis_index("band")
    odd = lax.rem(me, 2)
    is_even = odd == 0
    forcing = relaid[0]
    for source in range(1, bands):
        forcing = forcing + relaid[source]
    has_south = jnp.where(me > 0, 1.0, 0.0)
    has_north = jnp.where(me < bands - 1, 1.0, 0.0)
    sea_south = relaid[jnp.maximum(me - 1, 0)][10:12] * has_south
    sea_north = relaid[jnp.minimum(me + 1, bands - 1)][10:12] * has_north
    seas = sea[...].astype(jnp.float32)

    def pick(low, high):
        return jnp.where(is_even, low, high)

    def put(index, value):
        par[index : index + 1, :] = jnp.broadcast_to(value, (1, LANES))

    tau = jnp.where(is_even, 1.0, -1.0)
    north = [forcing[i : i + 1] for i in range(4)]
    face = [0.5 * (north[i] + north[i + 1]) for i in range(3)]
    put(CUR_A, tau * pick(face[0], face[2]))
    put(CUR_M, tau * face[1])
    put(CUR_B, tau * pick(face[2], face[0]))
    lane = lax.broadcasted_iota(jnp.int32, (1, LANES), 1)
    inside = jnp.where(lane == 0, 0.0, 1.0)
    east_speed = [forcing[4:5], forcing[5:6]]
    shifted = [0.5 * inside * (v + pltpu.roll(v, 1, 1)) for v in east_speed]
    put(CX_A, pick(shifted[0], shifted[1]))
    put(CX_B, pick(shifted[1], shifted[0]))
    put(W0_A, pick(forcing[6:7], forcing[7:8]))
    put(W0_B, pick(forcing[7:8], forcing[6:7]))
    put(W1_A, pick(forcing[8:9], forcing[9:10]))
    put(W1_B, pick(forcing[9:10], forcing[8:9]))
    put(SEA_A, pick(seas[0:1], seas[1:2]))
    put(SEA_B, pick(seas[1:2], seas[0:1]))
    put(SEA_A1, pick(sea_south[1:2], sea_north[0:1]))
    put(SEA_A2, pick(sea_south[0:1], sea_north[1:2]))
    put(SEA_B1, pick(sea_north[0:1], sea_south[1:2]))
    put(SEA_B2, pick(sea_north[1:2], sea_south[0:1]))
    put(TAU, tau)
    icos = [geometry[me, 0], geometry[me, 1]]
    put(ICOS_A, inside * pick(icos[0], icos[1]))
    put(ICOS_B, inside * pick(icos[1], icos[0]))
    put(KAP_A, geometry[me, 2])
    put(MU_A, geometry[me, 3])
    put(MU_B, geometry[me, 4])
    put(KAP_B, geometry[me, 5])
    put(TAN_A, geometry[me, 6])
    put(TAN_B, geometry[me, 7])
    put(ICOS_0, icos[0])
    put(ICOS_1, icos[1])
    par[26:32, :] = jnp.zeros((6, LANES), jnp.float32)

    sub = lax.broadcasted_iota(jnp.int32, (LANES, LANES), 0)
    both = jnp.where(
        lax.rem(sub, 2) == 0,
        jnp.broadcast_to(seas[0:1], (LANES, LANES)),
        jnp.broadcast_to(seas[1:2], (LANES, LANES)),
    )
    full = ROWS // LANES
    for block in range(WIDE // LANES):
        at = block * LANES
        if block < full:
            cells = spectra[at : at + LANES, :] * both
        else:
            left = ROWS - at
            line[...] = jnp.zeros((LANES, LANES), jnp.float32)
            line[0:left, :] = spectra[at : at + left, :] * both[0:left]
            line[left : left + 2, :] = forcing[4:6]
            cells = line[...]
        turned = cells.T
        west[:, at : at + LANES] = turned[0:2]
        east[:, at : at + LANES] = turned[LANES - 2 : LANES]


def base_kernel(table, par, spectra, beyond, west, east, from_west, from_east, base, tall, fix):
    odd = lax.rem(lax.axis_index("band"), 2)
    lane = lax.broadcasted_iota(jnp.int32, (1, WIDE), 1)
    even_row = lax.rem(lane, 2) == 0
    speed = table[0:1] * par[ICOS_0 : ICOS_0 + 1, 0:1] + table[1:2] * par[ICOS_1 : ICOS_1 + 1, 0:1]

    def column(ref, row):
        cells = ref[row : row + 1, :]
        drift = jnp.where(even_row, cells[:, ROWS : ROWS + 1], cells[:, ROWS + 1 : ROWS + 2])
        return cells, drift

    xm2, _ = column(from_west, 0)
    xm1, dm1 = column(from_west, 1)
    x0, d0 = column(west, 0)
    x1, d1 = column(west, 1)
    y2, d2 = column(east, 0)
    y1, dy1 = column(east, 1)
    z0, dz0 = column(from_east, 0)
    z1, _ = column(from_east, 1)
    first = flux(xm2, xm1, x0, x1, speed + 0.5 * (dm1 + d0))
    last = flux(y2, y1, z0, z1, speed + 0.5 * (dy1 + dz0))
    c = speed + 0.5 * (d0 + d1)
    second = jnp.where(c >= 0.0, -c * (1.0 - c * c) * (1.0 / 6.0), 0.0) * (xm1 - y1)
    c = speed + 0.5 * (d2 + dy1)
    before = jnp.where(c >= 0.0, 0.0, -c * (1.0 - c * c) * (1.0 / 6.0)) * (z0 - x0)
    tall[...] = jnp.zeros((LANES, WIDE), jnp.float32)
    tall[0:1, :] = first - second
    tall[1:2, :] = second
    tall[LANES - 2 : LANES - 1, :] = -before
    tall[LANES - 1 : LANES, :] = before - last
    for block in range(WIDE // LANES):
        at = block * LANES
        fix[at : at + LANES, :] = tall[:, at : at + LANES].T

    sea_a, sea_b = wide_row(par, SEA_A), wide_row(par, SEA_B)
    sea_b1, sea_b2 = wide_row(par, SEA_B1), wide_row(par, SEA_B2)
    cur_a, cur_m, cur_b = wide_row(par, CUR_A), wide_row(par, CUR_M), wide_row(par, CUR_B)
    cx_a, cx_b = wide_row(par, CX_A), wide_row(par, CX_B)
    kap_a, mu_a = wide_row(par, KAP_A), wide_row(par, MU_A)
    mu_b, kap_b = wide_row(par, MU_B), wide_row(par, KAP_B)
    tau = wide_row(par, TAU)
    icos_a, icos_b = wide_row(par, ICOS_A), wide_row(par, ICOS_B)

    def along_east(x, speed_x, current_x, cosine):
        crossing = flux(
            pltpu.roll(x, 2, 1),
            pltpu.roll(x, 1, 1),
            x,
            pltpu.roll(x, LANES - 1, 1),
            speed_x * cosine + current_x,
        )
        return crossing - pltpu.roll(crossing, LANES - 1, 1)

    def one_group(g, speeds):
        start = g * GROUP_ROWS
        north = speeds * tau
        east_a, east_b = speeds * icos_a, speeds * icos_b
        for d in range(HALF):
            row_a = pl.ds(start + 2 * d + odd, 8, stride=ND)
            row_b = pl.ds(start + 2 * d + 1 - odd, 8, stride=ND)
            a = spectra[row_a, :] * sea_a
            b = spectra[row_b, :] * sea_b
            b1 = beyond[row_a, :] * sea_b1
            b2 = beyond[row_b, :] * sea_b2
            c = north * SIN[d] + cur_a
            w = (1.0 / 6.0) - (c * c) * (1.0 / 6.0)
            flux_a = c * (0.5 * (a - c * a) - w * jnp.where(c >= 0.0, a, b - 2.0 * a))
            flux_m = flux(0.0, a, b, b1, north * SIN[d] + cur_m)
            flux_b = flux(a, b, b1, b2, north * SIN[d] + cur_b)
            to_a = along_east(a, east_a, cx_a, COS[d]) + fix[row_a, :]
            to_b = along_east(b, east_b, cx_b, COS[d]) + fix[row_b, :]
            at = pl.multiple_of(g * (HALF * 16) + d * 16, 8)
            base[pl.ds(at, 8), :] = a + to_a + kap_a * flux_a - mu_a * flux_m
            base[pl.ds(at + 8, 8), :] = b + to_b + mu_b * flux_m - kap_b * flux_b
        return speeds * FREQ_STEP**-GF

    lax.fori_loop(0, GROUPS, one_group, group_speed())


def turn(cells, rate):
    after = [swap_halves(cells[0]), swap_halves(cells[1])]
    lower = swap_halves(cells[HALF - 1])
    ring = [lower] + cells + after
    fluxes = []
    for d in range(HALF):
        mean = 0.5 * (COS[d] + COS[d + 1])
        fluxes.append(flux(ring[d], ring[d + 1], ring[d + 2], ring[d + 3], rate * mean))
    last = swap_halves(fluxes[HALF - 1])
    return [cells[d] - (fluxes[d] - (fluxes[d - 1] if d else last)) for d in range(HALF)]


def finish_groups(first, count, par, base, ahead, turned, odd, total):
    sea_a1, sea_a2 = wide_row(par, SEA_A1), wide_row(par, SEA_A2)
    cur_a, cur_m = wide_row(par, CUR_A), wide_row(par, CUR_M)
    kap_a, mu_a, mu_b = wide_row(par, KAP_A), wide_row(par, MU_A), wide_row(par, MU_B)
    tau = wide_row(par, TAU)
    tan_a, tan_b = wide_row(par, TAN_A), wide_row(par, TAN_B)

    def one_group(g, carry):
        speeds, weight, sum_a, sum_b = carry
        start = g * GROUP_ROWS
        north = speeds * tau
        cells_a, cells_b = [], []
        for d in range(HALF):
            n1 = ahead[pl.ds(start + 2 * d + 1 - odd, 8, stride=ND), :] * sea_a1
            n2 = ahead[pl.ds(start + 2 * d + odd, 8, stride=ND), :] * sea_a2
            c = north * SIN[d] + cur_a
            w = (1.0 / 6.0) - (c * c) * (1.0 / 6.0)
            flux_a = c * (0.5 * (n1 + c * n1) - w * jnp.where(c >= 0.0, n2 - 2.0 * n1, n1))
            c = north * SIN[d] + cur_m
            w = (c * c) * (1.0 / 6.0) - (1.0 / 6.0)
            flux_m = jnp.where(c >= 0.0, c * w, 0.0) * n1
            at = pl.multiple_of(g * (HALF * 16) + d * 16, 8)
            cells_a.append(base[pl.ds(at, 8), :] + kap_a * flux_a - mu_a * flux_m)
            cells_b.append(base[pl.ds(at + 8, 8), :] + mu_b * flux_m)
        square_a = square_b = 0.0
        for d, v in enumerate(turn(cells_a, speeds * tan_a)):
            at = pl.multiple_of(g * (HALF * 16) + d * 16, 8)
            turned[pl.ds(at, 8), :] = v
            square_a = square_a + v * v
        for d, v in enumerate(turn(cells_b, speeds * tan_b)):
            at = pl.multiple_of(g * (HALF * 16) + d * 16 + 8, 8)
            turned[pl.ds(at, 8), :] = v
            square_b = square_b + v * v
        return (
            speeds * FREQ_STEP**-GF,
            weight + GF / NF,
            sum_a + weight * square_a,
            sum_b + weight * square_b,
        )

    speeds = group_speed() * FREQ_STEP ** -(GF * first)
    weight = freq_weight() + GF * first / NF
    carry = (speeds, weight, total[0:8, :], total[8:16, :])
    return lax.fori_loop(0, count, one_group, carry)[2:]


def fetch(bands, first, count, straight, split, ahead, sem):
    me = lax.axis_index("band")
    middle = jnp.logical_or(me == bands // 2 - 1, me == bands // 2)
    rows = count * GROUP_ROWS

    @pl.when(middle)
    def _():
        copy = pltpu.make_async_copy(split, ahead, sem)
        copy.start()
        copy.wait()

    @pl.when(jnp.logical_not(middle))
    def _():
        copy = pltpu.make_async_copy(straight.at[pl.ds(first * GROUP_ROWS, rows)], ahead, sem)
        copy.start()
        copy.wait()


def first_kernel(bands, par, base, straight, split, turned, total, ahead, sem):
    odd = lax.rem(lax.axis_index("band"), 2)
    fetch(bands, 0, DIRECT_GROUPS, straight, split, ahead, sem)
    total[...] = jnp.zeros((16, LANES), jnp.float32)
    sums = finish_groups(0, DIRECT_GROUPS, par, base, ahead, turned, odd, total)
    total[0:8, :] = sums[0]
    total[8:16, :] = sums[1]


def last_kernel(bands, par, base, straight, split, done, total, out, ahead, turned, sem):
    odd = lax.rem(lax.axis_index("band"), 2)
    later = GROUPS - DIRECT_GROUPS
    fetch(bands, DIRECT_GROUPS, later, straight, split, ahead, sem)
    sums = finish_groups(DIRECT_GROUPS, later, par, base, ahead, turned, odd, total)
    scale = 2.0 / (NF * ND)
    steep_a = jnp.sum(sums[0], axis=0, keepdims=True) * scale
    steep_b = jnp.sum(sums[1], axis=0, keepdims=True) * scale
    sea_a, sea_b = wide_row(par, SEA_A), wide_row(par, SEA_B)
    w0_a, w0_b = wide_row(par, W0_A), wide_row(par, W0_B)
    w1_a, w1_b = wide_row(par, W1_A), wide_row(par, W1_B)

    def one_group(first, ref, g, carry):
        coupling, weight = carry
        start = (first + g) * GROUP_ROWS
        gain_a = sea_a / (1.0 + weight * steep_a)
        gain_b = sea_b / (1.0 + weight * steep_b)
        wa0, wa1 = w0_a * coupling, w1_a * coupling
        wb0, wb1 = w0_b * coupling, w1_b * coupling
        for d in range(HALF):
            at = pl.multiple_of(g * (HALF * 16) + d * 16, 8)
            growth_a = jnp.maximum(wa0 * COS[d] + wa1 * SIN[d] + (1.0 - GROWTH), 1.0)
            growth_b = jnp.maximum(wb0 * COS[d] + wb1 * SIN[d] + (1.0 - GROWTH), 1.0)
            out[pl.ds(start + 2 * d + odd, 8, stride=ND), :] = (
                ref[pl.ds(at, 8), :] * gain_a * growth_a
            )
            out[pl.ds(start + 2 * d + 1 - odd, 8, stride=ND), :] = (
                ref[pl.ds(at + 8, 8), :] * gain_b * growth_b
            )
        return coupling * FREQ_STEP**GF, weight + GF / NF

    k = lax.broadcasted_iota(jnp.int32, (8, LANES), 0)
    coupling = jnp.zeros((8, LANES), jnp.float32)
    for i in range(GF):
        for h in range(2):
            value = GROWTH * WIND_COUPLING * FREQ_STEP**i * (1.0 - 2.0 * h)
            coupling = jnp.where(k == 2 * i + h, value, coupling)
    carry = (coupling, freq_weight())
    carry = lax.fori_loop(0, DIRECT_GROUPS, functools.partial(one_group, 0, done), carry)
    lax.fori_loop(0, later, functools.partial(one_group, DIRECT_GROUPS, turned), carry)


def geometry_table(bands):
    total = 2 * bands

    def angle(position):
        return (LAT_SOUTH + (LAT_NORTH - LAT_SOUTH) * position / total) * (math.pi / 180.0)

    table = np.zeros((bands, 8), np.float32)
    for b in range(bands):
        cells = [angle(2 * b + 0.5), angle(2 * b + 1.5)]
        faces = [angle(2 * b), angle(2 * b + 1), angle(2 * b + 2)]
        icos = [1.0 / math.cos(v) for v in cells]
        near, far = (0, 1) if b % 2 == 0 else (1, 0)
        face_a, face_b = (faces[0], faces[2]) if b % 2 == 0 else (faces[2], faces[0])
        table[b] = [
            icos[0],
            icos[1],
            math.cos(face_a) * icos[near],
            math.cos(faces[1]) * icos[near],
            math.cos(faces[1]) * icos[far],
            math.cos(face_b) * icos[far],
            -TURNING * math.tan(cells[near]),
            -TURNING * math.tan(cells[far]),
        ]
    return table


def speed_table():
    table = np.zeros((2, WIDE), np.float32)
    for k in range(NF * ND):
        value = SPEED_TOP * FREQ_STEP ** -(k // ND) * math.cos(2.0 * math.pi * (k % ND) / ND)
        table[0, 2 * k] = value
        table[1, 2 * k + 1] = value
    return table


VMEM = pl.BlockSpec(memory_space=pltpu.VMEM)
SMEM = pl.BlockSpec(memory_space=pltpu.SMEM)
ANY = pl.BlockSpec(memory_space=pl.ANY)
PARAMS = pltpu.CompilerParams(vmem_limit_bytes=40 * 1024 * 1024)


def call(kernel, name, operands, specs, shapes, scratch, micros):
    outs = [jax.ShapeDtypeStruct(s, jnp.float32) for s in shapes]
    return pl.pallas_call(
        kernel,
        name=name,
        out_shape=outs,
        in_specs=specs,
        out_specs=[VMEM] * len(outs),
        scratch_shapes=scratch,
        compiler_params=PARAMS,
        cost_estimate=pl.CostEstimate(
            flops=0, bytes_accessed=int(micros * 3.0e6), transcendentals=0
        ),
    )(*operands)


def per_device(bands, spec_count, spectra, sea_mask, wind, current):
    comp_count, row_count, col_count = spectra.shape
    cells = spectra.reshape(comp_count * row_count, col_count)
    middle = bands // 2 - 1
    direct_rows = DIRECT_GROUPS * GROUP_ROWS

    side_pairs = [(b, b + 1) for b in range(1, bands - 1, 2) if b != middle]
    both_ways = side_pairs + [(t, s) for s, t in side_pairs]
    straight = lax.ppermute(cells, "band", both_ways)
    relay = lax.ppermute(
        cells[direct_rows:], "band", [(middle, bands - 1), (middle + 1, 0)]
    )
    direct = lax.ppermute(
        cells[:direct_rows], "band", [(middle, middle + 1), (middle + 1, middle)]
    )
    relayed = lax.ppermute(relay, "band", [(bands - 1, middle + 1), (0, middle)])

    pairs = [(b, b + 1) for b in range(0, bands, 2)]
    beyond = lax.ppermute(cells, "band", pairs + [(t, s) for s, t in pairs])

    (packed,) = call(
        functools.partial(pack_kernel, bands),
        "pack_forcing",
        (wind, current, sea_mask),
        [VMEM] * 3,
        [(bands, 16, LANES)],
        [pltpu.VMEM((4, 16 + wind.shape[1], LANES), jnp.float32)],
        0.5,
    )
    relaid = lax.all_to_all(packed, "band", split_axis=0, concat_axis=0, tiled=True)
    par, west, east = call(
        functools.partial(edge_kernel, bands),
        "edges",
        (jnp.asarray(geometry_table(bands)), relaid, cells, sea_mask),
        [SMEM, VMEM, VMEM, VMEM],
        [(PAR_ROWS, LANES), (2, WIDE), (2, WIDE)],
        [pltpu.VMEM((LANES, LANES), jnp.float32)],
        1.5,
    )
    ring = [(s, (s + 1) % spec_count) for s in range(spec_count)]
    from_west = lax.ppermute(east, "spec", ring)
    from_east = lax.ppermute(west, "spec", [(t, s) for s, t in ring])
    (base,) = call(
        base_kernel,
        "base",
        (jnp.asarray(speed_table()), par, cells, beyond, west, east, from_west, from_east),
        [VMEM] * 8,
        [(ROWS, LANES)],
        [pltpu.VMEM((LANES, WIDE), jnp.float32), pltpu.VMEM((WIDE, LANES), jnp.float32)],
        6.0,
    )
    later_rows = ROWS - direct_rows
    turned, total = call(
        functools.partial(first_kernel, bands),
        "first_groups",
        (par, base[:direct_rows], straight, direct),
        [VMEM, VMEM, ANY, ANY],
        [(direct_rows, LANES), (16, LANES)],
        [pltpu.VMEM((direct_rows, LANES), jnp.float32), pltpu.SemaphoreType.DMA],
        2.0,
    )
    (out,) = call(
        functools.partial(last_kernel, bands),
        "last_groups",
        (par, base[direct_rows:], straight, relayed, turned, total),
        [VMEM, VMEM, ANY, ANY, VMEM, VMEM],
        [(ROWS, LANES)],
        [
            pltpu.VMEM((later_rows, LANES), jnp.float32),
            pltpu.VMEM((later_rows, LANES), jnp.float32),
            pltpu.SemaphoreType.DMA,
        ],
        3.0,
    )
    return out.reshape(comp_count, row_count, col_count)


def solution(mesh):
    placed = (
        P(None, "band", "spec"),
        P("band", "spec"),
        P(None, None, ("spec", "band")),
        P(None, None, ("spec", "band")),
    )
    return jax.shard_map(
        functools.partial(per_device, mesh.shape["band"], mesh.shape["spec"]),
        mesh=mesh,
        in_specs=placed,
        out_specs=P(None, "band", "spec"),
        check_vma=False,
    )
```

time: 93.7 us -> 48.1 us (0.51); the launches traced: 92.1 us -> 47.8 us
  other arithmetic: 61.8 us -> 0 us
  waiting for transfers between devices: 0.07 us -> 14.2 us
  local copies, waits for them, and re-layouts: 15.9 us -> 2.39 us
  blocking collectives: 0 us -> 12.5 us
  Pallas kernels: 0 us -> 8.46 us
  starting transfers between devices: 14 us -> 10.1 us
    mul x13 -> x0, other arithmetic: 26.2 us -> none  [the longest x2 18.9 us: face_flux(): return courant * face_value]
    concatenate x4 -> x0, other arithmetic: 20 us -> none  [the longest x2 13.3 us: padded(): block = jnp.concatenate([low, block, high], axis=dim)]
    ppermute x4 -> x7, waiting for transfers between devices: 0.07 us -> 14.2 us  [the longest x1 8.62 us: per_device(): lax.ppermute(cells[direct_rows:], 'band', [(middle, bands - 1), (middle +...]
    all_to_all x0 -> x1, blocking collectives: none -> 12.5 us  [per_device(): lax.all_to_all(packed, 'band', split_axis=0, concat_axis=0, tiled=True)]
    pallas_call x0 -> x5, Pallas kernels: none -> 8.46 us  [call(): pl.pallas_call(kernel, name=name, out_shape=outs, in_specs=specs, out_spe...]
    add x6 -> x0, other arithmetic: 6.16 us -> none  [the longest x2 4.24 us: propagate(): north_speed = (group_speed * sin_dir)[:, None, None] + current_tall[1][None]]
    all_to_all x1 -> x0, starting transfers between devices: 5.17 us -> none  [per_device(): lax.all_to_all(forcing, 'band', split_axis=1, concat_axis=2, tiled=True)]
    ppermute x2 -> x0, local copies, waits for them, and re-layouts: 4.14 us -> none  [the longest x1 2.67 us: padded(): lax.ppermute(lax.slice_in_dim(block, 0, width, axis=dim), axis, backward)]
  transfers between devices with their start and end apart: 5 -> 7, of which waited for: 1 -> 3; matrix products, arithmetic and copies ran while one was open for 45% -> 5% of each run, Pallas kernels for 0% -> 13%
where the time goes in v1:
time: 48.1 us; the launch traced here: 47.8 us
  waiting for transfers between devices  14.2 us (30%)
  blocking collectives  12.5 us (26%)
  starting transfers between devices  10.1 us (21%)
  Pallas kernels  8.46 us (18%)
  local copies, waits for them, and re-layouts  2.39 us (5%)
    all_to_all x1, blocking collectives, per_device(): lax.all_to_all(packed, 'band', split_axis=0, concat_axis=0, tiled=True)  12.5 us
    ppermute x1, waiting for transfers between devices, per_device(): lax.ppermute(cells[direct_rows:], 'band', [(middle, bands - 1), (middle +...  8.62 us
    pallas_call x5, Pallas kernels, call(): pl.pallas_call(kernel, name=name, out_shape=outs, in_specs=specs, out_spe...  8.46 us
    ppermute x1, waiting for transfers between devices, per_device(): from_west = lax.ppermute(east, 'spec', ring)  3.8 us
    ppermute x1, starting transfers between devices, per_device(): lax.ppermute(relay, 'band', [(bands - 1, middle + 1), (0, middle)])  2.68 us
    ppermute x1, starting transfers between devices, per_device(): from_west = lax.ppermute(east, 'spec', ring)  2.11 us
    ppermute x1, starting transfers between devices, per_device(): from_east = lax.ppermute(west, 'spec', [(t, s) for s, t in ring])  2.02 us
    ppermute x1, waiting for transfers between devices, per_device(): from_east = lax.ppermute(west, 'spec', [(t, s) for s, t in ring])  1.77 us
  transfers between devices with their start and end apart: 7, of which 3 were waited for; matrix products, arithmetic and copies ran while one was open for 5% of the time, Pallas kernels for 13%

profile of v1, /device:TPU:0, one launch (start us, length us, event | category | flops | bytes accessed | tf_op | source)
XLA Modules:
  0.0 47.8 jit_solution(7857891059950840478)
XLA Ops:
  0.0 0.0 copy-start.2
  0.0 0.0 copy-start.3
  0.0 0.0 copy-start.5
  0.0 0.0 copy-start
  0.0 0.0 copy-start.4
  0.0 0.5 %collective-permute-start = (f32[2592,128]{1,0:T(8,128)}, f32[2592,128]{1,0:T(8,128)S(1)}, u32[]{:S(2)}, u32[]{:S(2)}) collective-permute-start(f32[2592,128]{1,0:T(8,128)} %bitcast.4), channel_id=1, source_target_pairs={{0,4},{8,12},{16,20},{24,28},{4,0},{12,8},{20,16},{28,24},{1,5},{9... | collective-permute-start | bytes 3981320 | tf_op jit(solution)/shard_map/ppermute | solution.py:485
  0.6 0.7 %collective-permute-start.3 = (f32[2592,128]{1,0:T(8,128)}, f32[2592,128]{1,0:T(8,128)S(1)}, u32[]{:S(2)}, u32[]{:S(2)}) collective-permute-start(f32[2592,128]{1,0:T(8,128)} %bitcast.5), channel_id=1, source_target_pairs={{4,8},{20,24},{8,4},{24,20},{5,9},{21,25},{9,5},{25,21},{6,10},{22... | collective-permute-start | bytes 3981320 | tf_op jit(solution)/shard_map/ppermute | solution.py:475
  1.3 1.1 %slice.19 = f32[576,2,128]{2,1,0:T(2,128)S(1)} slice(f32[1296,2,128]{2,1,0:T(2,128)} %param.6), slice={[720:1296], [0:2], [0:128]} | slice | bytes 1179648 | tf_op jit(solution)/shard_map/slice | solution.py:477
  2.4 0.0 copy-start.1
  2.4 1.3 %collective-permute-start.4 = (f32[1152,128]{1,0:T(8,128)S(1)}, f32[1152,128]{1,0:T(8,128)S(1)}, u32[]{:S(2)}, u32[]{:S(2)}) collective-permute-start(f32[1152,128]{1,0:T(8,128)S(1)} %bitcast.9), channel_id=1, source_target_pairs={{12,28},{16,0},{13,29},{17,1},{14,30},{18,2},{15,31},{19,3}} | collective-permute-start | bytes 1769480 | tf_op jit(solution)/shard_map/ppermute | solution.py:476
  3.7 1.2 %slice.22 = f32[720,2,128]{2,1,0:T(2,128)S(1)} slice(f32[1296,2,128]{2,1,0:T(2,128)} %param.6), slice={[0:720], [0:2], [0:128]} | slice | bytes 1474560 | tf_op jit(solution)/shard_map/slice | solution.py:480
  4.9 0.7 %collective-permute-start.6 = (f32[1440,128]{1,0:T(8,128)S(1)}, f32[1440,128]{1,0:T(8,128)S(1)}, u32[]{:S(2)}, u32[]{:S(2)}) collective-permute-start(f32[1440,128]{1,0:T(8,128)S(1)} %bitcast.8), channel_id=1, source_target_pairs={{12,16},{16,12},{13,17},{17,13},{14,18},{18,14},{15,19},{19,15}} | collective-permute-start | bytes 2211848 | tf_op jit(solution)/shard_map/ppermute | solution.py:479
  5.6 8.6 %collective-permute-done.4 = f32[1152,128]{1,0:T(8,128)S(1)} collective-permute-done((f32[1152,128]{1,0:T(8,128)S(1)}, f32[1152,128]{1,0:T(8,128)S(1)}, u32[]{:S(2)}, u32[]{:S(2)}) %collective-permute-start.4) | collective-permute-done | bytes 589856 | tf_op jit(solution)/shard_map/ppermute | solution.py:476
  14.2 2.7 %collective-permute-start.5 = (f32[1152,128]{1,0:T(8,128)S(1)}, f32[1152,128]{1,0:T(8,128)S(1)}, u32[]{:S(2)}, u32[]{:S(2)}) collective-permute-start(f32[1152,128]{1,0:T(8,128)S(1)} %collective-permute-done.4), channel_id=1, source_target_pairs={{28,16},{0,12},{29,17},{1,13},{30,18},{2,14},{31,19},{3,15}} | collective-permute-start | bytes 1769480 | tf_op jit(solution)/shard_map/ppermute | solution.py:482
  16.9 0.0 copy-done.2
  16.9 0.0 copy-done.3
  16.9 0.0 copy-done.5
  16.9 0.1 pack_forcing.1
  17.0 12.5 %all_to_all.5.relaid = f32[8,16,128]{2,1,0:T(8,128)S(1)} all-to-all(f32[8,16,128]{2,1,0:T(8,128)S(1)} %pack_forcing.1), channel_id=1, replica_groups=mesh['band'=8,'spec'=4] {'band'}, dimensions={0} | all-to-all | bytes 131072 | tf_op jit(solution)/shard_map/all_to_all | solution.py:496
  29.6 0.0 copy-done
  29.6 0.0 copy-done.4
  29.6 1.0 %edges.1 = (f32[32,128]{1,0:T(8,128)S(1)}, f32[2,2688]{1,0:T(2,128)S(1)}, f32[2,2688]{1,0:T(2,128)S(1)}) custom-call(f32[8,8]{1,0:T(8,128)S(1)} %copy-done.4, f32[8,16,128]{2,1,0:T(8,128)S(1)} %all_to_all.5.relaid, f32[2592,128]{1,0:T(8,128)S(1)} %bitcast.6, s32[2,128]{1,0:T(2,128)S(1)} %copy-done.5), custom_call_target="tpu_custom_call" | custom-call | bytes 4500000 | tf_op jit(solution)/shard_map/edges/pallas_call | solution.py:453
  30.6 2.1 %collective-permute-start.1 = (f32[2,2688]{1,0:T(2,128)S(1)}, f32[2,2688]{1,0:T(2,128)S(1)}, u32[]{:S(2)}, u32[]{:S(2)}) collective-permute-start(f32[2,2688]{1,0:T(2,128)S(1)} %get-tuple-element.12.east), channel_id=1, source_target_pairs={{0,1},{1,2},{2,3},{3,0},{4,5},{5,6},{6,7},{7,4},{8,9},{9,10},{10,1... | collective-permute-start | bytes 64520 | tf_op jit(solution)/shard_map/ppermute | solution.py:507
  32.7 3.8 %collective-permute-done.1.from_west = f32[2,2688]{1,0:T(2,128)S(1)} collective-permute-done((f32[2,2688]{1,0:T(2,128)S(1)}, f32[2,2688]{1,0:T(2,128)S(1)}, u32[]{:S(2)}, u32[]{:S(2)}) %collective-permute-start.1) | collective-permute-done | bytes 21536 | tf_op jit(solution)/shard_map/ppermute | solution.py:507
  36.5 2.0 %collective-permute-start.2 = (f32[2,2688]{1,0:T(2,128)S(1)}, f32[2,2688]{1,0:T(2,128)S(1)}, u32[]{:S(2)}, u32[]{:S(2)}) collective-permute-start(f32[2,2688]{1,0:T(2,128)S(1)} %get-tuple-element.11.west), channel_id=1, source_target_pairs={{1,0},{2,1},{3,2},{0,3},{5,4},{6,5},{7,6},{4,7},{9,8},{10,9},{11,1... | collective-permute-start | bytes 64520 | tf_op jit(solution)/shard_map/ppermute | solution.py:508
  38.5 1.8 %collective-permute-done.2.from_east = f32[2,2688]{1,0:T(2,128)S(1)} collective-permute-done((f32[2,2688]{1,0:T(2,128)S(1)}, f32[2,2688]{1,0:T(2,128)S(1)}, u32[]{:S(2)}, u32[]{:S(2)}) %collective-permute-start.2) | collective-permute-done | bytes 21536 | tf_op jit(solution)/shard_map/ppermute | solution.py:508
  40.3 0.0 collective-permute-done.beyond
  40.3 0.0 copy-done.1
  40.3 3.8 %base.1 = f32[2592,128]{1,0:T(8,128)S(1)} custom-call(f32[2,2688]{1,0:T(2,128)S(1)} %copy-done.1, f32[32,128]{1,0:T(8,128)S(1)} %get-tuple-element.10.par, f32[2592,128]{1,0:T(8,128)S(1)} %bitcast.7, f32[2592,128]{1,0:T(8,128)S(1)} %collective-permute-done.beyond, f32[2,2688]{1,0:T(2,128)S(1)} %get-tuple-element.11.west, ...), custom_call_target="tpu_custom_call" | custom-call | bytes 18000000 | tf_op jit(solution)/shard_map/base/pallas_call | solution.py:453
  44.2 0.0 collective-permute-done.6.split
  44.2 0.0 collective-permute-done.3.straight
  44.2 1.3 %first_groups.1 = (f32[1440,128]{1,0:T(8,128)S(1)}, f32[16,128]{1,0:T(8,128)S(1)}) custom-call(f32[32,128]{1,0:T(8,128)S(1)} %get-tuple-element.10.par, f32[1440,128]{1,0:T(8,128)S(1)} %slice.25.base, f32[2592,128]{1,0:T(8,128)S(1)} %collective-permute-done.3.straight, f32[1440,128]{1,0:T(8,128)S(1)} %collective-permute-done.6.split), custom_call_target="tpu_custom_call" | custom-call | bytes 6000000 | tf_op jit(solution)/shard_map/first_groups/pallas_call | solution.py:453
  45.5 0.0 collective-permute-done.5.split
  45.5 2.3 %last_groups.1 = f32[2592,128]{1,0:T(8,128)} custom-call(f32[32,128]{1,0:T(8,128)S(1)} %get-tuple-element.10.par, f32[1152,128]{1,0:T(8,128)S(1)} %slice.24.base, f32[2592,128]{1,0:T(8,128)S(1)} %collective-permute-done.3.straight, f32[1152,128]{1,0:T(8,128)S(1)} %collective-permute-done.5.split, f32[1440,128]{1,0:T(8,128)S(1)} %get-tuple-element.13.done, ...), custom_call_target="tpu_custom_call" | custom-call | bytes 9000000 | tf_op jit(solution)/shard_map/last_groups/pallas_call | solution.py:453
  (2 shorter events, 0.1 us)
Async XLA Ops:
  0.0 16.9 %copy-start.2 = (f32[2,16,16]{2,1,0:T(8,128)S(1)}, f32[2,16,16]{2,1,0:T(8,128)}, u32[]{:S(2)}) copy-start(f32[2,16,16]{2,1,0:T(8,128)} %wind.1) | copy-start | bytes 6148
  0.0 16.9 %copy-start.3 = (f32[2,16,16]{2,1,0:T(8,128)S(1)}, f32[2,16,16]{2,1,0:T(8,128)}, u32[]{:S(2)}) copy-start(f32[2,16,16]{2,1,0:T(8,128)} %current.1) | copy-start | bytes 6148
  0.0 16.9 %copy-start.5 = (s32[2,128]{1,0:T(2,128)S(1)}, s32[2,128]{1,0:T(2,128)}, u32[]{:S(2)}) copy-start(s32[2,128]{1,0:T(2,128)} %sea.3) | copy-start | bytes 3076
  0.0 29.6 %copy-start = (f32[1296,2,128]{2,1,0:T(2,128)S(1)}, f32[1296,2,128]{2,1,0:T(2,128)}, u32[]{:S(2)}) copy-start(f32[1296,2,128]{2,1,0:T(2,128)} %param.6) | copy-start | bytes 3981316
  0.0 29.6 %copy-start.4 = (f32[8,8]{1,0:T(8,128)S(1)}, f32[8,8]{1,0:T(8,128)}, u32[]{:S(2)}) copy-start(f32[8,8]{1,0:T(8,128)} %constant.4.clone.geometry) | copy-start | bytes 772
  0.0 40.3 %collective-permute-start = (f32[2592,128]{1,0:T(8,128)}, f32[2592,128]{1,0:T(8,128)S(1)}, u32[]{:S(2)}, u32[]{:S(2)}) collective-permute-start(f32[2592,128]{1,0:T(8,128)} %bitcast.4), channel_id=1, source_target_pairs={{0,4},{8,12},{16,20},{24,28},{4,0},{12,8},{20,16},{28,24},{1,5},{9... | collective-permute-start | bytes 3981320 | tf_op jit(solution)/shard_map/ppermute | solution.py:485
  0.6 43.7 %collective-permute-start.3 = (f32[2592,128]{1,0:T(8,128)}, f32[2592,128]{1,0:T(8,128)S(1)}, u32[]{:S(2)}, u32[]{:S(2)}) collective-permute-start(f32[2592,128]{1,0:T(8,128)} %bitcast.5), channel_id=1, source_target_pairs={{4,8},{20,24},{8,4},{24,20},{5,9},{21,25},{9,5},{25,21},{6,10},{22... | collective-permute-start | bytes 3981320 | tf_op jit(solution)/shard_map/ppermute | solution.py:475
  2.4 37.9 %copy-start.1 = (f32[2,2688]{1,0:T(2,128)S(1)}, f32[2,2688]{1,0:T(2,128)}, u32[]{:S(2)}) copy-start(f32[2,2688]{1,0:T(2,128)} %constant.5.clone.table) | copy-start | bytes 64516
  2.4 11.8 %collective-permute-start.4 = (f32[1152,128]{1,0:T(8,128)S(1)}, f32[1152,128]{1,0:T(8,128)S(1)}, u32[]{:S(2)}, u32[]{:S(2)}) collective-permute-start(f32[1152,128]{1,0:T(8,128)S(1)} %bitcast.9), channel_id=1, source_target_pairs={{12,28},{16,0},{13,29},{17,1},{14,30},{18,2},{15,31},{19,3}} | collective-permute-start | bytes 1769480 | tf_op jit(solution)/shard_map/ppermute | solution.py:476
  4.9 39.3 %collective-permute-start.6 = (f32[1440,128]{1,0:T(8,128)S(1)}, f32[1440,128]{1,0:T(8,128)S(1)}, u32[]{:S(2)}, u32[]{:S(2)}) collective-permute-start(f32[1440,128]{1,0:T(8,128)S(1)} %bitcast.8), channel_id=1, source_target_pairs={{12,16},{16,12},{13,17},{17,13},{14,18},{18,14},{15,19},{19,15}} | collective-permute-start | bytes 2211848 | tf_op jit(solution)/shard_map/ppermute | solution.py:479
  14.2 31.3 %collective-permute-start.5 = (f32[1152,128]{1,0:T(8,128)S(1)}, f32[1152,128]{1,0:T(8,128)S(1)}, u32[]{:S(2)}, u32[]{:S(2)}) collective-permute-start(f32[1152,128]{1,0:T(8,128)S(1)} %collective-permute-done.4), channel_id=1, source_target_pairs={{28,16},{0,12},{29,17},{1,13},{30,18},{2,14},{31,19},{3,15}} | collective-permute-start | bytes 1769480 | tf_op jit(solution)/shard_map/ppermute | solution.py:482
  30.6 5.9 %collective-permute-start.1 = (f32[2,2688]{1,0:T(2,128)S(1)}, f32[2,2688]{1,0:T(2,128)S(1)}, u32[]{:S(2)}, u32[]{:S(2)}) collective-permute-start(f32[2,2688]{1,0:T(2,128)S(1)} %get-tuple-element.12.east), channel_id=1, source_target_pairs={{0,1},{1,2},{2,3},{3,0},{4,5},{5,6},{6,7},{7,4},{8,9},{9,10},{10,1... | collective-permute-start | bytes 64520 | tf_op jit(solution)/shard_map/ppermute | solution.py:507
  36.5 3.8 %collective-permute-start.2 = (f32[2,2688]{1,0:T(2,128)S(1)}, f32[2,2688]{1,0:T(2,128)S(1)}, u32[]{:S(2)}, u32[]{:S(2)}) collective-permute-start(f32[2,2688]{1,0:T(2,128)S(1)} %get-tuple-element.11.west), channel_id=1, source_target_pairs={{1,0},{2,1},{3,2},{0,3},{5,4},{6,5},{7,6},{4,7},{9,8},{10,9},{11,1... | collective-permute-start | bytes 64520 | tf_op jit(solution)/shard_map/ppermute | solution.py:508

commit v2 on v1

--- a/solution.py
+++ b/solution.py
@@ -23,7 +23,7 @@
 GF = 4
 GROUPS = NF // GF
 GROUP_ROWS = GF * ND * 2
-DIRECT_GROUPS = 5
+FIRST_GROUPS = 4
 LANES = 128
 ROWS = NF * ND * 2
 WIDE = -(-(ROWS + 2) // LANES) * LANES
@@ -99,43 +99,42 @@
     return jnp.broadcast_to(par[index : index + 1, :], (8, LANES))
 
 
-def pack_kernel(bands, wind, current, sea, out, line):
+def pack_kernel(wind, current, sea, out):
     me = lax.axis_index("band")
     rows, strip = wind.shape[1], wind.shape[2]
-
-    def placed(ref, part):
-        empty = jnp.zeros((rows, LANES - strip), jnp.float32)
-        return pltpu.roll(jnp.concatenate([ref[part], empty], axis=1), me * strip, 1)
-
-    empty = jnp.zeros((8, LANES), jnp.float32)
-    line[0, 0:8, :] = empty
-    line[0, 8 + rows : 16 + rows, :] = empty
-    line[0, 8 : 8 + rows, :] = placed(current, 1)
-    line[1, 8 : 8 + rows, :] = placed(current, 0)
-    line[2, 8 : 8 + rows, :] = placed(wind, 0)
-    line[3, 8 : 8 + rows, :] = placed(wind, 1)
+    empty = jnp.zeros((rows, LANES - strip), jnp.float32)
+    for part, ref in enumerate((current, wind)):
+        for axis in range(2):
+            wide = jnp.concatenate([ref[axis], empty], axis=1)
+            out[2 * part + axis] = pltpu.roll(wide, me * strip, 1)
+    out[4] = jnp.zeros((rows, LANES), jnp.float32)
     seas = sea[...].astype(jnp.float32)
-    for t in range(bands):
-        at = 8 + 2 * t
-        out[t, 0:4, :] = line[0, at - 1 : at + 3, :]
-        for part in range(1, 4):
-            out[t, 2 + 2 * part : 4 + 2 * part, :] = line[part, at : at + 2, :]
-        out[t, 10:12, :] = seas
-        out[t, 12:16, :] = jnp.zeros((4, LANES), jnp.float32)
-
-
-def edge_kernel(bands, geometry, relaid, spectra, sea, par, west, east, line):
+    out[4, pl.ds(2 * me, 1), :] = seas[0:1]
+    out[4, pl.ds(2 * me + 1, 1), :] = seas[1:2]
+
+
+def split_kernel(spectra, relayed, direct):
+    relayed[...] = spectra[0 : relayed.shape[0], :]
+    direct[...] = spectra[relayed.shape[0] :, :]
+
+
+def edge_kernel(bands, geometry, forcing, spectra, par, west, east, line):
     me = lax.axis_index("band")
-    odd = lax.rem(me, 2)
-    is_even = odd == 0
-    forcing = relaid[0]
-    for source in range(1, bands):
-        forcing = forcing + relaid[source]
+    is_even = lax.rem(me, 2) == 0
+    row = 2 * me
     has_south = jnp.where(me > 0, 1.0, 0.0)
     has_north = jnp.where(me < bands - 1, 1.0, 0.0)
-    sea_south = relaid[jnp.maximum(me - 1, 0)][10:12] * has_south
-    sea_north = relaid[jnp.minimum(me + 1, bands - 1)][10:12] * has_north
-    seas = sea[...].astype(jnp.float32)
+
+    def around(part):
+        south = [jnp.maximum(row - 2, 0), jnp.maximum(row - 1, 0)]
+        north = [jnp.minimum(row + 2, 2 * bands - 1), jnp.minimum(row + 3, 2 * bands - 1)]
+        return (
+            [forcing[part, pl.ds(i, 1), :] * has_south for i in south]
+            + [forcing[part, pl.ds(row + i, 1), :] for i in range(2)]
+            + [forcing[part, pl.ds(i, 1), :] * has_north for i in north]
+        )
+
+    seas = around(4)
 
     def pick(low, high):
         return jnp.where(is_even, low, high)
@@ -144,27 +143,28 @@
         par[index : index + 1, :] = jnp.broadcast_to(value, (1, LANES))
 
     tau = jnp.where(is_even, 1.0, -1.0)
-    north = [forcing[i : i + 1] for i in range(4)]
-    face = [0.5 * (north[i] + north[i + 1]) for i in range(3)]
+    north = around(1)
+    face = [0.5 * (north[i] + north[i + 1]) for i in range(1, 4)]
     put(CUR_A, tau * pick(face[0], face[2]))
     put(CUR_M, tau * face[1])
     put(CUR_B, tau * pick(face[2], face[0]))
     lane = lax.broadcasted_iota(jnp.int32, (1, LANES), 1)
     inside = jnp.where(lane == 0, 0.0, 1.0)
-    east_speed = [forcing[4:5], forcing[5:6]]
+    east_speed = around(0)[2:4]
+    wind_0, wind_1 = around(2)[2:4], around(3)[2:4]
     shifted = [0.5 * inside * (v + pltpu.roll(v, 1, 1)) for v in east_speed]
     put(CX_A, pick(shifted[0], shifted[1]))
     put(CX_B, pick(shifted[1], shifted[0]))
-    put(W0_A, pick(forcing[6:7], forcing[7:8]))
-    put(W0_B, pick(forcing[7:8], forcing[6:7]))
-    put(W1_A, pick(forcing[8:9], forcing[9:10]))
-    put(W1_B, pick(forcing[9:10], forcing[8:9]))
-    put(SEA_A, pick(seas[0:1], seas[1:2]))
-    put(SEA_B, pick(seas[1:2], seas[0:1]))
-    put(SEA_A1, pick(sea_south[1:2], sea_north[0:1]))
-    put(SEA_A2, pick(sea_south[0:1], sea_north[1:2]))
-    put(SEA_B1, pick(sea_north[0:1], sea_south[1:2]))
-    put(SEA_B2, pick(sea_north[1:2], sea_south[0:1]))
+    put(W0_A, pick(wind_0[0], wind_0[1]))
+    put(W0_B, pick(wind_0[1], wind_0[0]))
+    put(W1_A, pick(wind_1[0], wind_1[1]))
+    put(W1_B, pick(wind_1[1], wind_1[0]))
+    put(SEA_A, pick(seas[2], seas[3]))
+    put(SEA_B, pick(seas[3], seas[2]))
+    put(SEA_A1, pick(seas[1], seas[4]))
+    put(SEA_A2, pick(seas[0], seas[5]))
+    put(SEA_B1, pick(seas[4], seas[1]))
+    put(SEA_B2, pick(seas[5], seas[0]))
     put(TAU, tau)
     icos = [geometry[me, 0], geometry[me, 1]]
     put(ICOS_A, inside * pick(icos[0], icos[1]))
@@ -182,8 +182,8 @@
     sub = lax.broadcasted_iota(jnp.int32, (LANES, LANES), 0)
     both = jnp.where(
         lax.rem(sub, 2) == 0,
-        jnp.broadcast_to(seas[0:1], (LANES, LANES)),
-        jnp.broadcast_to(seas[1:2], (LANES, LANES)),
+        jnp.broadcast_to(seas[2], (LANES, LANES)),
+        jnp.broadcast_to(seas[3], (LANES, LANES)),
     )
     full = ROWS // LANES
     for block in range(WIDE // LANES):
@@ -194,15 +194,15 @@
             left = ROWS - at
             line[...] = jnp.zeros((LANES, LANES), jnp.float32)
             line[0:left, :] = spectra[at : at + left, :] * both[0:left]
-            line[left : left + 2, :] = forcing[4:6]
+            line[left : left + 1, :] = east_speed[0]
+            line[left + 1 : left + 2, :] = east_speed[1]
             cells = line[...]
         turned = cells.T
         west[:, at : at + LANES] = turned[0:2]
         east[:, at : at + LANES] = turned[LANES - 2 : LANES]
 
 
-def base_kernel(table, par, spectra, beyond, west, east, from_west, from_east, base, tall, fix):
-    odd = lax.rem(lax.axis_index("band"), 2)
+def fix_kernel(table, par, west, east, from_west, from_east, fix, tall):
     lane = lax.broadcasted_iota(jnp.int32, (1, WIDE), 1)
     even_row = lax.rem(lane, 2) == 0
     speed = table[0:1] * par[ICOS_0 : ICOS_0 + 1, 0:1] + table[1:2] * par[ICOS_1 : ICOS_1 + 1, 0:1]
@@ -235,6 +235,9 @@
         at = block * LANES
         fix[at : at + LANES, :] = tall[:, at : at + LANES].T
 
+
+def base_kernel(par, spectra, beyond, base_first, base_last):
+    odd = lax.rem(lax.axis_index("band"), 2)
     sea_a, sea_b = wide_row(par, SEA_A), wide_row(par, SEA_B)
     sea_b1, sea_b2 = wide_row(par, SEA_B1), wide_row(par, SEA_B2)
     cur_a, cur_m, cur_b = wide_row(par, CUR_A), wide_row(par, CUR_M), wide_row(par, CUR_B)
@@ -254,8 +257,8 @@
         )
         return crossing - pltpu.roll(crossing, LANES - 1, 1)
 
-    def one_group(g, speeds):
-        start = g * GROUP_ROWS
+    def one_group(base, first, g, speeds):
+        start = (first + g) * GROUP_ROWS
         north = speeds * tau
         east_a, east_b = speeds * icos_a, speeds * icos_b
         for d in range(HALF):
@@ -270,14 +273,19 @@
             flux_a = c * (0.5 * (a - c * a) - w * jnp.where(c >= 0.0, a, b - 2.0 * a))
             flux_m = flux(0.0, a, b, b1, north * SIN[d] + cur_m)
             flux_b = flux(a, b, b1, b2, north * SIN[d] + cur_b)
-            to_a = along_east(a, east_a, cx_a, COS[d]) + fix[row_a, :]
-            to_b = along_east(b, east_b, cx_b, COS[d]) + fix[row_b, :]
+            to_a = along_east(a, east_a, cx_a, COS[d])
+            to_b = along_east(b, east_b, cx_b, COS[d])
             at = pl.multiple_of(g * (HALF * 16) + d * 16, 8)
             base[pl.ds(at, 8), :] = a + to_a + kap_a * flux_a - mu_a * flux_m
             base[pl.ds(at + 8, 8), :] = b + to_b + mu_b * flux_m - kap_b * flux_b
         return speeds * FREQ_STEP**-GF
 
-    lax.fori_loop(0, GROUPS, one_group, group_speed())
+    speeds = lax.fori_loop(
+        0, FIRST_GROUPS, functools.partial(one_group, base_first, 0), group_speed()
+    )
+    lax.fori_loop(
+        0, GROUPS - FIRST_GROUPS, functools.partial(one_group, base_last, FIRST_GROUPS), speeds
+    )
 
 
 def turn(cells, rate):
@@ -292,7 +300,8 @@
     return [cells[d] - (fluxes[d] - (fluxes[d - 1] if d else last)) for d in range(HALF)]
 
 
-def finish_groups(first, count, par, base, ahead, turned, odd, total):
+def finish_groups(first, count, skip, par, base, fix, ahead, turned, total):
+    odd = lax.rem(lax.axis_index("band"), 2)
     sea_a1, sea_a2 = wide_row(par, SEA_A1), wide_row(par, SEA_A2)
     cur_a, cur_m = wide_row(par, CUR_A), wide_row(par, CUR_M)
     kap_a, mu_a, mu_b = wide_row(par, KAP_A), wide_row(par, MU_A), wide_row(par, MU_B)
@@ -301,12 +310,15 @@
 
     def one_group(g, carry):
         speeds, weight, sum_a, sum_b = carry
-        start = g * GROUP_ROWS
+        start = (skip + g) * GROUP_ROWS
+        fix_start = (first + g) * GROUP_ROWS
         north = speeds * tau
         cells_a, cells_b = [], []
         for d in range(HALF):
             n1 = ahead[pl.ds(start + 2 * d + 1 - odd, 8, stride=ND), :] * sea_a1
             n2 = ahead[pl.ds(start + 2 * d + odd, 8, stride=ND), :] * sea_a2
+            fix_a = fix[pl.ds(fix_start + 2 * d + odd, 8, stride=ND), :]
+            fix_b = fix[pl.ds(fix_start + 2 * d + 1 - odd, 8, stride=ND), :]
             c = north * SIN[d] + cur_a
             w = (1.0 / 6.0) - (c * c) * (1.0 / 6.0)
             flux_a = c * (0.5 * (n1 + c * n1) - w * jnp.where(c >= 0.0, n2 - 2.0 * n1, n1))
@@ -314,8 +326,8 @@
             w = (c * c) * (1.0 / 6.0) - (1.0 / 6.0)
             flux_m = jnp.where(c >= 0.0, c * w, 0.0) * n1
             at = pl.multiple_of(g * (HALF * 16) + d * 16, 8)
-            cells_a.append(base[pl.ds(at, 8), :] + kap_a * flux_a - mu_a * flux_m)
-            cells_b.append(base[pl.ds(at + 8, 8), :] + mu_b * flux_m)
+            cells_a.append(base[pl.ds(at, 8), :] + fix_a + kap_a * flux_a - mu_a * flux_m)
+            cells_b.append(base[pl.ds(at + 8, 8), :] + fix_b + mu_b * flux_m)
         square_a = square_b = 0.0
         for d, v in enumerate(turn(cells_a, speeds * tan_a)):
             at = pl.multiple_of(g * (HALF * 16) + d * 16, 8)
@@ -335,44 +347,35 @@
     speeds = group_speed() * FREQ_STEP ** -(GF * first)
     weight = freq_weight() + GF * first / NF
     carry = (speeds, weight, total[0:8, :], total[8:16, :])
-    return lax.fori_loop(0, count, one_group, carry)[2:]
-
-
-def fetch(bands, first, count, straight, split, ahead, sem):
+    _, _, total[0:8, :], total[8:16, :] = lax.fori_loop(0, count, one_group, carry)
+
+
+def finish_either(bands, first, count, par, base, fix, straight, split, turned, total):
     me = lax.axis_index("band")
     middle = jnp.logical_or(me == bands // 2 - 1, me == bands // 2)
-    rows = count * GROUP_ROWS
 
     @pl.when(middle)
     def _():
-        copy = pltpu.make_async_copy(split, ahead, sem)
-        copy.start()
-        copy.wait()
+        finish_groups(first, count, 0, par, base, fix, split, turned, total)
 
     @pl.when(jnp.logical_not(middle))
     def _():
-        copy = pltpu.make_async_copy(straight.at[pl.ds(first * GROUP_ROWS, rows)], ahead, sem)
-        copy.start()
-        copy.wait()
-
-
-def first_kernel(bands, par, base, straight, split, turned, total, ahead, sem):
+        finish_groups(first, count, first, par, base, fix, straight, turned, total)
+
+
+def first_kernel(bands, par, base, fix, straight, split, turned, total):
+    total[...] = jnp.zeros((16, LANES), jnp.float32)
+    finish_either(bands, 0, FIRST_GROUPS, par, base, fix, straight, split, turned, total)
+
+
+def last_kernel(bands, par, base, fix, straight, split, done, before, out, turned, total):
     odd = lax.rem(lax.axis_index("band"), 2)
-    fetch(bands, 0, DIRECT_GROUPS, straight, split, ahead, sem)
-    total[...] = jnp.zeros((16, LANES), jnp.float32)
-    sums = finish_groups(0, DIRECT_GROUPS, par, base, ahead, turned, odd, total)
-    total[0:8, :] = sums[0]
-    total[8:16, :] = sums[1]
-
-
-def last_kernel(bands, par, base, straight, split, done, total, out, ahead, turned, sem):
-    odd = lax.rem(lax.axis_index("band"), 2)
-    later = GROUPS - DIRECT_GROUPS
-    fetch(bands, DIRECT_GROUPS, later, straight, split, ahead, sem)
-    sums = finish_groups(DIRECT_GROUPS, later, par, base, ahead, turned, odd, total)
+    later = GROUPS - FIRST_GROUPS
+    total[...] = before[...]
+    finish_either(bands, FIRST_GROUPS, later, par, base, fix, straight, split, turned, total)
     scale = 2.0 / (NF * ND)
-    steep_a = jnp.sum(sums[0], axis=0, keepdims=True) * scale
-    steep_b = jnp.sum(sums[1], axis=0, keepdims=True) * scale
+    steep_a = jnp.sum(total[0:8, :], axis=0, keepdims=True) * scale
+    steep_b = jnp.sum(total[8:16, :], axis=0, keepdims=True) * scale
     sea_a, sea_b = wide_row(par, SEA_A), wide_row(par, SEA_B)
     w0_a, w0_b = wide_row(par, W0_A), wide_row(par, W0_B)
     w1_a, w1_b = wide_row(par, W1_A), wide_row(par, W1_B)
@@ -403,8 +406,8 @@
             value = GROWTH * WIND_COUPLING * FREQ_STEP**i * (1.0 - 2.0 * h)
             coupling = jnp.where(k == 2 * i + h, value, coupling)
     carry = (coupling, freq_weight())
-    carry = lax.fori_loop(0, DIRECT_GROUPS, functools.partial(one_group, 0, done), carry)
-    lax.fori_loop(0, later, functools.partial(one_group, DIRECT_GROUPS, turned), carry)
+    carry = lax.fori_loop(0, FIRST_GROUPS, functools.partial(one_group, 0, done), carry)
+    lax.fori_loop(0, later, functools.partial(one_group, FIRST_GROUPS, turned), carry)
 
 
 def geometry_table(bands):
@@ -464,79 +467,109 @@
     )(*operands)
 
 
+def swapped(pairs):
+    return pairs + [(t, s) for s, t in pairs]
+
+
 def per_device(bands, spec_count, spectra, sea_mask, wind, current):
     comp_count, row_count, col_count = spectra.shape
     cells = spectra.reshape(comp_count * row_count, col_count)
     middle = bands // 2 - 1
-    direct_rows = DIRECT_GROUPS * GROUP_ROWS
-
-    side_pairs = [(b, b + 1) for b in range(1, bands - 1, 2) if b != middle]
-    both_ways = side_pairs + [(t, s) for s, t in side_pairs]
-    straight = lax.ppermute(cells, "band", both_ways)
-    relay = lax.ppermute(
-        cells[direct_rows:], "band", [(middle, bands - 1), (middle + 1, 0)]
-    )
-    direct = lax.ppermute(
-        cells[:direct_rows], "band", [(middle, middle + 1), (middle + 1, middle)]
-    )
-    relayed = lax.ppermute(relay, "band", [(bands - 1, middle + 1), (0, middle)])
-
+    first_rows = FIRST_GROUPS * GROUP_ROWS
+    last_rows = ROWS - first_rows
+
+    straight = lax.ppermute(
+        cells, "band", swapped([(b, b + 1) for b in range(1, bands - 1, 2) if b != middle])
+    )
     pairs = [(b, b + 1) for b in range(0, bands, 2)]
-    beyond = lax.ppermute(cells, "band", pairs + [(t, s) for s, t in pairs])
-
-    (packed,) = call(
-        functools.partial(pack_kernel, bands),
+    beyond = lax.ppermute(cells, "band", swapped(pairs))
+    part_relayed, part_direct = call(
+        split_kernel,
+        "split",
+        (cells,),
+        [VMEM],
+        [(first_rows, LANES), (last_rows, LANES)],
+        [],
+        0.3,
+    )
+
+    (forcing,) = call(
+        pack_kernel,
         "pack_forcing",
         (wind, current, sea_mask),
         [VMEM] * 3,
-        [(bands, 16, LANES)],
-        [pltpu.VMEM((4, 16 + wind.shape[1], LANES), jnp.float32)],
-        0.5,
-    )
-    relaid = lax.all_to_all(packed, "band", split_axis=0, concat_axis=0, tiled=True)
+        [(5, wind.shape[1], LANES)],
+        [],
+        0.3,
+    )
+    forcing = forcing + lax.ppermute(forcing, "band", swapped(pairs))
+    bit = 4
+    while bit < bands:
+        turnabout = [(b, b ^ bit) for b in range(bands)]
+        forcing = forcing + lax.ppermute(forcing, "band", turnabout)
+        bit *= 2
+    part_relayed, forcing = lax.optimization_barrier((part_relayed, forcing))
+    relay = lax.ppermute(part_relayed, "band", [(middle, bands - 1), (middle + 1, 0)])
+    free = [2 * chip + chip % 2 for chip in range(bands // 2)]
+    across = lax.ppermute(
+        forcing, "band", [(b, free[chip ^ 1]) for chip, b in enumerate(free)]
+    )
+    along = lax.ppermute(across, "band", [(b, b ^ 1) for b in free])
+    forcing = forcing + across + along
+    part_direct, forcing = lax.optimization_barrier((part_direct, forcing))
+    direct = lax.ppermute(
+        part_direct, "band", [(middle, middle + 1), (middle + 1, middle)]
+    )
+    relayed = lax.ppermute(relay, "band", [(bands - 1, middle + 1), (0, middle)])
+
     par, west, east = call(
         functools.partial(edge_kernel, bands),
         "edges",
-        (jnp.asarray(geometry_table(bands)), relaid, cells, sea_mask),
-        [SMEM, VMEM, VMEM, VMEM],
+        (jnp.asarray(geometry_table(bands)), forcing, cells),
+        [SMEM, VMEM, VMEM],
         [(PAR_ROWS, LANES), (2, WIDE), (2, WIDE)],
         [pltpu.VMEM((LANES, LANES), jnp.float32)],
-        1.5,
+        1.0,
     )
     ring = [(s, (s + 1) % spec_count) for s in range(spec_count)]
     from_west = lax.ppermute(east, "spec", ring)
     from_east = lax.ppermute(west, "spec", [(t, s) for s, t in ring])
-    (base,) = call(
+    base_first, base_last = call(
         base_kernel,
         "base",
-        (jnp.asarray(speed_table()), par, cells, beyond, west, east, from_west, from_east),
-        [VMEM] * 8,
-        [(ROWS, LANES)],
-        [pltpu.VMEM((LANES, WIDE), jnp.float32), pltpu.VMEM((WIDE, LANES), jnp.float32)],
-        6.0,
-    )
-    later_rows = ROWS - direct_rows
+        (par, cells, beyond),
+        [VMEM] * 3,
+        [(first_rows, LANES), (last_rows, LANES)],
+        [],
+        4.0,
+    )
+    base_first, from_west, from_east = lax.optimization_barrier((base_first, from_west, from_east))
+    (fix,) = call(
+        fix_kernel,
+        "fix",
+        (jnp.asarray(speed_table()), par, west, east, from_west, from_east),
+        [VMEM] * 6,
+        [(WIDE, LANES)],
+        [pltpu.VMEM((LANES, WIDE), jnp.float32)],
+        1.0,
+    )
     turned, total = call(
         functools.partial(first_kernel, bands),
         "first_groups",
-        (par, base[:direct_rows], straight, direct),
-        [VMEM, VMEM, ANY, ANY],
-        [(direct_rows, LANES), (16, LANES)],
-        [pltpu.VMEM((direct_rows, LANES), jnp.float32), pltpu.SemaphoreType.DMA],
-        2.0,
+        (par, base_first, fix, straight, relayed),
+        [VMEM] * 5,
+        [(first_rows, LANES), (16, LANES)],
+        [],
+        1.0,
     )
     (out,) = call(
         functools.partial(last_kernel, bands),
         "last_groups",
-        (par, base[direct_rows:], straight, relayed, turned, total),
-        [VMEM, VMEM, ANY, ANY, VMEM, VMEM],
+        (par, base_last, fix, straight, direct, turned, total),
+        [VMEM] * 7,
         [(ROWS, LANES)],
-        [
-            pltpu.VMEM((later_rows, LANES), jnp.float32),
-            pltpu.VMEM((later_rows, LANES), jnp.float32),
-            pltpu.SemaphoreType.DMA,
-        ],
-        3.0,
+        [pltpu.VMEM((last_rows, LANES), jnp.float32), pltpu.VMEM((16, LANES), jnp.float32)],
+        2.0,
     )
     return out.reshape(comp_count, row_count, col_count)
 

time: 48.1 us -> 43.5 us (0.904)
  blocking collectives: 12.5 us -> 0 us
  starting transfers between devices: 10.1 us -> 22.2 us
  waiting for transfers between devices: 14.2 us -> 9.17 us
  local copies, waits for them, and re-layouts: 2.39 us -> 3.44 us
    all_to_all x1 -> x0, blocking collectives: 12.5 us -> none  [per_device(): lax.all_to_all(packed, 'band', split_axis=0, concat_axis=0, tiled=True)]
    ppermute x4 -> x8, starting transfers between devices: 3.27 us -> 13.3 us  [the longest x1 3.77 us: per_device(): forcing = forcing + lax.ppermute(forcing, 'band', swapped(pairs))]
    unnamed x12 -> x14, local copies, waits for them, and re-layouts: 0.03 us -> 3.44 us
    ppermute x1, starting transfers between devices: 2.68 us -> 5.22 us  [per_device(): lax.ppermute(relay, 'band', [(bands - 1, middle + 1), (0, middle)])]
    slice x4 -> x0, local copies, waits for them, and re-layouts: 2.36 us -> none  [the longest x1 1.17 us: per_device(): cells[:direct_rows]]
    ppermute x1, starting transfers between devices: 2.11 us -> 0.01 us  [per_device(): from_west = lax.ppermute(east, 'spec', ring)]
    ppermute x4 -> x8, waiting for transfers between devices: 8.63 us -> 6.81 us  [the longest x1 2.23 us: per_device(): lax.ppermute(forcing, 'band', [(b, free[chip ^ 1]) for chip, b in enumera...]
    ppermute x1, waiting for transfers between devices: 1.77 us -> 0.01 us  [per_device(): from_east = lax.ppermute(west, 'spec', [(t, s) for s, t in ring])]
  transfers between devices with their start and end apart: 7 -> 11, of which waited for: 3 -> 6; matrix products, arithmetic and copies ran while one was open for 5% -> 0% of each run, Pallas kernels for 13% -> 13%
where the time goes in v2:
time: 43.5 us; the launch traced here: 43.1 us
  starting transfers between devices  22.2 us (51%)
  waiting for transfers between devices  9.17 us (21%)
  Pallas kernels  8.12 us (19%)
  local copies, waits for them, and re-layouts  3.44 us (8%)
    pallas_call x7, Pallas kernels, call(): pl.pallas_call(kernel, name=name, out_shape=outs, in_specs=specs, out_spe...  8.12 us
    ppermute x1, starting transfers between devices, per_device(): lax.ppermute(relay, 'band', [(bands - 1, middle + 1), (0, middle)])  5.22 us
    ppermute x1, starting transfers between devices, per_device(): forcing = forcing + lax.ppermute(forcing, 'band', swapped(pairs))  3.77 us
    ppermute x1, starting transfers between devices, per_device(): from_east = lax.ppermute(west, 'spec', [(t, s) for s, t in ring])  3.65 us
    ppermute x1, starting transfers between devices, per_device(): lax.ppermute(forcing, 'band', [(b, free[chip ^ 1]) for chip, b in enumera...  3.59 us
    unnamed x14, local copies, waits for them, and re-layouts  3.44 us
    ppermute x1, waiting for transfers between devices, per_device(): from_west = lax.ppermute(east, 'spec', ring)  2.36 us
    ppermute x1, waiting for transfers between devices, per_device(): lax.ppermute(forcing, 'band', [(b, free[chip ^ 1]) for chip, b in enumera...  2.23 us
  transfers between devices with their start and end apart: 11, of which 6 were waited for; matrix products, arithmetic and copies ran while one was open for 0% of the time, Pallas kernels for 13%

profile of v2, /device:TPU:0, one launch (start us, length us, event | category | flops | bytes accessed | tf_op | source)
XLA Modules:
  0.0 43.1 jit_solution(17020541275060063920)
XLA Ops:
  0.0 0.5 %collective-permute-start.4 = (f32[2592,128]{1,0:T(8,128)}, f32[2592,128]{1,0:T(8,128)S(1)}, u32[]{:S(2)}, u32[]{:S(2)}) collective-permute-start(f32[2592,128]{1,0:T(8,128)} %bitcast.2), channel_id=1, source_target_pairs={{0,4},{8,12},{16,20},{24,28},{4,0},{12,8},{20,16},{28,24},{1,5},{9... | collective-permute-start | bytes 3981320 | tf_op jit(solution)/shard_map/ppermute | solution.py:485
  0.5 0.7 %collective-permute-start.7 = (f32[2592,128]{1,0:T(8,128)}, f32[2592,128]{1,0:T(8,128)S(1)}, u32[]{:S(2)}, u32[]{:S(2)}) collective-permute-start(f32[2592,128]{1,0:T(8,128)} %bitcast.3), channel_id=1, source_target_pairs={{4,8},{20,24},{8,4},{24,20},{5,9},{21,25},{9,5},{25,21},{6,10},{22... | collective-permute-start | bytes 3981320 | tf_op jit(solution)/shard_map/ppermute | solution.py:481
  1.2 0.0 copy-start.3
  1.2 0.7 %copy-done.3 = f32[2,16,16]{2,1,0:T(8,128)S(1)} copy-done((f32[2,16,16]{2,1,0:T(8,128)S(1)}, f32[2,16,16]{2,1,0:T(8,128)}, u32[]{:S(2)}) %copy-start.3) | copy-done | bytes 2072
  1.9 0.0 copy-start.4
  1.9 0.7 %copy-done.4 = f32[2,16,16]{2,1,0:T(8,128)S(1)} copy-done((f32[2,16,16]{2,1,0:T(8,128)S(1)}, f32[2,16,16]{2,1,0:T(8,128)}, u32[]{:S(2)}) %copy-start.4) | copy-done | bytes 2072
  2.6 0.0 copy-start.6
  2.6 0.7 %copy-done.6 = s32[2,128]{1,0:T(2,128)S(1)} copy-done((s32[2,128]{1,0:T(2,128)S(1)}, s32[2,128]{1,0:T(2,128)}, u32[]{:S(2)}) %copy-start.6) | copy-done | bytes 1048
  3.3 0.0 copy-start.5
  3.3 0.1 pack_forcing.1
  3.4 3.8 %collective-permute-start = (f32[5,16,128]{2,1,0:T(8,128)S(1)}, f32[5,16,128]{2,1,0:T(8,128)S(1)}, u32[]{:S(2)}, u32[]{:S(2)}) collective-permute-start(f32[5,16,128]{2,1,0:T(8,128)S(1)} %pack_forcing.1), channel_id=1, source_target_pairs={{0,4},{8,12},{16,20},{24,28},{4,0},{12,8},{20,16},{28,24},{1,5},{9... | collective-permute-start | bytes 122888 | tf_op jit(solution)/shard_map/ppermute | solution.py:505
  7.2 0.9 %collective-permute-done = f32[5,16,128]{2,1,0:T(8,128)S(1)} collective-permute-done((f32[5,16,128]{2,1,0:T(8,128)S(1)}, f32[5,16,128]{2,1,0:T(8,128)S(1)}, u32[]{:S(2)}, u32[]{:S(2)}) %collective-permute-start) | collective-permute-done | bytes 40992 | tf_op jit(solution)/shard_map/ppermute | solution.py:505
  8.0 1.5 %collective-permute-start.1 = (f32[5,16,128]{2,1,0:T(8,128)S(1)}, f32[5,16,128]{2,1,0:T(8,128)S(1)}, u32[]{:S(2)}, u32[]{:S(2)}) collective-permute-start(f32[5,16,128]{2,1,0:T(8,128)S(1)} %add.12), channel_id=1, source_target_pairs={{0,16},{4,20},{8,24},{12,28},{16,0},{20,4},{24,8},{28,12},{1,17},{... | collective-permute-start | bytes 122888 | tf_op jit(solution)/shard_map/ppermute | solution.py:509
  9.6 0.0 copy-start
  9.6 1.3 %copy-done = f32[1296,2,128]{2,1,0:T(2,128)S(1)} copy-done((f32[1296,2,128]{2,1,0:T(2,128)S(1)}, f32[1296,2,128]{2,1,0:T(2,128)}, u32[]{:S(2)}) %copy-start) | copy-done | bytes 1327128
  10.9 0.0 copy-start.1
  10.9 0.1 split.1
  11.0 1.1 %collective-permute-done.1 = f32[5,16,128]{2,1,0:T(8,128)S(1)} collective-permute-done((f32[5,16,128]{2,1,0:T(8,128)S(1)}, f32[5,16,128]{2,1,0:T(8,128)S(1)}, u32[]{:S(2)}, u32[]{:S(2)}) %collective-permute-start.1) | collective-permute-done | bytes 40992 | tf_op jit(solution)/shard_map/ppermute | solution.py:509
  12.1 1.3 %collective-permute-start.9 = (f32[1152,128]{1,0:T(8,128)S(1)}, f32[1152,128]{1,0:T(8,128)S(1)}, u32[]{:S(2)}, u32[]{:S(2)}) collective-permute-start(f32[1152,128]{1,0:T(8,128)S(1)} %get-tuple-element.34), channel_id=1, source_target_pairs={{12,28},{16,0},{13,29},{17,1},{14,30},{18,2},{15,31},{19,3}} | collective-permute-start | bytes 1769480 | tf_op jit(solution)/shard_map/ppermute | solution.py:512
  13.3 3.6 %collective-permute-start.2 = (f32[5,16,128]{2,1,0:T(8,128)S(1)}, f32[5,16,128]{2,1,0:T(8,128)S(1)}, u32[]{:S(2)}, u32[]{:S(2)}) collective-permute-start(f32[5,16,128]{2,1,0:T(8,128)S(1)} %add.13), channel_id=1, source_target_pairs={{0,12},{12,0},{16,28},{28,16},{1,13},{13,1},{17,29},{29,17},{2,14}... | collective-permute-start | bytes 122888 | tf_op jit(solution)/shard_map/ppermute | solution.py:514
  16.9 2.2 %collective-permute-done.2 = f32[5,16,128]{2,1,0:T(8,128)S(1)} collective-permute-done((f32[5,16,128]{2,1,0:T(8,128)S(1)}, f32[5,16,128]{2,1,0:T(8,128)S(1)}, u32[]{:S(2)}, u32[]{:S(2)}) %collective-permute-start.2) | collective-permute-done | bytes 40992 | tf_op jit(solution)/shard_map/ppermute | solution.py:514
  19.2 1.3 %collective-permute-start.3 = (f32[5,16,128]{2,1,0:T(8,128)S(1)}, f32[5,16,128]{2,1,0:T(8,128)S(1)}, u32[]{:S(2)}, u32[]{:S(2)}) collective-permute-start(f32[5,16,128]{2,1,0:T(8,128)S(1)} %collective-permute-done.2), channel_id=1, source_target_pairs={{0,4},{12,8},{16,20},{28,24},{1,5},{13,9},{17,21},{29,25},{2,6},{1... | collective-permute-start | bytes 122888 | tf_op jit(solution)/shard_map/ppermute | solution.py:517
  20.4 0.9 %collective-permute-done.3 = f32[5,16,128]{2,1,0:T(8,128)S(1)} collective-permute-done((f32[5,16,128]{2,1,0:T(8,128)S(1)}, f32[5,16,128]{2,1,0:T(8,128)S(1)}, u32[]{:S(2)}, u32[]{:S(2)}) %collective-permute-start.3) | collective-permute-done | bytes 40992 | tf_op jit(solution)/shard_map/ppermute | solution.py:517
  21.3 0.7 %collective-permute-start.8 = (f32[1440,128]{1,0:T(8,128)S(1)}, f32[1440,128]{1,0:T(8,128)S(1)}, u32[]{:S(2)}, u32[]{:S(2)}) collective-permute-start(f32[1440,128]{1,0:T(8,128)S(1)} %get-tuple-element.32), channel_id=1, source_target_pairs={{12,16},{16,12},{13,17},{17,13},{14,18},{18,14},{15,19},{19,15}} | collective-permute-start | bytes 2211848 | tf_op jit(solution)/shard_map/ppermute | solution.py:520
  22.0 1.8 %collective-permute-done.9 = f32[1152,128]{1,0:T(8,128)S(1)} collective-permute-done((f32[1152,128]{1,0:T(8,128)S(1)}, f32[1152,128]{1,0:T(8,128)S(1)}, u32[]{:S(2)}, u32[]{:S(2)}) %collective-permute-start.9) | collective-permute-done | bytes 589856 | tf_op jit(solution)/shard_map/ppermute | solution.py:512
  23.8 5.2 %collective-permute-start.10 = (f32[1152,128]{1,0:T(8,128)S(1)}, f32[1152,128]{1,0:T(8,128)S(1)}, u32[]{:S(2)}, u32[]{:S(2)}) collective-permute-start(f32[1152,128]{1,0:T(8,128)S(1)} %collective-permute-done.9), channel_id=1, source_target_pairs={{28,16},{0,12},{29,17},{1,13},{30,18},{2,14},{31,19},{3,15}} | collective-permute-start | bytes 1769480 | tf_op jit(solution)/shard_map/ppermute | solution.py:523
  29.0 0.0 copy-done.5
  29.1 0.0 copy-done.1
  29.1 1.0 %edges.1 = (f32[32,128]{1,0:T(8,128)S(1)}, f32[2,2688]{1,0:T(2,128)S(1)}, f32[2,2688]{1,0:T(2,128)S(1)}) custom-call(f32[8,8]{1,0:T(8,128)S(1)} %copy-done.5, f32[5,16,128]{2,1,0:T(8,128)S(1)} %add_add_fusion.forcing, f32[2592,128]{1,0:T(8,128)S(1)} %bitcast.5), custom_call_target="tpu_custom_call" | custom-call | bytes 3000000 | tf_op jit(solution)/shard_map/edges/pallas_call | solution.py:456
  30.1 3.7 %collective-permute-start.6 = (f32[2,2688]{1,0:T(2,128)S(1)}, f32[2,2688]{1,0:T(2,128)S(1)}, u32[]{:S(2)}, u32[]{:S(2)}) collective-permute-start(f32[2,2688]{1,0:T(2,128)S(1)} %get-tuple-element.27.west), channel_id=1, source_target_pairs={{1,0},{2,1},{3,2},{0,3},{5,4},{6,5},{7,6},{4,7},{9,8},{10,9},{11,1... | collective-permute-start | bytes 64520 | tf_op jit(solution)/shard_map/ppermute | solution.py:536
  33.8 0.0 collective-permute-done.4.beyond
  33.8 0.0 collective-permute-start.5
  33.8 0.0 copy-start.2
  33.8 3.2 %base.1 = (f32[1152,128]{1,0:T(8,128)S(1)}, f32[1440,128]{1,0:T(8,128)S(1)}) custom-call(f32[32,128]{1,0:T(8,128)S(1)} %get-tuple-element.25.par, f32[2592,128]{1,0:T(8,128)S(1)} %bitcast.6, f32[2592,128]{1,0:T(8,128)S(1)} %collective-permute-done.4.beyond), custom_call_target="tpu_custom_call" | custom-call | bytes 12000000 | tf_op jit(solution)/shard_map/base/pallas_call | solution.py:456
  37.0 0.0 collective-permute-done.6.from_east
  37.0 2.4 %collective-permute-done.5.from_west = f32[2,2688]{1,0:T(2,128)S(1)} collective-permute-done((f32[2,2688]{1,0:T(2,128)S(1)}, f32[2,2688]{1,0:T(2,128)S(1)}, u32[]{:S(2)}, u32[]{:S(2)}) %collective-permute-start.5) | collective-permute-done | bytes 21536 | tf_op jit(solution)/shard_map/ppermute | solution.py:535
  39.4 0.0 copy-done.2
  39.4 0.5 %fix.1 = f32[2688,128]{1,0:T(8,128)S(1)} custom-call(f32[2,2688]{1,0:T(2,128)S(1)} %copy-done.2, f32[32,128]{1,0:T(8,128)S(1)} %get-tuple-element.25.par, f32[2,2688]{1,0:T(2,128)S(1)} %get-tuple-element.27.west, f32[2,2688]{1,0:T(2,128)S(1)} %get-tuple-element.28.east, f32[2,2688]{1,0:T(2,128)S(1)} %collective-permute-done.5.from_west, ...), custom_call_target="tpu_custom_call" | custom-call | bytes 3000000 | tf_op jit(solution)/shard_map/fix/pallas_call | solution.py:456
  39.9 0.0 collective-permute-done.10.split
  39.9 0.0 collective-permute-done.7.straight
  39.9 0.8 %first_groups.1 = (f32[1152,128]{1,0:T(8,128)S(1)}, f32[16,128]{1,0:T(8,128)S(1)}) custom-call(f32[32,128]{1,0:T(8,128)S(1)} %get-tuple-element.25.par, f32[1152,128]{1,0:T(8,128)S(1)} %get-tuple-element.33.base, f32[2688,128]{1,0:T(8,128)S(1)} %fix.1, f32[2592,128]{1,0:T(8,128)S(1)} %collective-permute-done.7.straight, ...), custom_call_target="tpu_custom_call" | custom-call | bytes 3000000 | tf_op jit(solution)/shard_map/first_groups/pallas_call | solution.py:456
  40.7 0.0 collective-permute-done.8.split
  40.7 2.4 %last_groups.1 = f32[2592,128]{1,0:T(8,128)} custom-call(f32[32,128]{1,0:T(8,128)S(1)} %get-tuple-element.25.par, f32[1440,128]{1,0:T(8,128)S(1)} %get-tuple-element.26.base, f32[2688,128]{1,0:T(8,128)S(1)} %fix.1, f32[2592,128]{1,0:T(8,128)S(1)} %collective-permute-done.7.straight, f32[1440,128]{1,0:T(8,128)S(1)} %collective-permute-done.8.split, ...), custom_call_target="tpu_custom_call" | custom-call | bytes 6000000 | tf_op jit(solution)/shard_map/last_groups/pallas_call | solution.py:456
  (3 shorter events, 0.0 us)
Async XLA Ops:
  0.0 33.8 %collective-permute-start.4 = (f32[2592,128]{1,0:T(8,128)}, f32[2592,128]{1,0:T(8,128)S(1)}, u32[]{:S(2)}, u32[]{:S(2)}) collective-permute-start(f32[2592,128]{1,0:T(8,128)} %bitcast.2), channel_id=1, source_target_pairs={{0,4},{8,12},{16,20},{24,28},{4,0},{12,8},{20,16},{28,24},{1,5},{9... | collective-permute-start | bytes 3981320 | tf_op jit(solution)/shard_map/ppermute | solution.py:485
  0.5 39.5 %collective-permute-start.7 = (f32[2592,128]{1,0:T(8,128)}, f32[2592,128]{1,0:T(8,128)S(1)}, u32[]{:S(2)}, u32[]{:S(2)}) collective-permute-start(f32[2592,128]{1,0:T(8,128)} %bitcast.3), channel_id=1, source_target_pairs={{4,8},{20,24},{8,4},{24,20},{5,9},{21,25},{9,5},{25,21},{6,10},{22... | collective-permute-start | bytes 3981320 | tf_op jit(solution)/shard_map/ppermute | solution.py:481
  1.2 0.7 %copy-start.3 = (f32[2,16,16]{2,1,0:T(8,128)S(1)}, f32[2,16,16]{2,1,0:T(8,128)}, u32[]{:S(2)}) copy-start(f32[2,16,16]{2,1,0:T(8,128)} %wind.1) | copy-start | bytes 6148
  1.9 0.7 %copy-start.4 = (f32[2,16,16]{2,1,0:T(8,128)S(1)}, f32[2,16,16]{2,1,0:T(8,128)}, u32[]{:S(2)}) copy-start(f32[2,16,16]{2,1,0:T(8,128)} %current.1) | copy-start | bytes 6148
  2.6 0.7 %copy-start.6 = (s32[2,128]{1,0:T(2,128)S(1)}, s32[2,128]{1,0:T(2,128)}, u32[]{:S(2)}) copy-start(s32[2,128]{1,0:T(2,128)} %sea.1) | copy-start | bytes 3076
  3.3 25.7 %copy-start.5 = (f32[8,8]{1,0:T(8,128)S(1)}, f32[8,8]{1,0:T(8,128)}, u32[]{:S(2)}) copy-start(f32[8,8]{1,0:T(8,128)} %constant.4.clone.geometry) | copy-start | bytes 772
  3.4 4.6 %collective-permute-start = (f32[5,16,128]{2,1,0:T(8,128)S(1)}, f32[5,16,128]{2,1,0:T(8,128)S(1)}, u32[]{:S(2)}, u32[]{:S(2)}) collective-permute-start(f32[5,16,128]{2,1,0:T(8,128)S(1)} %pack_forcing.1), channel_id=1, source_target_pairs={{0,4},{8,12},{16,20},{24,28},{4,0},{12,8},{20,16},{28,24},{1,5},{9... | collective-permute-start | bytes 122888 | tf_op jit(solution)/shard_map/ppermute | solution.py:505
  8.0 4.0 %collective-permute-start.1 = (f32[5,16,128]{2,1,0:T(8,128)S(1)}, f32[5,16,128]{2,1,0:T(8,128)S(1)}, u32[]{:S(2)}, u32[]{:S(2)}) collective-permute-start(f32[5,16,128]{2,1,0:T(8,128)S(1)} %add.12), channel_id=1, source_target_pairs={{0,16},{4,20},{8,24},{12,28},{16,0},{20,4},{24,8},{28,12},{1,17},{... | collective-permute-start | bytes 122888 | tf_op jit(solution)/shard_map/ppermute | solution.py:509
  9.6 1.3 %copy-start = (f32[1296,2,128]{2,1,0:T(2,128)S(1)}, f32[1296,2,128]{2,1,0:T(2,128)}, u32[]{:S(2)}) copy-start(f32[1296,2,128]{2,1,0:T(2,128)} %param.6) | copy-start | bytes 3981316
  10.9 18.2 %copy-start.1 = (f32[1296,2,128]{2,1,0:T(2,128)S(1)}, f32[1296,2,128]{2,1,0:T(2,128)}, u32[]{:S(2)}) copy-start(f32[1296,2,128]{2,1,0:T(2,128)} %param.6) | copy-start | bytes 3981316
  12.1 11.8 %collective-permute-start.9 = (f32[1152,128]{1,0:T(8,128)S(1)}, f32[1152,128]{1,0:T(8,128)S(1)}, u32[]{:S(2)}, u32[]{:S(2)}) collective-permute-start(f32[1152,128]{1,0:T(8,128)S(1)} %get-tuple-element.34), channel_id=1, source_target_pairs={{12,28},{16,0},{13,29},{17,1},{14,30},{18,2},{15,31},{19,3}} | collective-permute-start | bytes 1769480 | tf_op jit(solution)/shard_map/ppermute | solution.py:512
  13.3 5.8 %collective-permute-start.2 = (f32[5,16,128]{2,1,0:T(8,128)S(1)}, f32[5,16,128]{2,1,0:T(8,128)S(1)}, u32[]{:S(2)}, u32[]{:S(2)}) collective-permute-start(f32[5,16,128]{2,1,0:T(8,128)S(1)} %add.13), channel_id=1, source_target_pairs={{0,12},{12,0},{16,28},{28,16},{1,13},{13,1},{17,29},{29,17},{2,14}... | collective-permute-start | bytes 122888 | tf_op jit(solution)/shard_map/ppermute | solution.py:514
  19.2 2.1 %collective-permute-start.3 = (f32[5,16,128]{2,1,0:T(8,128)S(1)}, f32[5,16,128]{2,1,0:T(8,128)S(1)}, u32[]{:S(2)}, u32[]{:S(2)}) collective-permute-start(f32[5,16,128]{2,1,0:T(8,128)S(1)} %collective-permute-done.2), channel_id=1, source_target_pairs={{0,4},{12,8},{16,20},{28,24},{1,5},{13,9},{17,21},{29,25},{2,6},{1... | collective-permute-start | bytes 122888 | tf_op jit(solution)/shard_map/ppermute | solution.py:517
  21.3 19.4 %collective-permute-start.8 = (f32[1440,128]{1,0:T(8,128)S(1)}, f32[1440,128]{1,0:T(8,128)S(1)}, u32[]{:S(2)}, u32[]{:S(2)}) collective-permute-start(f32[1440,128]{1,0:T(8,128)S(1)} %get-tuple-element.32), channel_id=1, source_target_pairs={{12,16},{16,12},{13,17},{17,13},{14,18},{18,14},{15,19},{19,15}} | collective-permute-start | bytes 2211848 | tf_op jit(solution)/shard_map/ppermute | solution.py:520
  23.8 16.1 %collective-permute-start.10 = (f32[1152,128]{1,0:T(8,128)S(1)}, f32[1152,128]{1,0:T(8,128)S(1)}, u32[]{:S(2)}, u32[]{:S(2)}) collective-permute-start(f32[1152,128]{1,0:T(8,128)S(1)} %collective-permute-done.9), channel_id=1, source_target_pairs={{28,16},{0,12},{29,17},{1,13},{30,18},{2,14},{31,19},{3,15}} | collective-permute-start | bytes 1769480 | tf_op jit(solution)/shard_map/ppermute | solution.py:523
  30.1 6.9 %collective-permute-start.6 = (f32[2,2688]{1,0:T(2,128)S(1)}, f32[2,2688]{1,0:T(2,128)S(1)}, u32[]{:S(2)}, u32[]{:S(2)}) collective-permute-start(f32[2,2688]{1,0:T(2,128)S(1)} %get-tuple-element.27.west), channel_id=1, source_target_pairs={{1,0},{2,1},{3,2},{0,3},{5,4},{6,5},{7,6},{4,7},{9,8},{10,9},{11,1... | collective-permute-start | bytes 64520 | tf_op jit(solution)/shard_map/ppermute | solution.py:536
  33.8 5.6 %collective-permute-start.5 = (f32[2,2688]{1,0:T(2,128)S(1)}, f32[2,2688]{1,0:T(2,128)S(1)}, u32[]{:S(2)}, u32[]{:S(2)}) collective-permute-start(f32[2,2688]{1,0:T(2,128)S(1)} %get-tuple-element.28.east), channel_id=1, source_target_pairs={{0,1},{1,2},{2,3},{3,0},{4,5},{5,6},{6,7},{7,4},{8,9},{9,10},{10,1... | collective-permute-start | bytes 64520 | tf_op jit(solution)/shard_map/ppermute | solution.py:535
  33.8 5.6 %copy-start.2 = (f32[2,2688]{1,0:T(2,128)S(1)}, f32[2,2688]{1,0:T(2,128)}, u32[]{:S(2)}) copy-start(f32[2,2688]{1,0:T(2,128)} %constant.5.clone.table) | copy-start | bytes 64516

commit v3 on v2

--- a/solution.py
+++ b/solution.py
@@ -99,26 +99,68 @@
     return jnp.broadcast_to(par[index : index + 1, :], (8, LANES))
 
 
-def pack_kernel(wind, current, sea, out):
+def pack_kernel(wind, current, sea, out, wind_here, current_here, sea_here, sems):
     me = lax.axis_index("band")
     rows, strip = wind.shape[1], wind.shape[2]
+    copies = [
+        pltpu.make_async_copy(wind, wind_here, sems.at[0]),
+        pltpu.make_async_copy(current, current_here, sems.at[1]),
+        pltpu.make_async_copy(sea, sea_here, sems.at[2]),
+    ]
+    for copy in copies:
+        copy.start()
+    out[4] = jnp.zeros((rows, LANES), jnp.float32)
     empty = jnp.zeros((rows, LANES - strip), jnp.float32)
-    for part, ref in enumerate((current, wind)):
+    for copy in copies:
+        copy.wait()
+    for part, ref in enumerate((current_here, wind_here)):
         for axis in range(2):
             wide = jnp.concatenate([ref[axis], empty], axis=1)
             out[2 * part + axis] = pltpu.roll(wide, me * strip, 1)
-    out[4] = jnp.zeros((rows, LANES), jnp.float32)
-    seas = sea[...].astype(jnp.float32)
+    seas = sea_here[...].astype(jnp.float32)
     out[4, pl.ds(2 * me, 1), :] = seas[0:1]
     out[4, pl.ds(2 * me + 1, 1), :] = seas[1:2]
 
 
-def split_kernel(spectra, relayed, direct):
-    relayed[...] = spectra[0 : relayed.shape[0], :]
-    direct[...] = spectra[relayed.shape[0] :, :]
-
-
-def edge_kernel(bands, geometry, forcing, spectra, par, west, east, line):
+def split_kernel(source, mask, relayed, direct, west, east, spectra, sea, line, sems):
+    first = relayed.shape[0]
+    whole = pltpu.make_async_copy(source, spectra, sems.at[0])
+    parts = [
+        pltpu.make_async_copy(source.at[0:first], relayed, sems.at[1]),
+        pltpu.make_async_copy(source.at[first:ROWS], direct, sems.at[2]),
+    ]
+    masking = pltpu.make_async_copy(mask, sea, sems.at[3])
+    masking.start()
+    whole.start()
+    for part in parts:
+        part.start()
+    masking.wait()
+    whole.wait()
+    seas = sea[...].astype(jnp.float32)
+    sub = lax.broadcasted_iota(jnp.int32, (LANES, LANES), 0)
+    both = jnp.where(
+        lax.rem(sub, 2) == 0,
+        jnp.broadcast_to(seas[0:1], (LANES, LANES)),
+        jnp.broadcast_to(seas[1:2], (LANES, LANES)),
+    )
+    full = ROWS // LANES
+    for block in range(WIDE // LANES):
+        at = block * LANES
+        if block < full:
+            cells = spectra[at : at + LANES, :] * both
+        else:
+            left = ROWS - at
+            line[...] = jnp.zeros((LANES, LANES), jnp.float32)
+            line[0:left, :] = spectra[at : at + left, :] * both[0:left]
+            cells = line[...]
+        turned = cells.T
+        west[:, at : at + LANES] = turned[0:2]
+        east[:, at : at + LANES] = turned[LANES - 2 : LANES]
+    for part in parts:
+        part.wait()
+
+
+def table_kernel(bands, geometry, forcing, west_in, east_in, par, west, east):
     me = lax.axis_index("band")
     is_even = lax.rem(me, 2) == 0
     row = 2 * me
@@ -179,27 +221,15 @@
     put(ICOS_1, icos[1])
     par[26:32, :] = jnp.zeros((6, LANES), jnp.float32)
 
-    sub = lax.broadcasted_iota(jnp.int32, (LANES, LANES), 0)
-    both = jnp.where(
-        lax.rem(sub, 2) == 0,
-        jnp.broadcast_to(seas[2], (LANES, LANES)),
-        jnp.broadcast_to(seas[3], (LANES, LANES)),
-    )
-    full = ROWS // LANES
-    for block in range(WIDE // LANES):
-        at = block * LANES
-        if block < full:
-            cells = spectra[at : at + LANES, :] * both
-        else:
-            left = ROWS - at
-            line[...] = jnp.zeros((LANES, LANES), jnp.float32)
-            line[0:left, :] = spectra[at : at + left, :] * both[0:left]
-            line[left : left + 1, :] = east_speed[0]
-            line[left + 1 : left + 2, :] = east_speed[1]
-            cells = line[...]
-        turned = cells.T
-        west[:, at : at + LANES] = turned[0:2]
-        east[:, at : at + LANES] = turned[LANES - 2 : LANES]
+    west[...] = west_in[...]
+    east[...] = east_in[...]
+    for i in range(2):
+        west[:, ROWS + i : ROWS + i + 1] = jnp.concatenate(
+            [east_speed[i][:, j : j + 1] for j in range(2)], axis=0
+        )
+        east[:, ROWS + i : ROWS + i + 1] = jnp.concatenate(
+            [east_speed[i][:, j : j + 1] for j in (LANES - 2, LANES - 1)], axis=0
+        )
 
 
 def fix_kernel(table, par, west, east, from_west, from_east, fix, tall):
@@ -447,7 +477,7 @@
 
 VMEM = pl.BlockSpec(memory_space=pltpu.VMEM)
 SMEM = pl.BlockSpec(memory_space=pltpu.SMEM)
-ANY = pl.BlockSpec(memory_space=pl.ANY)
+HBM = pl.BlockSpec(memory_space=pltpu.HBM)
 PARAMS = pltpu.CompilerParams(vmem_limit_bytes=40 * 1024 * 1024)
 
 
@@ -478,59 +508,65 @@
     first_rows = FIRST_GROUPS * GROUP_ROWS
     last_rows = ROWS - first_rows
 
+    (own,) = call(
+        pack_kernel,
+        "pack_forcing",
+        tuple(pltpu.with_memory_space_constraint(v, pltpu.HBM) for v in (wind, current, sea_mask)),
+        [HBM] * 3,
+        [(5, wind.shape[1], LANES)],
+        [
+            pltpu.VMEM(wind.shape, jnp.float32),
+            pltpu.VMEM(current.shape, jnp.float32),
+            pltpu.VMEM(sea_mask.shape, jnp.int32),
+            pltpu.SemaphoreType.DMA((3,)),
+        ],
+        0.3,
+    )
+    forcing = own + lax.ppermute(own, "band", [(b, b ^ 2) for b in range(bands)])
+
+    rows_after, forcing = lax.optimization_barrier((cells, forcing))
     straight = lax.ppermute(
-        cells, "band", swapped([(b, b + 1) for b in range(1, bands - 1, 2) if b != middle])
+        rows_after, "band", swapped([(b, b + 1) for b in range(1, bands - 1, 2) if b != middle])
     )
     pairs = [(b, b + 1) for b in range(0, bands, 2)]
-    beyond = lax.ppermute(cells, "band", swapped(pairs))
-    part_relayed, part_direct = call(
+    beyond = lax.ppermute(rows_after, "band", swapped(pairs))
+    part_relayed, part_direct, west, east = call(
         split_kernel,
         "split",
-        (cells,),
-        [VMEM],
-        [(first_rows, LANES), (last_rows, LANES)],
-        [],
-        0.3,
-    )
-
-    (forcing,) = call(
-        pack_kernel,
-        "pack_forcing",
-        (wind, current, sea_mask),
-        [VMEM] * 3,
-        [(5, wind.shape[1], LANES)],
-        [],
-        0.3,
-    )
-    forcing = forcing + lax.ppermute(forcing, "band", swapped(pairs))
+        tuple(pltpu.with_memory_space_constraint(v, pltpu.HBM) for v in (cells, sea_mask)),
+        [HBM, HBM],
+        [(first_rows, LANES), (last_rows, LANES), (2, WIDE), (2, WIDE)],
+        [
+            pltpu.VMEM((ROWS, LANES), jnp.float32),
+            pltpu.VMEM(sea_mask.shape, jnp.int32),
+            pltpu.VMEM((LANES, LANES), jnp.float32),
+            pltpu.SemaphoreType.DMA((4,)),
+        ],
+        1.0,
+    )
+
     bit = 4
     while bit < bands:
-        turnabout = [(b, b ^ bit) for b in range(bands)]
-        forcing = forcing + lax.ppermute(forcing, "band", turnabout)
+        forcing = forcing + lax.ppermute(forcing, "band", [(b, b ^ bit) for b in range(bands)])
         bit *= 2
     part_relayed, forcing = lax.optimization_barrier((part_relayed, forcing))
     relay = lax.ppermute(part_relayed, "band", [(middle, bands - 1), (middle + 1, 0)])
-    free = [2 * chip + chip % 2 for chip in range(bands // 2)]
-    across = lax.ppermute(
-        forcing, "band", [(b, free[chip ^ 1]) for chip, b in enumerate(free)]
-    )
-    along = lax.ppermute(across, "band", [(b, b ^ 1) for b in free])
-    forcing = forcing + across + along
+    forcing = forcing + lax.ppermute(forcing, "band", swapped(pairs))
     part_direct, forcing = lax.optimization_barrier((part_direct, forcing))
     direct = lax.ppermute(
         part_direct, "band", [(middle, middle + 1), (middle + 1, middle)]
     )
+
+    par, west, east = call(
+        functools.partial(table_kernel, bands),
+        "tables",
+        (jnp.asarray(geometry_table(bands)), forcing, west, east),
+        [SMEM, VMEM, VMEM, VMEM],
+        [(PAR_ROWS, LANES), (2, WIDE), (2, WIDE)],
+        [],
+        0.3,
+    )
     relayed = lax.ppermute(relay, "band", [(bands - 1, middle + 1), (0, middle)])
-
-    par, west, east = call(
-        functools.partial(edge_kernel, bands),
-        "edges",
-        (jnp.asarray(geometry_table(bands)), forcing, cells),
-        [SMEM, VMEM, VMEM],
-        [(PAR_ROWS, LANES), (2, WIDE), (2, WIDE)],
-        [pltpu.VMEM((LANES, LANES), jnp.float32)],
-        1.0,
-    )
     ring = [(s, (s + 1) % spec_count) for s in range(spec_count)]
     from_west = lax.ppermute(east, "spec", ring)
     from_east = lax.ppermute(west, "spec", [(t, s) for s, t in ring])

time: 43.5 us -> 38.3 us (0.88)
  starting transfers between devices: 22.2 us -> 15.2 us
  local copies, waits for them, and re-layouts: 3.44 us -> 0.01 us
  waiting for transfers between devices: 9.17 us -> 12.3 us
  Pallas kernels: 8.12 us -> 10.5 us
    ppermute x1, waiting for transfers between devices: 1.79 us -> 6.99 us  [per_device(): lax.ppermute(part_relayed, 'band', [(middle, bands - 1), (middle + 1, 0)])]
    ppermute x1, starting transfers between devices: 5.22 us -> 1.32 us  [per_device(): lax.ppermute(relay, 'band', [(bands - 1, middle + 1), (0, middle)])]
    unnamed x14 -> x6, local copies, waits for them, and re-layouts: 3.44 us -> 0.01 us
    pallas_call x7, Pallas kernels: 8.12 us -> 10.5 us  [call(): pl.pallas_call(kernel, name=name, out_shape=outs, in_specs=specs, out_spe...]
    ppermute x5 -> x4, waiting for transfers between devices: 4.15 us -> 2.07 us  [the longest x1 1.98 us: per_device(): lax.ppermute(own, 'band', [(b, b ^ 2) for b in range(bands)])]
    ppermute x1, starting transfers between devices: 3.77 us -> 1.91 us  [per_device(): forcing = forcing + lax.ppermute(forcing, 'band', swapped(pairs))]
    ppermute x5 -> x4, starting transfers between devices: 7.57 us -> 5.87 us  [the longest x1 3 us: per_device(): lax.ppermute(own, 'band', [(b, b ^ 2) for b in range(bands)])]
    ppermute x1, starting transfers between devices: 3.65 us -> 4.1 us  [per_device(): from_east = lax.ppermute(west, 'spec', [(t, s) for s, t in ring])]
  transfers between devices with their start and end apart: 11 -> 10, of which waited for: 6 -> 5; matrix products, arithmetic and copies ran while one was open for 0% -> 0% of each run, Pallas kernels for 13% -> 19%
where the time goes in v3:
time: 38.3 us; the launch traced here: 38.1 us
  starting transfers between devices  15.2 us (40%)
  waiting for transfers between devices  12.3 us (32%)
  Pallas kernels  10.5 us (27%)
    pallas_call x7, Pallas kernels, call(): pl.pallas_call(kernel, name=name, out_shape=outs, in_specs=specs, out_spe...  10.5 us
    ppermute x1, waiting for transfers between devices, per_device(): lax.ppermute(part_relayed, 'band', [(middle, bands - 1), (middle + 1, 0)])  6.99 us
    ppermute x1, starting transfers between devices, per_device(): from_east = lax.ppermute(west, 'spec', [(t, s) for s, t in ring])  4.1 us
    ppermute x1, starting transfers between devices, per_device(): lax.ppermute(own, 'band', [(b, b ^ 2) for b in range(bands)])  3 us
    ppermute x1, waiting for transfers between devices, per_device(): from_west = lax.ppermute(east, 'spec', ring)  2.34 us
    ppermute x1, starting transfers between devices, per_device(): lax.ppermute(forcing, 'band', [(b, b ^ bit) for b in range(bands)])  2.11 us
    ppermute x1, waiting for transfers between devices, per_device(): lax.ppermute(own, 'band', [(b, b ^ 2) for b in range(bands)])  1.98 us
    ppermute x1, starting transfers between devices, per_device(): forcing = forcing + lax.ppermute(forcing, 'band', swapped(pairs))  1.91 us
  transfers between devices with their start and end apart: 10, of which 5 were waited for; matrix products, arithmetic and copies ran while one was open for 0% of the time, Pallas kernels for 19%

profile of v3, /device:TPU:0, one launch (start us, length us, event | category | flops | bytes accessed | tf_op | source)
XLA Modules:
  0.0 38.1 jit_solution(17411727494598898253)
XLA Ops:
  0.0 0.0 copy-start.2
  0.0 0.0 copy-start
  0.0 0.9 %pack_forcing.1 = f32[5,16,128]{2,1,0:T(8,128)S(1)} custom-call(f32[2,16,16]{2,1,0:T(8,128)} %wind.1, f32[2,16,16]{2,1,0:T(8,128)} %current.1, s32[2,128]{1,0:T(2,128)} %sea.1), custom_call_target="tpu_custom_call" | custom-call | bytes 900000 | tf_op jit(solution)/shard_map/pack_forcing/pallas_call | solution.py:486
  1.0 3.0 %collective-permute-start = (f32[5,16,128]{2,1,0:T(8,128)S(1)}, f32[5,16,128]{2,1,0:T(8,128)S(1)}, u32[]{:S(2)}, u32[]{:S(2)}) collective-permute-start(f32[5,16,128]{2,1,0:T(8,128)S(1)} %pack_forcing.1), channel_id=1, source_target_pairs={{0,8},{4,12},{8,0},{12,4},{16,24},{20,28},{24,16},{28,20},{1,9},{5... | collective-permute-start | bytes 122888 | tf_op jit(solution)/shard_map/ppermute | solution.py:525
  4.0 2.0 %collective-permute-done = f32[5,16,128]{2,1,0:T(8,128)S(1)} collective-permute-done((f32[5,16,128]{2,1,0:T(8,128)S(1)}, f32[5,16,128]{2,1,0:T(8,128)S(1)}, u32[]{:S(2)}, u32[]{:S(2)}) %collective-permute-start) | collective-permute-done | bytes 40992 | tf_op jit(solution)/shard_map/ppermute | solution.py:525
  5.9 0.0 collective-permute-start.3
  6.0 0.7 %collective-permute-start.6 = (f32[2592,128]{1,0:T(8,128)}, f32[2592,128]{1,0:T(8,128)S(1)}, u32[]{:S(2)}, u32[]{:S(2)}) collective-permute-start(f32[2592,128]{1,0:T(8,128)} %bitcast.3), channel_id=1, source_target_pairs={{4,8},{20,24},{8,4},{24,20},{5,9},{21,25},{9,5},{25,21},{6,10},{22... | collective-permute-start | bytes 3981320 | tf_op jit(solution)/shard_map/ppermute | solution.py:528
  6.7 2.1 %collective-permute-start.1 = (f32[5,16,128]{2,1,0:T(8,128)S(1)}, f32[5,16,128]{2,1,0:T(8,128)S(1)}, u32[]{:S(2)}, u32[]{:S(2)}) collective-permute-start(f32[5,16,128]{2,1,0:T(8,128)S(1)} %add.9), channel_id=1, source_target_pairs={{0,16},{4,20},{8,24},{12,28},{16,0},{20,4},{24,8},{28,12},{1,17},{... | collective-permute-start | bytes 122888 | tf_op jit(solution)/shard_map/ppermute | solution.py:550
  8.8 1.9 %split.1 = (f32[1152,128]{1,0:T(8,128)S(1)}, f32[1440,128]{1,0:T(8,128)S(1)}, f32[2,2688]{1,0:T(2,128)S(1)}, f32[2,2688]{1,0:T(2,128)S(1)}) custom-call(f32[2592,128]{1,0:T(8,128)} %bitcast.4, s32[2,128]{1,0:T(2,128)} %sea.1), custom_call_target="tpu_custom_call" | custom-call | bytes 3000000 | tf_op jit(solution)/shard_map/split/pallas_call | solution.py:486
  10.7 0.1 collective-permute-done.1
  10.8 1.3 %collective-permute-start.8 = (f32[1152,128]{1,0:T(8,128)S(1)}, f32[1152,128]{1,0:T(8,128)S(1)}, u32[]{:S(2)}, u32[]{:S(2)}) collective-permute-start(f32[1152,128]{1,0:T(8,128)S(1)} %get-tuple-element.42), channel_id=1, source_target_pairs={{12,28},{16,0},{13,29},{17,1},{14,30},{18,2},{15,31},{19,3}} | collective-permute-start | bytes 1769480 | tf_op jit(solution)/shard_map/ppermute | solution.py:553
  12.1 1.9 %collective-permute-start.2 = (f32[5,16,128]{2,1,0:T(8,128)S(1)}, f32[5,16,128]{2,1,0:T(8,128)S(1)}, u32[]{:S(2)}, u32[]{:S(2)}) collective-permute-start(f32[5,16,128]{2,1,0:T(8,128)S(1)} %add.10), channel_id=1, source_target_pairs={{0,4},{8,12},{16,20},{24,28},{4,0},{12,8},{20,16},{28,24},{1,5},{9... | collective-permute-start | bytes 122888 | tf_op jit(solution)/shard_map/ppermute | solution.py:554
  14.0 0.9 %collective-permute-done.2 = f32[5,16,128]{2,1,0:T(8,128)S(1)} collective-permute-done((f32[5,16,128]{2,1,0:T(8,128)S(1)}, f32[5,16,128]{2,1,0:T(8,128)S(1)}, u32[]{:S(2)}, u32[]{:S(2)}) %collective-permute-start.2) | collective-permute-done | bytes 40992 | tf_op jit(solution)/shard_map/ppermute | solution.py:554
  14.9 0.7 %collective-permute-start.7 = (f32[1440,128]{1,0:T(8,128)S(1)}, f32[1440,128]{1,0:T(8,128)S(1)}, u32[]{:S(2)}, u32[]{:S(2)}) collective-permute-start(f32[1440,128]{1,0:T(8,128)S(1)} %get-tuple-element.40), channel_id=1, source_target_pairs={{12,16},{16,12},{13,17},{17,13},{14,18},{18,14},{15,19},{19,15}} | collective-permute-start | bytes 2211848 | tf_op jit(solution)/shard_map/ppermute | solution.py:556
  15.6 7.0 %collective-permute-done.8 = f32[1152,128]{1,0:T(8,128)S(1)} collective-permute-done((f32[1152,128]{1,0:T(8,128)S(1)}, f32[1152,128]{1,0:T(8,128)S(1)}, u32[]{:S(2)}, u32[]{:S(2)}) %collective-permute-start.8) | collective-permute-done | bytes 589856 | tf_op jit(solution)/shard_map/ppermute | solution.py:553
  22.6 1.3 %collective-permute-start.9 = (f32[1152,128]{1,0:T(8,128)S(1)}, f32[1152,128]{1,0:T(8,128)S(1)}, u32[]{:S(2)}, u32[]{:S(2)}) collective-permute-start(f32[1152,128]{1,0:T(8,128)S(1)} %collective-permute-done.8), channel_id=1, source_target_pairs={{28,16},{0,12},{29,17},{1,13},{30,18},{2,14},{31,19},{3,15}} | collective-permute-start | bytes 1769480 | tf_op jit(solution)/shard_map/ppermute | solution.py:569
  23.9 0.0 copy-done.2
  23.9 0.8 %tables.1 = (f32[32,128]{1,0:T(8,128)S(1)}, f32[2,2688]{1,0:T(2,128)S(1)}, f32[2,2688]{1,0:T(2,128)S(1)}) custom-call(f32[8,8]{1,0:T(8,128)S(1)} %copy-done.2, f32[5,16,128]{2,1,0:T(8,128)S(1)} %add.11.forcing, f32[2,2688]{1,0:T(2,128)S(1)} %get-tuple-element.30.west_in, f32[2,2688]{1,0:T(2,128)S(1)} %get-tuple-element.31.east_in), custom_call_target="tpu_custom_call" | custom-call | bytes 900000 | tf_op jit(solution)/shard_map/tables/pallas_call | solution.py:486
  24.7 4.1 %collective-permute-start.5 = (f32[2,2688]{1,0:T(2,128)S(1)}, f32[2,2688]{1,0:T(2,128)S(1)}, u32[]{:S(2)}, u32[]{:S(2)}) collective-permute-start(f32[2,2688]{1,0:T(2,128)S(1)} %get-tuple-element.35.west), channel_id=1, source_target_pairs={{1,0},{2,1},{3,2},{0,3},{5,4},{6,5},{7,6},{4,7},{9,8},{10,9},{11,1... | collective-permute-start | bytes 64520 | tf_op jit(solution)/shard_map/ppermute | solution.py:572
  28.8 0.0 collective-permute-done.3.beyond
  28.8 0.0 collective-permute-start.4
  28.8 0.0 copy-done
  28.8 0.0 copy-start.1
  28.8 3.2 %base.1 = (f32[1152,128]{1,0:T(8,128)S(1)}, f32[1440,128]{1,0:T(8,128)S(1)}) custom-call(f32[32,128]{1,0:T(8,128)S(1)} %get-tuple-element.32.par, f32[2592,128]{1,0:T(8,128)S(1)} %bitcast.5, f32[2592,128]{1,0:T(8,128)S(1)} %collective-permute-done.3.beyond), custom_call_target="tpu_custom_call" | custom-call | bytes 12000000 | tf_op jit(solution)/shard_map/base/pallas_call | solution.py:486
  32.0 0.0 collective-permute-done.5.from_east
  32.0 2.3 %collective-permute-done.4.from_west = f32[2,2688]{1,0:T(2,128)S(1)} collective-permute-done((f32[2,2688]{1,0:T(2,128)S(1)}, f32[2,2688]{1,0:T(2,128)S(1)}, u32[]{:S(2)}, u32[]{:S(2)}) %collective-permute-start.4) | collective-permute-done | bytes 21536 | tf_op jit(solution)/shard_map/ppermute | solution.py:571
  34.4 0.0 copy-done.1
  34.4 0.5 %fix.1 = f32[2688,128]{1,0:T(8,128)S(1)} custom-call(f32[2,2688]{1,0:T(2,128)S(1)} %copy-done.1, f32[32,128]{1,0:T(8,128)S(1)} %get-tuple-element.32.par, f32[2,2688]{1,0:T(2,128)S(1)} %get-tuple-element.35.west, f32[2,2688]{1,0:T(2,128)S(1)} %get-tuple-element.36.east, f32[2,2688]{1,0:T(2,128)S(1)} %collective-permute-done.4.from_west, ...), custom_call_target="tpu_custom_call" | custom-call | bytes 3000000 | tf_op jit(solution)/shard_map/fix/pallas_call | solution.py:486
  34.9 0.0 collective-permute-done.9.split
  34.9 0.0 collective-permute-done.6.straight
  34.9 0.8 %first_groups.1 = (f32[1152,128]{1,0:T(8,128)S(1)}, f32[16,128]{1,0:T(8,128)S(1)}) custom-call(f32[32,128]{1,0:T(8,128)S(1)} %get-tuple-element.32.par, f32[1152,128]{1,0:T(8,128)S(1)} %get-tuple-element.41.base, f32[2688,128]{1,0:T(8,128)S(1)} %fix.1, f32[2592,128]{1,0:T(8,128)S(1)} %collective-permute-done.6.straight, ...), custom_call_target="tpu_custom_call" | custom-call | bytes 3000000 | tf_op jit(solution)/shard_map/first_groups/pallas_call | solution.py:486
  35.7 0.0 collective-permute-done.7.split
  35.7 2.4 %last_groups.1 = f32[2592,128]{1,0:T(8,128)} custom-call(f32[32,128]{1,0:T(8,128)S(1)} %get-tuple-element.32.par, f32[1440,128]{1,0:T(8,128)S(1)} %get-tuple-element.34.base, f32[2688,128]{1,0:T(8,128)S(1)} %fix.1, f32[2592,128]{1,0:T(8,128)S(1)} %collective-permute-done.6.straight, f32[1440,128]{1,0:T(8,128)S(1)} %collective-permute-done.7.split, ...), custom_call_target="tpu_custom_call" | custom-call | bytes 6000000 | tf_op jit(solution)/shard_map/last_groups/pallas_call | solution.py:486
  (3 shorter events, 0.0 us)
Async XLA Ops:
  0.0 23.9 %copy-start.2 = (f32[8,8]{1,0:T(8,128)S(1)}, f32[8,8]{1,0:T(8,128)}, u32[]{:S(2)}) copy-start(f32[8,8]{1,0:T(8,128)} %constant.4.clone.geometry) | copy-start | bytes 772
  0.0 28.8 %copy-start = (f32[1296,2,128]{2,1,0:T(2,128)S(1)}, f32[1296,2,128]{2,1,0:T(2,128)}, u32[]{:S(2)}) copy-start(f32[1296,2,128]{2,1,0:T(2,128)} %param.6) | copy-start | bytes 3981316
  1.0 5.0 %collective-permute-start = (f32[5,16,128]{2,1,0:T(8,128)S(1)}, f32[5,16,128]{2,1,0:T(8,128)S(1)}, u32[]{:S(2)}, u32[]{:S(2)}) collective-permute-start(f32[5,16,128]{2,1,0:T(8,128)S(1)} %pack_forcing.1), channel_id=1, source_target_pairs={{0,8},{4,12},{8,0},{12,4},{16,24},{20,28},{24,16},{28,20},{1,9},{5... | collective-permute-start | bytes 122888 | tf_op jit(solution)/shard_map/ppermute | solution.py:525
  5.9 22.8 %collective-permute-start.3 = (f32[2592,128]{1,0:T(8,128)}, f32[2592,128]{1,0:T(8,128)S(1)}, u32[]{:S(2)}, u32[]{:S(2)}) collective-permute-start(f32[2592,128]{1,0:T(8,128)} %bitcast.2), channel_id=1, source_target_pairs={{0,4},{8,12},{16,20},{24,28},{4,0},{12,8},{20,16},{28,24},{1,5},{9... | collective-permute-start | bytes 3981320 | tf_op jit(solution)/shard_map/ppermute | solution.py:532
  6.0 29.0 %collective-permute-start.6 = (f32[2592,128]{1,0:T(8,128)}, f32[2592,128]{1,0:T(8,128)S(1)}, u32[]{:S(2)}, u32[]{:S(2)}) collective-permute-start(f32[2592,128]{1,0:T(8,128)} %bitcast.3), channel_id=1, source_target_pairs={{4,8},{20,24},{8,4},{24,20},{5,9},{21,25},{9,5},{25,21},{6,10},{22... | collective-permute-start | bytes 3981320 | tf_op jit(solution)/shard_map/ppermute | solution.py:528
  6.7 4.1 %collective-permute-start.1 = (f32[5,16,128]{2,1,0:T(8,128)S(1)}, f32[5,16,128]{2,1,0:T(8,128)S(1)}, u32[]{:S(2)}, u32[]{:S(2)}) collective-permute-start(f32[5,16,128]{2,1,0:T(8,128)S(1)} %add.9), channel_id=1, source_target_pairs={{0,16},{4,20},{8,24},{12,28},{16,0},{20,4},{24,8},{28,12},{1,17},{... | collective-permute-start | bytes 122888 | tf_op jit(solution)/shard_map/ppermute | solution.py:550
  10.8 11.8 %collective-permute-start.8 = (f32[1152,128]{1,0:T(8,128)S(1)}, f32[1152,128]{1,0:T(8,128)S(1)}, u32[]{:S(2)}, u32[]{:S(2)}) collective-permute-start(f32[1152,128]{1,0:T(8,128)S(1)} %get-tuple-element.42), channel_id=1, source_target_pairs={{12,28},{16,0},{13,29},{17,1},{14,30},{18,2},{15,31},{19,3}} | collective-permute-start | bytes 1769480 | tf_op jit(solution)/shard_map/ppermute | solution.py:553
  12.1 2.8 %collective-permute-start.2 = (f32[5,16,128]{2,1,0:T(8,128)S(1)}, f32[5,16,128]{2,1,0:T(8,128)S(1)}, u32[]{:S(2)}, u32[]{:S(2)}) collective-permute-start(f32[5,16,128]{2,1,0:T(8,128)S(1)} %add.10), channel_id=1, source_target_pairs={{0,4},{8,12},{16,20},{24,28},{4,0},{12,8},{20,16},{28,24},{1,5},{9... | collective-permute-start | bytes 122888 | tf_op jit(solution)/shard_map/ppermute | solution.py:554
  14.9 20.8 %collective-permute-start.7 = (f32[1440,128]{1,0:T(8,128)S(1)}, f32[1440,128]{1,0:T(8,128)S(1)}, u32[]{:S(2)}, u32[]{:S(2)}) collective-permute-start(f32[1440,128]{1,0:T(8,128)S(1)} %get-tuple-element.40), channel_id=1, source_target_pairs={{12,16},{16,12},{13,17},{17,13},{14,18},{18,14},{15,19},{19,15}} | collective-permute-start | bytes 2211848 | tf_op jit(solution)/shard_map/ppermute | solution.py:556
  22.6 12.3 %collective-permute-start.9 = (f32[1152,128]{1,0:T(8,128)S(1)}, f32[1152,128]{1,0:T(8,128)S(1)}, u32[]{:S(2)}, u32[]{:S(2)}) collective-permute-start(f32[1152,128]{1,0:T(8,128)S(1)} %collective-permute-done.8), channel_id=1, source_target_pairs={{28,16},{0,12},{29,17},{1,13},{30,18},{2,14},{31,19},{3,15}} | collective-permute-start | bytes 1769480 | tf_op jit(solution)/shard_map/ppermute | solution.py:569
  24.7 7.3 %collective-permute-start.5 = (f32[2,2688]{1,0:T(2,128)S(1)}, f32[2,2688]{1,0:T(2,128)S(1)}, u32[]{:S(2)}, u32[]{:S(2)}) collective-permute-start(f32[2,2688]{1,0:T(2,128)S(1)} %get-tuple-element.35.west), channel_id=1, source_target_pairs={{1,0},{2,1},{3,2},{0,3},{5,4},{6,5},{7,6},{4,7},{9,8},{10,9},{11,1... | collective-permute-start | bytes 64520 | tf_op jit(solution)/shard_map/ppermute | solution.py:572
  28.8 5.6 %collective-permute-start.4 = (f32[2,2688]{1,0:T(2,128)S(1)}, f32[2,2688]{1,0:T(2,128)S(1)}, u32[]{:S(2)}, u32[]{:S(2)}) collective-permute-start(f32[2,2688]{1,0:T(2,128)S(1)} %get-tuple-element.36.east), channel_id=1, source_target_pairs={{0,1},{1,2},{2,3},{3,0},{4,5},{5,6},{6,7},{7,4},{8,9},{9,10},{10,1... | collective-permute-start | bytes 64520 | tf_op jit(solution)/shard_map/ppermute | solution.py:571
  28.8 5.6 %copy-start.1 = (f32[2,2688]{1,0:T(2,128)S(1)}, f32[2,2688]{1,0:T(2,128)}, u32[]{:S(2)}) copy-start(f32[2,2688]{1,0:T(2,128)} %constant.5.clone.table) | copy-start | bytes 64516

commit v4 on v3

--- a/solution.py
+++ b/solution.py
@@ -122,20 +122,19 @@
     out[4, pl.ds(2 * me + 1, 1), :] = seas[1:2]
 
 
-def split_kernel(source, mask, relayed, direct, west, east, spectra, sea, line, sems):
+def split_kernel(source, relayed, direct, sems):
     first = relayed.shape[0]
-    whole = pltpu.make_async_copy(source, spectra, sems.at[0])
     parts = [
-        pltpu.make_async_copy(source.at[0:first], relayed, sems.at[1]),
-        pltpu.make_async_copy(source.at[first:ROWS], direct, sems.at[2]),
+        pltpu.make_async_copy(source.at[0:first], relayed, sems.at[0]),
+        pltpu.make_async_copy(source.at[first:ROWS], direct, sems.at[1]),
     ]
-    masking = pltpu.make_async_copy(mask, sea, sems.at[3])
-    masking.start()
-    whole.start()
     for part in parts:
         part.start()
-    masking.wait()
-    whole.wait()
+    for part in parts:
+        part.wait()
+
+
+def ends_kernel(spectra, sea, west, east, line):
     seas = sea[...].astype(jnp.float32)
     sub = lax.broadcasted_iota(jnp.int32, (LANES, LANES), 0)
     both = jnp.where(
@@ -156,8 +155,6 @@
         turned = cells.T
         west[:, at : at + LANES] = turned[0:2]
         east[:, at : at + LANES] = turned[LANES - 2 : LANES]
-    for part in parts:
-        part.wait()
 
 
 def table_kernel(bands, geometry, forcing, west_in, east_in, par, west, east):
@@ -266,7 +263,7 @@
         fix[at : at + LANES, :] = tall[:, at : at + LANES].T
 
 
-def base_kernel(par, spectra, beyond, base_first, base_last):
+def base_kernel(par, spectra, beyond_first, beyond_last, base_first, base_last):
     odd = lax.rem(lax.axis_index("band"), 2)
     sea_a, sea_b = wide_row(par, SEA_A), wide_row(par, SEA_B)
     sea_b1, sea_b2 = wide_row(par, SEA_B1), wide_row(par, SEA_B2)
@@ -287,8 +284,9 @@
         )
         return crossing - pltpu.roll(crossing, LANES - 1, 1)
 
-    def one_group(base, first, g, speeds):
+    def one_group(base, beyond, first, g, speeds):
         start = (first + g) * GROUP_ROWS
+        far = g * GROUP_ROWS
         north = speeds * tau
         east_a, east_b = speeds * icos_a, speeds * icos_b
         for d in range(HALF):
@@ -296,8 +294,8 @@
             row_b = pl.ds(start + 2 * d + 1 - odd, 8, stride=ND)
             a = spectra[row_a, :] * sea_a
             b = spectra[row_b, :] * sea_b
-            b1 = beyond[row_a, :] * sea_b1
-            b2 = beyond[row_b, :] * sea_b2
+            b1 = beyond[pl.ds(far + 2 * d + odd, 8, stride=ND), :] * sea_b1
+            b2 = beyond[pl.ds(far + 2 * d + 1 - odd, 8, stride=ND), :] * sea_b2
             c = north * SIN[d] + cur_a
             w = (1.0 / 6.0) - (c * c) * (1.0 / 6.0)
             flux_a = c * (0.5 * (a - c * a) - w * jnp.where(c >= 0.0, a, b - 2.0 * a))
@@ -311,10 +309,13 @@
         return speeds * FREQ_STEP**-GF
 
     speeds = lax.fori_loop(
-        0, FIRST_GROUPS, functools.partial(one_group, base_first, 0), group_speed()
+        0, FIRST_GROUPS, functools.partial(one_group, base_first, beyond_first, 0), group_speed()
     )
     lax.fori_loop(
-        0, GROUPS - FIRST_GROUPS, functools.partial(one_group, base_last, FIRST_GROUPS), speeds
+        0,
+        GROUPS - FIRST_GROUPS,
+        functools.partial(one_group, base_last, beyond_last, FIRST_GROUPS),
+        speeds,
     )
 
 
@@ -524,34 +525,41 @@
     )
     forcing = own + lax.ppermute(own, "band", [(b, b ^ 2) for b in range(bands)])
 
-    rows_after, forcing = lax.optimization_barrier((cells, forcing))
+    part_relayed, part_direct = call(
+        split_kernel,
+        "split",
+        (pltpu.with_memory_space_constraint(cells, pltpu.HBM),),
+        [HBM],
+        [(first_rows, LANES), (last_rows, LANES)],
+        [pltpu.SemaphoreType.DMA((2,))],
+        1.0,
+    )
+    part_relayed, part_direct, forcing, rows_after = lax.optimization_barrier(
+        (part_relayed, part_direct, forcing, cells)
+    )
     straight = lax.ppermute(
         rows_after, "band", swapped([(b, b + 1) for b in range(1, bands - 1, 2) if b != middle])
     )
-    pairs = [(b, b + 1) for b in range(0, bands, 2)]
-    beyond = lax.ppermute(rows_after, "band", swapped(pairs))
-    part_relayed, part_direct, west, east = call(
-        split_kernel,
-        "split",
-        tuple(pltpu.with_memory_space_constraint(v, pltpu.HBM) for v in (cells, sea_mask)),
-        [HBM, HBM],
-        [(first_rows, LANES), (last_rows, LANES), (2, WIDE), (2, WIDE)],
-        [
-            pltpu.VMEM((ROWS, LANES), jnp.float32),
-            pltpu.VMEM(sea_mask.shape, jnp.int32),
-            pltpu.VMEM((LANES, LANES), jnp.float32),
-            pltpu.SemaphoreType.DMA((4,)),
-        ],
+    west, east = call(
+        ends_kernel,
+        "ends",
+        (cells, sea_mask),
+        [VMEM] * 2,
+        [(2, WIDE), (2, WIDE)],
+        [pltpu.VMEM((LANES, LANES), jnp.float32)],
         1.0,
     )
-
     bit = 4
     while bit < bands:
         forcing = forcing + lax.ppermute(forcing, "band", [(b, b ^ bit) for b in range(bands)])
         bit *= 2
-    part_relayed, forcing = lax.optimization_barrier((part_relayed, forcing))
+    part_relayed, part_direct, forcing, west, east = lax.optimization_barrier(
+        (part_relayed, part_direct, forcing, west, east)
+    )
     relay = lax.ppermute(part_relayed, "band", [(middle, bands - 1), (middle + 1, 0)])
+    pairs = [(b, b + 1) for b in range(0, bands, 2)]
     forcing = forcing + lax.ppermute(forcing, "band", swapped(pairs))
+    beyond = [lax.ppermute(part, "band", swapped(pairs)) for part in (part_relayed, part_direct)]
     part_direct, forcing = lax.optimization_barrier((part_direct, forcing))
     direct = lax.ppermute(
         part_direct, "band", [(middle, middle + 1), (middle + 1, middle)]
@@ -566,6 +574,7 @@
         [],
         0.3,
     )
+    relay, par = lax.optimization_barrier((relay, par))
     relayed = lax.ppermute(relay, "band", [(bands - 1, middle + 1), (0, middle)])
     ring = [(s, (s + 1) % spec_count) for s in range(spec_count)]
     from_west = lax.ppermute(east, "spec", ring)
@@ -573,8 +582,8 @@
     base_first, base_last = call(
         base_kernel,
         "base",
-        (par, cells, beyond),
-        [VMEM] * 3,
+        (par, cells, *beyond),
+        [VMEM] * 4,
         [(first_rows, LANES), (last_rows, LANES)],
         [],
         4.0,

time: 38.3 us -> 37.6 us (0.982)
  waiting for transfers between devices: 12.3 us -> 11.5 us
    ppermute x1, waiting for transfers between devices: 0.09 us -> 1.55 us  [per_device(): lax.ppermute(forcing, 'band', [(b, b ^ bit) for b in range(bands)])]
    ppermute x1, waiting for transfers between devices: 1.98 us -> 0.65 us  [per_device(): lax.ppermute(own, 'band', [(b, b ^ 2) for b in range(bands)])]
    ppermute x1, waiting for transfers between devices: 6.99 us -> 6.13 us  [per_device(): lax.ppermute(part_relayed, 'band', [(middle, bands - 1), (middle + 1, 0)])]
    ppermute x1 -> x2, starting transfers between devices: 0.01 us -> 0.49 us  [per_device(): lax.ppermute(part, 'band', swapped(pairs))]
    pallas_call x7 -> x8, Pallas kernels: 10.5 us -> 10.4 us  [call(): pl.pallas_call(kernel, name=name, out_shape=outs, in_specs=specs, out_spe...]
  transfers between devices with their start and end apart: 10 -> 11, of which waited for: 5 -> 5; matrix products, arithmetic and copies ran while one was open for 0% -> 0% of each run, Pallas kernels for 19% -> 19%
where the time goes in v4:
time: 37.6 us; the launch traced here: 37.4 us
  starting transfers between devices  15.4 us (41%)
  waiting for transfers between devices  11.5 us (31%)
  Pallas kernels  10.4 us (28%)
    pallas_call x8, Pallas kernels, call(): pl.pallas_call(kernel, name=name, out_shape=outs, in_specs=specs, out_spe...  10.4 us
    ppermute x1, waiting for transfers between devices, per_device(): lax.ppermute(part_relayed, 'band', [(middle, bands - 1), (middle + 1, 0)])  6.13 us
    ppermute x1, starting transfers between devices, per_device(): from_east = lax.ppermute(west, 'spec', [(t, s) for s, t in ring])  4.15 us
    ppermute x1, starting transfers between devices, per_device(): lax.ppermute(own, 'band', [(b, b ^ 2) for b in range(bands)])  3 us
    ppermute x1, waiting for transfers between devices, per_device(): from_west = lax.ppermute(east, 'spec', ring)  2.36 us
    ppermute x1, starting transfers between devices, per_device(): lax.ppermute(forcing, 'band', [(b, b ^ bit) for b in range(bands)])  2.11 us
    ppermute x1, starting transfers between devices, per_device(): forcing = forcing + lax.ppermute(forcing, 'band', swapped(pairs))  1.59 us
    ppermute x1, waiting for transfers between devices, per_device(): lax.ppermute(forcing, 'band', [(b, b ^ bit) for b in range(bands)])  1.55 us
  transfers between devices with their start and end apart: 11, of which 5 were waited for; matrix products, arithmetic and copies ran while one was open for 0% of the time, Pallas kernels for 19%

profile of v4, /device:TPU:0, one launch (start us, length us, event | category | flops | bytes accessed | tf_op | source)
XLA Modules:
  0.0 37.4 jit_solution(13452470361011802888)
XLA Ops:
  0.0 0.0 copy-start.2
  0.0 0.0 copy-start
  0.0 0.9 %pack_forcing.1 = f32[5,16,128]{2,1,0:T(8,128)S(1)} custom-call(f32[2,16,16]{2,1,0:T(8,128)} %wind.1, f32[2,16,16]{2,1,0:T(8,128)} %current.1, s32[2,128]{1,0:T(2,128)} %sea.3), custom_call_target="tpu_custom_call" | custom-call | bytes 900000 | tf_op jit(solution)/shard_map/pack_forcing/pallas_call | solution.py:487
  1.0 3.0 %collective-permute-start = (f32[5,16,128]{2,1,0:T(8,128)S(1)}, f32[5,16,128]{2,1,0:T(8,128)S(1)}, u32[]{:S(2)}, u32[]{:S(2)}) collective-permute-start(f32[5,16,128]{2,1,0:T(8,128)S(1)} %pack_forcing.1), channel_id=1, source_target_pairs={{0,8},{4,12},{8,0},{12,4},{16,24},{20,28},{24,16},{28,20},{1,9},{5... | collective-permute-start | bytes 122888 | tf_op jit(solution)/shard_map/ppermute | solution.py:526
  4.0 0.0 copy-start.3
  4.0 1.3 %split.1 = (f32[1152,128]{1,0:T(8,128)S(1)}, f32[1440,128]{1,0:T(8,128)S(1)}) custom-call(f32[2592,128]{1,0:T(8,128)} %bitcast.2), custom_call_target="tpu_custom_call" | custom-call | bytes 3000000 | tf_op jit(solution)/shard_map/split/pallas_call | solution.py:487
  5.3 0.6 %collective-permute-done = f32[5,16,128]{2,1,0:T(8,128)S(1)} collective-permute-done((f32[5,16,128]{2,1,0:T(8,128)S(1)}, f32[5,16,128]{2,1,0:T(8,128)S(1)}, u32[]{:S(2)}, u32[]{:S(2)}) %collective-permute-start) | collective-permute-done | bytes 40992 | tf_op jit(solution)/shard_map/ppermute | solution.py:526
  5.9 0.0 copy-done
  6.0 0.7 %collective-permute-start.8 = (f32[2592,128]{1,0:T(8,128)S(1)}, f32[2592,128]{1,0:T(8,128)S(1)}, u32[]{:S(2)}, u32[]{:S(2)}) collective-permute-start(f32[2592,128]{1,0:T(8,128)S(1)} %bitcast.3), channel_id=1, source_target_pairs={{4,8},{20,24},{8,4},{24,20},{5,9},{21,25},{9,5},{25,21},{6,10},{22... | collective-permute-start | bytes 3981320 | tf_op jit(solution)/shard_map/ppermute | solution.py:540
  6.7 2.1 %collective-permute-start.1 = (f32[5,16,128]{2,1,0:T(8,128)S(1)}, f32[5,16,128]{2,1,0:T(8,128)S(1)}, u32[]{:S(2)}, u32[]{:S(2)}) collective-permute-start(f32[5,16,128]{2,1,0:T(8,128)S(1)} %add.9), channel_id=1, source_target_pairs={{0,16},{4,20},{8,24},{12,28},{16,0},{20,4},{24,8},{28,12},{1,17},{... | collective-permute-start | bytes 122888 | tf_op jit(solution)/shard_map/ppermute | solution.py:554
  8.8 0.0 copy-done.2
  8.8 0.4 %ends.1 = (f32[2,2688]{1,0:T(2,128)S(1)}, f32[2,2688]{1,0:T(2,128)S(1)}) custom-call(f32[2592,128]{1,0:T(8,128)S(1)} %bitcast.4, s32[2,128]{1,0:T(2,128)S(1)} %copy-done.2), custom_call_target="tpu_custom_call" | custom-call | bytes 3000000 | tf_op jit(solution)/shard_map/ends/pallas_call | solution.py:487
  9.3 1.6 %collective-permute-done.1 = f32[5,16,128]{2,1,0:T(8,128)S(1)} collective-permute-done((f32[5,16,128]{2,1,0:T(8,128)S(1)}, f32[5,16,128]{2,1,0:T(8,128)S(1)}, u32[]{:S(2)}, u32[]{:S(2)}) %collective-permute-start.1) | collective-permute-done | bytes 40992 | tf_op jit(solution)/shard_map/ppermute | solution.py:554
  10.8 1.3 %collective-permute-start.2 = (f32[1152,128]{1,0:T(8,128)S(1)}, f32[1152,128]{1,0:T(8,128)S(1)}, u32[]{:S(2)}, u32[]{:S(2)}) collective-permute-start(f32[1152,128]{1,0:T(8,128)S(1)} %get-tuple-element.39), channel_id=1, source_target_pairs={{12,28},{16,0},{13,29},{17,1},{14,30},{18,2},{15,31},{19,3}} | collective-permute-start | bytes 1769480 | tf_op jit(solution)/shard_map/ppermute | solution.py:559
  12.1 1.6 %collective-permute-start.3 = (f32[5,16,128]{2,1,0:T(8,128)S(1)}, f32[5,16,128]{2,1,0:T(8,128)S(1)}, u32[]{:S(2)}, u32[]{:S(2)}) collective-permute-start(f32[5,16,128]{2,1,0:T(8,128)S(1)} %add.10), channel_id=1, source_target_pairs={{0,4},{8,12},{16,20},{24,28},{4,0},{12,8},{20,16},{28,24},{1,5},{9... | collective-permute-start | bytes 122888 | tf_op jit(solution)/shard_map/ppermute | solution.py:561
  13.7 0.1 collective-permute-start.5
  13.8 0.8 %collective-permute-done.3 = f32[5,16,128]{2,1,0:T(8,128)S(1)} collective-permute-done((f32[5,16,128]{2,1,0:T(8,128)S(1)}, f32[5,16,128]{2,1,0:T(8,128)S(1)}, u32[]{:S(2)}, u32[]{:S(2)}) %collective-permute-start.3) | collective-permute-done | bytes 40992 | tf_op jit(solution)/shard_map/ppermute | solution.py:561
  14.6 0.7 %collective-permute-start.9 = (f32[1440,128]{1,0:T(8,128)S(1)}, f32[1440,128]{1,0:T(8,128)S(1)}, u32[]{:S(2)}, u32[]{:S(2)}) collective-permute-start(f32[1440,128]{1,0:T(8,128)S(1)} %get-tuple-element.54), channel_id=1, source_target_pairs={{12,16},{16,12},{13,17},{17,13},{14,18},{18,14},{15,19},{19,15}} | collective-permute-start | bytes 2211848 | tf_op jit(solution)/shard_map/ppermute | solution.py:564
  15.3 0.4 %collective-permute-start.4 = (f32[1152,128]{1,0:T(8,128)S(1)}, f32[1152,128]{1,0:T(8,128)S(1)}, u32[]{:S(2)}, u32[]{:S(2)}) collective-permute-start(f32[1152,128]{1,0:T(8,128)S(1)} %get-tuple-element.39), channel_id=1, source_target_pairs={{0,4},{8,12},{16,20},{24,28},{4,0},{12,8},{20,16},{28,24},{1,5},{9... | collective-permute-start | bytes 1769480 | tf_op jit(solution)/shard_map/ppermute | solution.py:562
  15.7 0.0 copy-done.3
  15.7 0.8 %tables.1 = (f32[32,128]{1,0:T(8,128)S(1)}, f32[2,2688]{1,0:T(2,128)S(1)}, f32[2,2688]{1,0:T(2,128)S(1)}) custom-call(f32[8,8]{1,0:T(8,128)S(1)} %copy-done.3, f32[5,16,128]{2,1,0:T(8,128)S(1)} %add.11.forcing, f32[2,2688]{1,0:T(2,128)S(1)} %get-tuple-element.43.west_in, f32[2,2688]{1,0:T(2,128)S(1)} %get-tuple-element.44.east_in), custom_call_target="tpu_custom_call" | custom-call | bytes 900000 | tf_op jit(solution)/shard_map/tables/pallas_call | solution.py:487
  16.4 6.1 %collective-permute-done.2 = f32[1152,128]{1,0:T(8,128)S(1)} collective-permute-done((f32[1152,128]{1,0:T(8,128)S(1)}, f32[1152,128]{1,0:T(8,128)S(1)}, u32[]{:S(2)}, u32[]{:S(2)}) %collective-permute-start.2) | collective-permute-done | bytes 589856 | tf_op jit(solution)/shard_map/ppermute | solution.py:559
  22.6 1.3 %collective-permute-start.10 = (f32[1152,128]{1,0:T(8,128)S(1)}, f32[1152,128]{1,0:T(8,128)S(1)}, u32[]{:S(2)}, u32[]{:S(2)}) collective-permute-start(f32[1152,128]{1,0:T(8,128)S(1)} %collective-permute-done.2), channel_id=1, source_target_pairs={{28,16},{0,12},{29,17},{1,13},{30,18},{2,14},{31,19},{3,15}} | collective-permute-start | bytes 1769480 | tf_op jit(solution)/shard_map/ppermute | solution.py:578
  23.9 0.0 collective-permute-done.4.beyond_first
  23.9 4.2 %collective-permute-start.7 = (f32[2,2688]{1,0:T(2,128)S(1)}, f32[2,2688]{1,0:T(2,128)S(1)}, u32[]{:S(2)}, u32[]{:S(2)}) collective-permute-start(f32[2,2688]{1,0:T(2,128)S(1)} %get-tuple-element.48.west), channel_id=1, source_target_pairs={{1,0},{2,1},{3,2},{0,3},{5,4},{6,5},{7,6},{4,7},{9,8},{10,9},{11,1... | collective-permute-start | bytes 64520 | tf_op jit(solution)/shard_map/ppermute | solution.py:581
  28.1 0.0 collective-permute-done.5.beyond_last
  28.1 0.0 copy-start.1
  28.1 0.0 collective-permute-start.6
  28.1 3.2 %base.1 = (f32[1152,128]{1,0:T(8,128)S(1)}, f32[1440,128]{1,0:T(8,128)S(1)}) custom-call(f32[32,128]{1,0:T(8,128)S(1)} %get-tuple-element.46.par, f32[2592,128]{1,0:T(8,128)S(1)} %bitcast.5, f32[1152,128]{1,0:T(8,128)S(1)} %collective-permute-done.4.beyond_first, f32[1440,128]{1,0:T(8,128)S(1)} %collective-permute-done.5.beyond_last), custom_call_target="tpu_custom_call" | custom-call | bytes 12000000 | tf_op jit(solution)/shard_map/base/pallas_call | solution.py:487
  31.3 0.0 collective-permute-done.7.from_east
  31.3 2.4 %collective-permute-done.6.from_west = f32[2,2688]{1,0:T(2,128)S(1)} collective-permute-done((f32[2,2688]{1,0:T(2,128)S(1)}, f32[2,2688]{1,0:T(2,128)S(1)}, u32[]{:S(2)}, u32[]{:S(2)}) %collective-permute-start.6) | collective-permute-done | bytes 21536 | tf_op jit(solution)/shard_map/ppermute | solution.py:580
  33.7 0.0 copy-done.1
  33.7 0.5 %fix.1 = f32[2688,128]{1,0:T(8,128)S(1)} custom-call(f32[2,2688]{1,0:T(2,128)S(1)} %copy-done.1, f32[32,128]{1,0:T(8,128)S(1)} %get-tuple-element.46.par, f32[2,2688]{1,0:T(2,128)S(1)} %get-tuple-element.48.west, f32[2,2688]{1,0:T(2,128)S(1)} %get-tuple-element.49.east, f32[2,2688]{1,0:T(2,128)S(1)} %collective-permute-done.6.from_west, ...), custom_call_target="tpu_custom_call" | custom-call | bytes 3000000 | tf_op jit(solution)/shard_map/fix/pallas_call | solution.py:487
  34.2 0.0 collective-permute-done.10.split
  34.2 0.0 collective-permute-done.8.straight
  34.2 0.8 %first_groups.1 = (f32[1152,128]{1,0:T(8,128)S(1)}, f32[16,128]{1,0:T(8,128)S(1)}) custom-call(f32[32,128]{1,0:T(8,128)S(1)} %get-tuple-element.46.par, f32[1152,128]{1,0:T(8,128)S(1)} %get-tuple-element.55.base, f32[2688,128]{1,0:T(8,128)S(1)} %fix.1, f32[2592,128]{1,0:T(8,128)S(1)} %collective-permute-done.8.straight, ...), custom_call_target="tpu_custom_call" | custom-call | bytes 3000000 | tf_op jit(solution)/shard_map/first_groups/pallas_call | solution.py:487
  35.0 0.0 collective-permute-done.9.split
  35.0 2.4 %last_groups.1 = f32[2592,128]{1,0:T(8,128)} custom-call(f32[32,128]{1,0:T(8,128)S(1)} %get-tuple-element.46.par, f32[1440,128]{1,0:T(8,128)S(1)} %get-tuple-element.47.base, f32[2688,128]{1,0:T(8,128)S(1)} %fix.1, f32[2592,128]{1,0:T(8,128)S(1)} %collective-permute-done.8.straight, f32[1440,128]{1,0:T(8,128)S(1)} %collective-permute-done.9.split, ...), custom_call_target="tpu_custom_call" | custom-call | bytes 6000000 | tf_op jit(solution)/shard_map/last_groups/pallas_call | solution.py:487
  (3 shorter events, 0.0 us)
Async XLA Ops:
  0.0 8.8 %copy-start.2 = (s32[2,128]{1,0:T(2,128)S(1)}, s32[2,128]{1,0:T(2,128)}, u32[]{:S(2)}) copy-start(s32[2,128]{1,0:T(2,128)} %sea.3) | copy-start | bytes 3076
  0.0 5.9 %copy-start = (f32[1296,2,128]{2,1,0:T(2,128)S(1)}, f32[1296,2,128]{2,1,0:T(2,128)}, u32[]{:S(2)}) copy-start(f32[1296,2,128]{2,1,0:T(2,128)} %param.6) | copy-start | bytes 3981316
  1.0 5.0 %collective-permute-start = (f32[5,16,128]{2,1,0:T(8,128)S(1)}, f32[5,16,128]{2,1,0:T(8,128)S(1)}, u32[]{:S(2)}, u32[]{:S(2)}) collective-permute-start(f32[5,16,128]{2,1,0:T(8,128)S(1)} %pack_forcing.1), channel_id=1, source_target_pairs={{0,8},{4,12},{8,0},{12,4},{16,24},{20,28},{24,16},{28,20},{1,9},{5... | collective-permute-start | bytes 122888 | tf_op jit(solution)/shard_map/ppermute | solution.py:526
  4.0 11.7 %copy-start.3 = (f32[8,8]{1,0:T(8,128)S(1)}, f32[8,8]{1,0:T(8,128)}, u32[]{:S(2)}) copy-start(f32[8,8]{1,0:T(8,128)} %constant.4.clone.geometry) | copy-start | bytes 772
  6.0 28.3 %collective-permute-start.8 = (f32[2592,128]{1,0:T(8,128)S(1)}, f32[2592,128]{1,0:T(8,128)S(1)}, u32[]{:S(2)}, u32[]{:S(2)}) collective-permute-start(f32[2592,128]{1,0:T(8,128)S(1)} %bitcast.3), channel_id=1, source_target_pairs={{4,8},{20,24},{8,4},{24,20},{5,9},{21,25},{9,5},{25,21},{6,10},{22... | collective-permute-start | bytes 3981320 | tf_op jit(solution)/shard_map/ppermute | solution.py:540
  6.7 4.1 %collective-permute-start.1 = (f32[5,16,128]{2,1,0:T(8,128)S(1)}, f32[5,16,128]{2,1,0:T(8,128)S(1)}, u32[]{:S(2)}, u32[]{:S(2)}) collective-permute-start(f32[5,16,128]{2,1,0:T(8,128)S(1)} %add.9), channel_id=1, source_target_pairs={{0,16},{4,20},{8,24},{12,28},{16,0},{20,4},{24,8},{28,12},{1,17},{... | collective-permute-start | bytes 122888 | tf_op jit(solution)/shard_map/ppermute | solution.py:554
  10.8 11.8 %collective-permute-start.2 = (f32[1152,128]{1,0:T(8,128)S(1)}, f32[1152,128]{1,0:T(8,128)S(1)}, u32[]{:S(2)}, u32[]{:S(2)}) collective-permute-start(f32[1152,128]{1,0:T(8,128)S(1)} %get-tuple-element.39), channel_id=1, source_target_pairs={{12,28},{16,0},{13,29},{17,1},{14,30},{18,2},{15,31},{19,3}} | collective-permute-start | bytes 1769480 | tf_op jit(solution)/shard_map/ppermute | solution.py:559
  12.1 2.5 %collective-permute-start.3 = (f32[5,16,128]{2,1,0:T(8,128)S(1)}, f32[5,16,128]{2,1,0:T(8,128)S(1)}, u32[]{:S(2)}, u32[]{:S(2)}) collective-permute-start(f32[5,16,128]{2,1,0:T(8,128)S(1)} %add.10), channel_id=1, source_target_pairs={{0,4},{8,12},{16,20},{24,28},{4,0},{12,8},{20,16},{28,24},{1,5},{9... | collective-permute-start | bytes 122888 | tf_op jit(solution)/shard_map/ppermute | solution.py:561
  13.7 14.4 %collective-permute-start.5 = (f32[1440,128]{1,0:T(8,128)S(1)}, f32[1440,128]{1,0:T(8,128)S(1)}, u32[]{:S(2)}, u32[]{:S(2)}) collective-permute-start(f32[1440,128]{1,0:T(8,128)S(1)} %get-tuple-element.54), channel_id=1, source_target_pairs={{0,4},{8,12},{16,20},{24,28},{4,0},{12,8},{20,16},{28,24},{1,5},{9... | collective-permute-start | bytes 2211848 | tf_op jit(solution)/shard_map/ppermute | solution.py:562
  14.6 20.4 %collective-permute-start.9 = (f32[1440,128]{1,0:T(8,128)S(1)}, f32[1440,128]{1,0:T(8,128)S(1)}, u32[]{:S(2)}, u32[]{:S(2)}) collective-permute-start(f32[1440,128]{1,0:T(8,128)S(1)} %get-tuple-element.54), channel_id=1, source_target_pairs={{12,16},{16,12},{13,17},{17,13},{14,18},{18,14},{15,19},{19,15}} | collective-permute-start | bytes 2211848 | tf_op jit(solution)/shard_map/ppermute | solution.py:564
  15.3 8.6 %collective-permute-start.4 = (f32[1152,128]{1,0:T(8,128)S(1)}, f32[1152,128]{1,0:T(8,128)S(1)}, u32[]{:S(2)}, u32[]{:S(2)}) collective-permute-start(f32[1152,128]{1,0:T(8,128)S(1)} %get-tuple-element.39), channel_id=1, source_target_pairs={{0,4},{8,12},{16,20},{24,28},{4,0},{12,8},{20,16},{28,24},{1,5},{9... | collective-permute-start | bytes 1769480 | tf_op jit(solution)/shard_map/ppermute | solution.py:562
  22.6 11.6 %collective-permute-start.10 = (f32[1152,128]{1,0:T(8,128)S(1)}, f32[1152,128]{1,0:T(8,128)S(1)}, u32[]{:S(2)}, u32[]{:S(2)}) collective-permute-start(f32[1152,128]{1,0:T(8,128)S(1)} %collective-permute-done.2), channel_id=1, source_target_pairs={{28,16},{0,12},{29,17},{1,13},{30,18},{2,14},{31,19},{3,15}} | collective-permute-start | bytes 1769480 | tf_op jit(solution)/shard_map/ppermute | solution.py:578
  23.9 7.4 %collective-permute-start.7 = (f32[2,2688]{1,0:T(2,128)S(1)}, f32[2,2688]{1,0:T(2,128)S(1)}, u32[]{:S(2)}, u32[]{:S(2)}) collective-permute-start(f32[2,2688]{1,0:T(2,128)S(1)} %get-tuple-element.48.west), channel_id=1, source_target_pairs={{1,0},{2,1},{3,2},{0,3},{5,4},{6,5},{7,6},{4,7},{9,8},{10,9},{11,1... | collective-permute-start | bytes 64520 | tf_op jit(solution)/shard_map/ppermute | solution.py:581
  28.1 5.6 %copy-start.1 = (f32[2,2688]{1,0:T(2,128)S(1)}, f32[2,2688]{1,0:T(2,128)}, u32[]{:S(2)}) copy-start(f32[2,2688]{1,0:T(2,128)} %constant.5.clone.table) | copy-start | bytes 64516
  28.1 5.6 %collective-permute-start.6 = (f32[2,2688]{1,0:T(2,128)S(1)}, f32[2,2688]{1,0:T(2,128)S(1)}, u32[]{:S(2)}, u32[]{:S(2)}) collective-permute-start(f32[2,2688]{1,0:T(2,128)S(1)} %get-tuple-element.49.east), channel_id=1, source_target_pairs={{0,1},{1,2},{2,3},{3,0},{4,5},{5,6},{6,7},{7,4},{8,9},{9,10},{10,1... | collective-permute-start | bytes 64520 | tf_op jit(solution)/shard_map/ppermute | solution.py:580

commit v5 on v4

--- a/solution.py
+++ b/solution.py
@@ -100,7 +100,6 @@
 
 
 def pack_kernel(wind, current, sea, out, wind_here, current_here, sea_here, sems):
-    me = lax.axis_index("band")
     rows, strip = wind.shape[1], wind.shape[2]
     copies = [
         pltpu.make_async_copy(wind, wind_here, sems.at[0]),
@@ -109,20 +108,24 @@
     ]
     for copy in copies:
         copy.start()
-    out[4] = jnp.zeros((rows, LANES), jnp.float32)
-    empty = jnp.zeros((rows, LANES - strip), jnp.float32)
+    empty = jnp.zeros((8, LANES - strip), jnp.float32)
     for copy in copies:
         copy.wait()
-    for part, ref in enumerate((current_here, wind_here)):
+    packed = jnp.zeros((8, LANES), jnp.float32)
+    piece = 0
+    for ref in (current_here, wind_here):
         for axis in range(2):
-            wide = jnp.concatenate([ref[axis], empty], axis=1)
-            out[2 * part + axis] = pltpu.roll(wide, me * strip, 1)
-    seas = sea_here[...].astype(jnp.float32)
-    out[4, pl.ds(2 * me, 1), :] = seas[0:1]
-    out[4, pl.ds(2 * me + 1, 1), :] = seas[1:2]
-
-
-def split_kernel(source, relayed, direct, sems):
+            for row in range(0, rows, 8):
+                wide = jnp.concatenate([ref[axis, row : row + 8, :], empty], axis=1)
+                packed = packed + (pltpu.roll(wide, piece * strip, 1) if piece else wide)
+                piece += 1
+    out[0:8, :] = packed
+    out[8:10, :] = sea_here[...].astype(jnp.float32)
+    out[10:16, :] = jnp.zeros((6, LANES), jnp.float32)
+
+
+def split_kernel(source, own, relayed, direct, sems):
+    del own
     first = relayed.shape[0]
     parts = [
         pltpu.make_async_copy(source.at[0:first], relayed, sems.at[0]),
@@ -157,23 +160,41 @@
         east[:, at : at + LANES] = turned[LANES - 2 : LANES]
 
 
-def table_kernel(bands, geometry, forcing, west_in, east_in, par, west, east):
+def table_kernel(bands, order, geometry, slots, west_in, east_in, par, west, east, line):
     me = lax.axis_index("band")
     is_even = lax.rem(me, 2) == 0
+    rows = 2 * bands
+    strip = LANES // bands
+    block = lax.div(lax.broadcasted_iota(jnp.int32, (8, LANES), 1), strip)
+    sources = [jnp.bitwise_xor(me, r) for r in order]
+    moved = [
+        pltpu.roll(slots[16 * k : 16 * k + 8, :], source * strip, 1)
+        for k, source in enumerate(sources)
+    ]
+    for piece in range(rows // 2):
+        row = jnp.zeros((8, LANES), jnp.float32)
+        for source, values in zip(sources, moved):
+            row = jnp.where(block == lax.rem(source + piece, bands), values, row)
+        line[8 * piece : 8 * piece + 8, :] = (
+            pltpu.roll(row, LANES - piece * strip, 1) if piece else row
+        )
+
+    def mask_of(band):
+        found = jnp.zeros((2, LANES), jnp.float32)
+        for k, source in enumerate(sources):
+            found = jnp.where(source == band, slots[16 * k + 8 : 16 * k + 10, :], found)
+        return [found[0:1], found[1:2]]
+
+    seas = mask_of(me - 1) + mask_of(me) + mask_of(me + 1)
     row = 2 * me
     has_south = jnp.where(me > 0, 1.0, 0.0)
     has_north = jnp.where(me < bands - 1, 1.0, 0.0)
 
     def around(part):
-        south = [jnp.maximum(row - 2, 0), jnp.maximum(row - 1, 0)]
-        north = [jnp.minimum(row + 2, 2 * bands - 1), jnp.minimum(row + 3, 2 * bands - 1)]
-        return (
-            [forcing[part, pl.ds(i, 1), :] * has_south for i in south]
-            + [forcing[part, pl.ds(row + i, 1), :] for i in range(2)]
-            + [forcing[part, pl.ds(i, 1), :] * has_north for i in north]
-        )
-
-    seas = around(4)
+        first = part * rows
+        south = line[pl.ds(first + jnp.maximum(row - 1, 0), 1), :] * has_south
+        north = line[pl.ds(first + jnp.minimum(row + 2, rows - 1), 1), :] * has_north
+        return [south] + [line[pl.ds(first + row + i, 1), :] for i in range(2)] + [north]
 
     def pick(low, high):
         return jnp.where(is_even, low, high)
@@ -183,14 +204,14 @@
 
     tau = jnp.where(is_even, 1.0, -1.0)
     north = around(1)
-    face = [0.5 * (north[i] + north[i + 1]) for i in range(1, 4)]
+    face = [0.5 * (north[i] + north[i + 1]) for i in range(3)]
     put(CUR_A, tau * pick(face[0], face[2]))
     put(CUR_M, tau * face[1])
     put(CUR_B, tau * pick(face[2], face[0]))
     lane = lax.broadcasted_iota(jnp.int32, (1, LANES), 1)
     inside = jnp.where(lane == 0, 0.0, 1.0)
-    east_speed = around(0)[2:4]
-    wind_0, wind_1 = around(2)[2:4], around(3)[2:4]
+    east_speed = around(0)[1:3]
+    wind_0, wind_1 = around(2)[1:3], around(3)[1:3]
     shifted = [0.5 * inside * (v + pltpu.roll(v, 1, 1)) for v in east_speed]
     put(CX_A, pick(shifted[0], shifted[1]))
     put(CX_B, pick(shifted[1], shifted[0]))
@@ -263,10 +284,14 @@
         fix[at : at + LANES, :] = tall[:, at : at + LANES].T
 
 
-def base_kernel(par, spectra, beyond_first, beyond_last, base_first, base_last):
+def base_kernel(par, spectra, beyond_first, beyond_last, base_first, base_last, gain_first, gain_last):
     odd = lax.rem(lax.axis_index("band"), 2)
     sea_a, sea_b = wide_row(par, SEA_A), wide_row(par, SEA_B)
     sea_b1, sea_b2 = wide_row(par, SEA_B1), wide_row(par, SEA_B2)
+    sea_a1 = wide_row(par, SEA_A1)
+    into_a1 = wide_row(par, KAP_A) * sea_a1
+    into_a2 = wide_row(par, KAP_A) * wide_row(par, SEA_A2)
+    over_a, over_b = wide_row(par, MU_A) * sea_a1, wide_row(par, MU_B) * sea_a1
     cur_a, cur_m, cur_b = wide_row(par, CUR_A), wide_row(par, CUR_M), wide_row(par, CUR_B)
     cx_a, cx_b = wide_row(par, CX_A), wide_row(par, CX_B)
     kap_a, mu_a = wide_row(par, KAP_A), wide_row(par, MU_A)
@@ -284,7 +309,7 @@
         )
         return crossing - pltpu.roll(crossing, LANES - 1, 1)
 
-    def one_group(base, beyond, first, g, speeds):
+    def one_group(base, gain, beyond, first, g, speeds):
         start = (first + g) * GROUP_ROWS
         far = g * GROUP_ROWS
         north = speeds * tau
@@ -298,67 +323,82 @@
             b2 = beyond[pl.ds(far + 2 * d + 1 - odd, 8, stride=ND), :] * sea_b2
             c = north * SIN[d] + cur_a
             w = (1.0 / 6.0) - (c * c) * (1.0 / 6.0)
-            flux_a = c * (0.5 * (a - c * a) - w * jnp.where(c >= 0.0, a, b - 2.0 * a))
-            flux_m = flux(0.0, a, b, b1, north * SIN[d] + cur_m)
+            inward = c >= 0.0
+            cw = c * w
+            half = 0.5 * c
+            flux_a = (half - half * c) * a - cw * jnp.where(inward, a, b - 2.0 * a)
+            cm = north * SIN[d] + cur_m
+            flux_m = flux(0.0, a, b, b1, cm)
+            away = jnp.where(cm >= 0.0, cm * ((cm * cm) * (1.0 / 6.0) - (1.0 / 6.0)), 0.0)
             flux_b = flux(a, b, b1, b2, north * SIN[d] + cur_b)
             to_a = along_east(a, east_a, cx_a, COS[d])
             to_b = along_east(b, east_b, cx_b, COS[d])
             at = pl.multiple_of(g * (HALF * 16) + d * 16, 8)
             base[pl.ds(at, 8), :] = a + to_a + kap_a * flux_a - mu_a * flux_m
             base[pl.ds(at + 8, 8), :] = b + to_b + mu_b * flux_m - kap_b * flux_b
+            at = pl.multiple_of(g * (HALF * 24) + d * 24, 8)
+            near = half + half * c + jnp.where(inward, 2.0 * cw, -cw)
+            gain[pl.ds(at, 8), :] = into_a1 * near - over_a * away
+            gain[pl.ds(at + 8, 8), :] = into_a2 * jnp.where(inward, -cw, 0.0)
+            gain[pl.ds(at + 16, 8), :] = over_b * away
         return speeds * FREQ_STEP**-GF
 
     speeds = lax.fori_loop(
-        0, FIRST_GROUPS, functools.partial(one_group, base_first, beyond_first, 0), group_speed()
+        0, FIRST_GROUPS, functools.partial(one_group, base_first, gain_first, beyond_first, 0), group_speed()
     )
     lax.fori_loop(
         0,
         GROUPS - FIRST_GROUPS,
-        functools.partial(one_group, base_last, beyond_last, FIRST_GROUPS),
+        functools.partial(one_group, base_last, gain_last, beyond_last, FIRST_GROUPS),
         speeds,
     )
 
 
 def turn(cells, rate):
-    after = [swap_halves(cells[0]), swap_halves(cells[1])]
-    lower = swap_halves(cells[HALF - 1])
-    ring = [lower] + cells + after
+    k = lax.broadcasted_iota(jnp.int32, (8, LANES), 0)
+    first = lax.rem(k, 2) == 0
+    cube = rate * rate * rate
+    ring = [swap_halves(cells[HALF - 1])] + cells
+    ring = ring + [swap_halves(cells[0]), swap_halves(cells[1])]
+    steps = [high - low for low, high in zip(ring, ring[1:])]
+    bends = [high - low for low, high in zip(steps, steps[1:])]
     fluxes = []
     for d in range(HALF):
         mean = 0.5 * (COS[d] + COS[d + 1])
-        fluxes.append(flux(ring[d], ring[d + 1], ring[d + 2], ring[d + 3], rate * mean))
+        low, high = (bends[d + 1], bends[d]) if mean > 0 else (bends[d], bends[d + 1])
+        bend = jnp.where(first, low, high)
+        both = ring[d + 1] + ring[d + 2]
+        weight = rate * (mean / 6.0) - cube * (mean**3 / 6.0)
+        fluxes.append(
+            (rate * (0.5 * mean)) * (both - (rate * mean) * steps[d + 1]) - weight * bend
+        )
     last = swap_halves(fluxes[HALF - 1])
     return [cells[d] - (fluxes[d] - (fluxes[d - 1] if d else last)) for d in range(HALF)]
 
 
-def finish_groups(first, count, skip, par, base, fix, ahead, turned, total):
+def finish_groups(first, count, skip, par, base, gain, fix, ahead, turned, total):
     odd = lax.rem(lax.axis_index("band"), 2)
-    sea_a1, sea_a2 = wide_row(par, SEA_A1), wide_row(par, SEA_A2)
-    cur_a, cur_m = wide_row(par, CUR_A), wide_row(par, CUR_M)
-    kap_a, mu_a, mu_b = wide_row(par, KAP_A), wide_row(par, MU_A), wide_row(par, MU_B)
-    tau = wide_row(par, TAU)
     tan_a, tan_b = wide_row(par, TAN_A), wide_row(par, TAN_B)
 
     def one_group(g, carry):
         speeds, weight, sum_a, sum_b = carry
         start = (skip + g) * GROUP_ROWS
         fix_start = (first + g) * GROUP_ROWS
-        north = speeds * tau
         cells_a, cells_b = [], []
         for d in range(HALF):
-            n1 = ahead[pl.ds(start + 2 * d + 1 - odd, 8, stride=ND), :] * sea_a1
-            n2 = ahead[pl.ds(start + 2 * d + odd, 8, stride=ND), :] * sea_a2
+            n1 = ahead[pl.ds(start + 2 * d + 1 - odd, 8, stride=ND), :]
+            n2 = ahead[pl.ds(start + 2 * d + odd, 8, stride=ND), :]
             fix_a = fix[pl.ds(fix_start + 2 * d + odd, 8, stride=ND), :]
             fix_b = fix[pl.ds(fix_start + 2 * d + 1 - odd, 8, stride=ND), :]
-            c = north * SIN[d] + cur_a
-            w = (1.0 / 6.0) - (c * c) * (1.0 / 6.0)
-            flux_a = c * (0.5 * (n1 + c * n1) - w * jnp.where(c >= 0.0, n2 - 2.0 * n1, n1))
-            c = north * SIN[d] + cur_m
-            w = (c * c) * (1.0 / 6.0) - (1.0 / 6.0)
-            flux_m = jnp.where(c >= 0.0, c * w, 0.0) * n1
             at = pl.multiple_of(g * (HALF * 16) + d * 16, 8)
-            cells_a.append(base[pl.ds(at, 8), :] + fix_a + kap_a * flux_a - mu_a * flux_m)
-            cells_b.append(base[pl.ds(at + 8, 8), :] + fix_b + mu_b * flux_m)
+            by = pl.multiple_of(g * (HALF * 24) + d * 24, 8)
+            cells_a.append(
+                base[pl.ds(at, 8), :]
+                + fix_a
+                + gain[pl.ds(by, 8), :] * n1
+                + gain[pl.ds(by + 8, 8), :] * n2
+            )
+            cells_b.append(base[pl.ds(at + 8, 8), :] + fix_b + gain[pl.ds(by + 16, 8), :] * n1)
         square_a = square_b = 0.0
         for d, v in enumerate(turn(cells_a, speeds * tan_a)):
             at = pl.multiple_of(g * (HALF * 16) + d * 16, 8)
@@ -381,35 +421,41 @@
     _, _, total[0:8, :], total[8:16, :] = lax.fori_loop(0, count, one_group, carry)
 
 
-def finish_either(bands, first, count, par, base, fix, straight, split, turned, total):
+def finish_either(bands, first, count, par, base, gain, fix, straight, split, turned, total):
     me = lax.axis_index("band")
     middle = jnp.logical_or(me == bands // 2 - 1, me == bands // 2)
 
     @pl.when(middle)
     def _():
-        finish_groups(first, count, 0, par, base, fix, split, turned, total)
+        finish_groups(first, count, 0, par, base, gain, fix, split, turned, total)
 
     @pl.when(jnp.logical_not(middle))
     def _():
-        finish_groups(first, count, first, par, base, fix, straight, turned, total)
-
-
-def first_kernel(bands, par, base, fix, straight, split, turned, total):
+        finish_groups(first, count, first, par, base, gain, fix, straight, turned, total)
+
+
+def first_kernel(bands, par, base, gain, fix, straight, split, turned, total):
     total[...] = jnp.zeros((16, LANES), jnp.float32)
-    finish_either(bands, 0, FIRST_GROUPS, par, base, fix, straight, split, turned, total)
-
-
-def last_kernel(bands, par, base, fix, straight, split, done, before, out, turned, total):
+    finish_either(bands, 0, FIRST_GROUPS, par, base, gain, fix, straight, split, turned, total)
+
+
+def last_kernel(
+    bands, par, base, gain, fix, straight, split, done, before, result, turned, total, out, sems
+):
     odd = lax.rem(lax.axis_index("band"), 2)
     later = GROUPS - FIRST_GROUPS
     total[...] = before[...]
-    finish_either(bands, FIRST_GROUPS, later, par, base, fix, straight, split, turned, total)
+    finish_either(bands, FIRST_GROUPS, later, par, base, gain, fix, straight, split, turned, total)
     scale = 2.0 / (NF * ND)
     steep_a = jnp.sum(total[0:8, :], axis=0, keepdims=True) * scale
     steep_b = jnp.sum(total[8:16, :], axis=0, keepdims=True) * scale
     sea_a, sea_b = wide_row(par, SEA_A), wide_row(par, SEA_B)
     w0_a, w0_b = wide_row(par, W0_A), wide_row(par, W0_B)
     w1_a, w1_b = wide_row(par, W1_A), wide_row(par, W1_B)
+
+    def copy_out(g):
+        rows = pl.ds(pl.multiple_of(g * GROUP_ROWS, 8), GROUP_ROWS)
+        return pltpu.make_async_copy(out.at[rows], result.at[rows], sems.at[g])
 
     def one_group(first, ref, g, carry):
         coupling, weight = carry
@@ -428,6 +474,7 @@
             out[pl.ds(start + 2 * d + 1 - odd, 8, stride=ND), :] = (
                 ref[pl.ds(at + 8, 8), :] * gain_b * growth_b
             )
+        copy_out(first + g).start()
         return coupling * FREQ_STEP**GF, weight + GF / NF
 
     k = lax.broadcasted_iota(jnp.int32, (8, LANES), 0)
@@ -439,6 +486,8 @@
     carry = (coupling, freq_weight())
     carry = lax.fori_loop(0, FIRST_GROUPS, functools.partial(one_group, 0, done), carry)
     lax.fori_loop(0, later, functools.partial(one_group, FIRST_GROUPS, turned), carry)
+    for g in range(GROUPS):
+        copy_out(g).wait()
 
 
 def geometry_table(bands):
@@ -479,17 +528,18 @@
 VMEM = pl.BlockSpec(memory_space=pltpu.VMEM)
 SMEM = pl.BlockSpec(memory_space=pltpu.SMEM)
 HBM = pl.BlockSpec(memory_space=pltpu.HBM)
+ANY = pl.BlockSpec(memory_space=pl.ANY)
 PARAMS = pltpu.CompilerParams(vmem_limit_bytes=40 * 1024 * 1024)
 
 
-def call(kernel, name, operands, specs, shapes, scratch, micros):
+def call(kernel, name, operands, specs, shapes, scratch, micros, outs_in=None):
     outs = [jax.ShapeDtypeStruct(s, jnp.float32) for s in shapes]
     return pl.pallas_call(
         kernel,
         name=name,
         out_shape=outs,
         in_specs=specs,
-        out_specs=[VMEM] * len(outs),
+        out_specs=[outs_in or VMEM] * len(outs),
         scratch_shapes=scratch,
         compiler_params=PARAMS,
         cost_estimate=pl.CostEstimate(
@@ -514,7 +564,7 @@
         "pack_forcing",
         tuple(pltpu.with_memory_space_constraint(v, pltpu.HBM) for v in (wind, current, sea_mask)),
         [HBM] * 3,
-        [(5, wind.shape[1], LANES)],
+        [(16, LANES)],
         [
             pltpu.VMEM(wind.shape, jnp.float32),
             pltpu.VMEM(current.shape, jnp.float32),
@@ -523,27 +573,33 @@
         ],
         0.3,
     )
-    forcing = own + lax.ppermute(own, "band", [(b, b ^ 2) for b in range(bands)])
+    order = [0]
+
+    def gathered(values, bit):
+        order.extend([r ^ bit for r in order])
+        other = lax.ppermute(values, "band", [(b, b ^ bit) for b in range(bands)])
+        return jnp.concatenate([values, other], axis=0)
+
+    forcing = gathered(own, 2)
 
     part_relayed, part_direct = call(
         split_kernel,
         "split",
-        (pltpu.with_memory_space_constraint(cells, pltpu.HBM),),
-        [HBM],
+        (pltpu.with_memory_space_constraint(cells, pltpu.HBM), own),
+        [HBM, VMEM],
         [(first_rows, LANES), (last_rows, LANES)],
         [pltpu.SemaphoreType.DMA((2,))],
         1.0,
     )
-    part_relayed, part_direct, forcing, rows_after = lax.optimization_barrier(
-        (part_relayed, part_direct, forcing, cells)
-    )
+    part_direct, rows_after = lax.optimization_barrier((part_direct, cells))
+    part_relayed, forcing, ends_sea = lax.optimization_barrier((part_relayed, forcing, sea_mask))
     straight = lax.ppermute(
         rows_after, "band", swapped([(b, b + 1) for b in range(1, bands - 1, 2) if b != middle])
     )
     west, east = call(
         ends_kernel,
         "ends",
-        (cells, sea_mask),
+        (cells, ends_sea),
         [VMEM] * 2,
         [(2, WIDE), (2, WIDE)],
         [pltpu.VMEM((LANES, LANES), jnp.float32)],
@@ -551,14 +607,14 @@
     )
     bit = 4
     while bit < bands:
-        forcing = forcing + lax.ppermute(forcing, "band", [(b, b ^ bit) for b in range(bands)])
+        forcing = gathered(forcing, bit)
         bit *= 2
     part_relayed, part_direct, forcing, west, east = lax.optimization_barrier(
         (part_relayed, part_direct, forcing, west, east)
     )
     relay = lax.ppermute(part_relayed, "band", [(middle, bands - 1), (middle + 1, 0)])
     pairs = [(b, b + 1) for b in range(0, bands, 2)]
-    forcing = forcing + lax.ppermute(forcing, "band", swapped(pairs))
+    forcing = gathered(forcing, 1)
     beyond = [lax.ppermute(part, "band", swapped(pairs)) for part in (part_relayed, part_direct)]
     part_direct, forcing = lax.optimization_barrier((part_direct, forcing))
     direct = lax.ppermute(
@@ -566,12 +622,12 @@
     )
 
     par, west, east = call(
-        functools.partial(table_kernel, bands),
+        functools.partial(table_kernel, bands, tuple(order)),
         "tables",
         (jnp.asarray(geometry_table(bands)), forcing, west, east),
         [SMEM, VMEM, VMEM, VMEM],
         [(PAR_ROWS, LANES), (2, WIDE), (2, WIDE)],
-        [],
+        [pltpu.VMEM((8 * bands, LANES), jnp.float32)],
         0.3,
     )
     relay, par = lax.optimization_barrier((relay, par))
@@ -579,12 +635,17 @@
     ring = [(s, (s + 1) % spec_count) for s in range(spec_count)]
     from_west = lax.ppermute(east, "spec", ring)
     from_east = lax.ppermute(west, "spec", [(t, s) for s, t in ring])
-    base_first, base_last = call(
+    base_first, base_last, gain_first, gain_last = call(
         base_kernel,
         "base",
         (par, cells, *beyond),
         [VMEM] * 4,
-        [(first_rows, LANES), (last_rows, LANES)],
+        [
+            (first_rows, LANES),
+            (last_rows, LANES),
+            (first_rows * 3 // 2, LANES),
+            (last_rows * 3 // 2, LANES),
+        ],
         [],
         4.0,
     )
@@ -601,8 +662,8 @@
     turned, total = call(
         functools.partial(first_kernel, bands),
         "first_groups",
-        (par, base_first, fix, straight, relayed),
-        [VMEM] * 5,
+        (par, base_first, gain_first, fix, straight, relayed),
+        [VMEM] * 6,
         [(first_rows, LANES), (16, LANES)],
         [],
         1.0,
@@ -610,11 +671,17 @@
     (out,) = call(
         functools.partial(last_kernel, bands),
         "last_groups",
-        (par, base_last, fix, straight, direct, turned, total),
-        [VMEM] * 7,
+        (par, base_last, gain_last, fix, straight, direct, turned, total),
+        [VMEM] * 8,
         [(ROWS, LANES)],
-        [pltpu.VMEM((last_rows, LANES), jnp.float32), pltpu.VMEM((16, LANES), jnp.float32)],
+        [
+            pltpu.VMEM((last_rows, LANES), jnp.float32),
+            pltpu.VMEM((16, LANES), jnp.float32),
+            pltpu.VMEM((ROWS, LANES), jnp.float32),
+            pltpu.SemaphoreType.DMA((GROUPS,)),
+        ],
         2.0,
+        outs_in=ANY,
     )
     return out.reshape(comp_count, row_count, col_count)
 

time: 37.6 us -> 35.4 us (0.941)
  starting transfers between devices: 15.4 us -> 13.1 us
  waiting for transfers between devices: 11.5 us -> 12.2 us
  Pallas kernels: 10.4 us -> 9.76 us
    ppermute x3, starting transfers between devices: 6.71 us -> 4.66 us  [gathered(): other = lax.ppermute(values, 'band', [(b, b ^ bit) for b in range(bands)])]
    ppermute x1, waiting for transfers between devices: 6.13 us -> 7.31 us  [per_device(): lax.ppermute(part_relayed, 'band', [(middle, bands - 1), (middle + 1, 0)])]
    pallas_call x8, Pallas kernels: 10.4 us -> 9.76 us  [call(): pl.pallas_call(kernel, name=name, out_shape=outs, in_specs=specs, out_spe...]
    ppermute x3, waiting for transfers between devices: 2.99 us -> 2.49 us  [gathered(): other = lax.ppermute(values, 'band', [(b, b ^ bit) for b in range(bands)])]
    ppermute x1, starting transfers between devices: 4.15 us -> 3.65 us  [per_device(): from_east = lax.ppermute(west, 'spec', [(t, s) for s, t in ring])]
  transfers between devices with their start and end apart: 11 -> 11, of which waited for: 5 -> 4; matrix products, arithmetic and copies ran while one was open for 0% -> 0% of each run, Pallas kernels for 19% -> 20%
where the time goes in v5:
time: 35.4 us; the launch traced here: 35.2 us
  starting transfers between devices  13.1 us (37%)
  waiting for transfers between devices  12.2 us (34%)
  Pallas kernels  9.76 us (28%)
    pallas_call x8, Pallas kernels, call(): pl.pallas_call(kernel, name=name, out_shape=outs, in_specs=specs, out_spe...  9.76 us
    ppermute x1, waiting for transfers between devices, per_device(): lax.ppermute(part_relayed, 'band', [(middle, bands - 1), (middle + 1, 0)])  7.31 us
    ppermute x3, starting transfers between devices, gathered(): other = lax.ppermute(values, 'band', [(b, b ^ bit) for b in range(bands)])  4.66 us
    ppermute x1, starting transfers between devices, per_device(): from_east = lax.ppermute(west, 'spec', [(t, s) for s, t in ring])  3.65 us
    ppermute x3, waiting for transfers between devices, gathered(): other = lax.ppermute(values, 'band', [(b, b ^ bit) for b in range(bands)])  2.49 us
    ppermute x1, waiting for transfers between devices, per_device(): from_west = lax.ppermute(east, 'spec', ring)  2.35 us
    ppermute x1, starting transfers between devices, per_device(): lax.ppermute(relay, 'band', [(bands - 1, middle + 1), (0, middle)])  1.32 us
    ppermute x1, starting transfers between devices, per_device(): lax.ppermute(part_relayed, 'band', [(middle, bands - 1), (middle + 1, 0)])  1.28 us
  transfers between devices with their start and end apart: 11, of which 4 were waited for; matrix products, arithmetic and copies ran while one was open for 0% of the time, Pallas kernels for 20%

profile of v5, /device:TPU:0, one launch (start us, length us, event | category | flops | bytes accessed | tf_op | source)
XLA Modules:
  0.0 35.2 jit_solution(3991238926442030427)
XLA Ops:
  0.0 0.0 copy-start.3
  0.0 0.0 copy-start
  0.0 0.9 %pack_forcing.1.own = f32[16,128]{1,0:T(8,128)S(1)} custom-call(f32[2,16,16]{2,1,0:T(8,128)} %wind.1, f32[2,16,16]{2,1,0:T(8,128)} %current.1, s32[2,128]{1,0:T(2,128)} %sea.2), custom_call_target="tpu_custom_call" | custom-call | bytes 900000 | tf_op jit(solution)/shard_map/pack_forcing/pallas_call | solution.py:537
  1.0 3.0 %collective-permute-start = (f32[16,128]{1,0:T(8,128)S(1)}, f32[16,128]{1,0:T(8,128)S(1)}, u32[]{:S(2)}, u32[]{:S(2)}) collective-permute-start(f32[16,128]{1,0:T(8,128)S(1)} %pack_forcing.1.own), channel_id=1, source_target_pairs={{0,8},{4,12},{8,0},{12,4},{16,24},{20,28},{24,16},{28,20},{1,9},{5... | collective-permute-start | bytes 24584 | tf_op jit(solution)/shard_map/ppermute | solution.py:580
  4.0 0.0 copy-start.2
  4.0 1.3 %split.1 = (f32[1152,128]{1,0:T(8,128)S(1)}, f32[1440,128]{1,0:T(8,128)S(1)}) custom-call(f32[2592,128]{1,0:T(8,128)} %bitcast.2, f32[16,128]{1,0:T(8,128)S(1)} %pack_forcing.1.own), custom_call_target="tpu_custom_call" | custom-call | bytes 3000000 | tf_op jit(solution)/shard_map/split/pallas_call | solution.py:537
  5.3 0.0 copy-done
  5.3 0.7 %collective-permute-start.8 = (f32[2592,128]{1,0:T(8,128)S(1)}, f32[2592,128]{1,0:T(8,128)S(1)}, u32[]{:S(2)}, u32[]{:S(2)}) collective-permute-start(f32[2592,128]{1,0:T(8,128)S(1)} %bitcast.3), channel_id=1, source_target_pairs={{4,8},{20,24},{8,4},{24,20},{5,9},{21,25},{9,5},{25,21},{6,10},{22... | collective-permute-start | bytes 3981320 | tf_op jit(solution)/shard_map/ppermute | solution.py:596
  6.1 0.0 collective-permute-done
  6.1 1.6 %collective-permute-start.1 = (f32[32,128]{1,0:T(8,128)S(1)}, f32[32,128]{1,0:T(8,128)S(1)}, u32[]{:S(2)}, u32[]{:S(2)}) collective-permute-start(f32[32,128]{1,0:T(8,128)S(1)} %pad_maximum_fusion.2), channel_id=1, source_target_pairs={{0,16},{4,20},{8,24},{12,28},{16,0},{20,4},{24,8},{28,12},{1,17},{... | collective-permute-start | bytes 49160 | tf_op jit(solution)/shard_map/ppermute | solution.py:580
  7.7 0.0 copy-done.3
  7.7 0.4 %ends.1 = (f32[2,2688]{1,0:T(2,128)S(1)}, f32[2,2688]{1,0:T(2,128)S(1)}) custom-call(f32[2592,128]{1,0:T(8,128)S(1)} %bitcast.4, s32[2,128]{1,0:T(2,128)S(1)} %copy-done.3), custom_call_target="tpu_custom_call" | custom-call | bytes 3000000 | tf_op jit(solution)/shard_map/ends/pallas_call | solution.py:537
  8.1 1.8 %collective-permute-done.1 = f32[32,128]{1,0:T(8,128)S(1)} collective-permute-done((f32[32,128]{1,0:T(8,128)S(1)}, f32[32,128]{1,0:T(8,128)S(1)}, u32[]{:S(2)}, u32[]{:S(2)}) %collective-permute-start.1) | collective-permute-done | bytes 16416 | tf_op jit(solution)/shard_map/ppermute | solution.py:580
  9.9 1.3 %collective-permute-start.2 = (f32[1152,128]{1,0:T(8,128)S(1)}, f32[1152,128]{1,0:T(8,128)S(1)}, u32[]{:S(2)}, u32[]{:S(2)}) collective-permute-start(f32[1152,128]{1,0:T(8,128)S(1)} %get-tuple-element.43), channel_id=1, source_target_pairs={{12,28},{16,0},{13,29},{17,1},{14,30},{18,2},{15,31},{19,3}} | collective-permute-start | bytes 1769480 | tf_op jit(solution)/shard_map/ppermute | solution.py:615
  11.2 0.1 collective-permute-start.3
  11.3 0.5 %collective-permute-start.5 = (f32[1440,128]{1,0:T(8,128)S(1)}, f32[1440,128]{1,0:T(8,128)S(1)}, u32[]{:S(2)}, u32[]{:S(2)}) collective-permute-start(f32[1440,128]{1,0:T(8,128)S(1)} %get-tuple-element.59), channel_id=1, source_target_pairs={{0,4},{8,12},{16,20},{24,28},{4,0},{12,8},{20,16},{28,24},{1,5},{9... | collective-permute-start | bytes 2211848 | tf_op jit(solution)/shard_map/ppermute | solution.py:618
  11.8 0.7 %collective-permute-done.3 = f32[64,128]{1,0:T(8,128)S(1)} collective-permute-done((f32[64,128]{1,0:T(8,128)S(1)}, f32[64,128]{1,0:T(8,128)S(1)}, u32[]{:S(2)}, u32[]{:S(2)}) %collective-permute-start.3) | collective-permute-done | bytes 32800 | tf_op jit(solution)/shard_map/ppermute | solution.py:580
  12.5 0.7 %collective-permute-start.9 = (f32[1440,128]{1,0:T(8,128)S(1)}, f32[1440,128]{1,0:T(8,128)S(1)}, u32[]{:S(2)}, u32[]{:S(2)}) collective-permute-start(f32[1440,128]{1,0:T(8,128)S(1)} %get-tuple-element.59), channel_id=1, source_target_pairs={{12,16},{16,12},{13,17},{17,13},{14,18},{18,14},{15,19},{19,15}} | collective-permute-start | bytes 2211848 | tf_op jit(solution)/shard_map/ppermute | solution.py:620
  13.2 0.2 collective-permute-start.4
  13.4 0.0 copy-done.2
  13.4 1.0 %tables.1 = (f32[32,128]{1,0:T(8,128)S(1)}, f32[2,2688]{1,0:T(2,128)S(1)}, f32[2,2688]{1,0:T(2,128)S(1)}) custom-call(f32[8,8]{1,0:T(8,128)S(1)} %copy-done.2, f32[128,128]{1,0:T(8,128)S(1)} %pad_maximum_fusion.slots, f32[2,2688]{1,0:T(2,128)S(1)} %get-tuple-element.47.west_in, f32[2,2688]{1,0:T(2,128)S(1)} %get-tuple-element.48.east_in), custom_call_target="tpu_custom_call" | custom-call | bytes 900000 | tf_op jit(solution)/shard_map/tables/pallas_call | solution.py:537
  14.3 7.3 %collective-permute-done.2 = f32[1152,128]{1,0:T(8,128)S(1)} collective-permute-done((f32[1152,128]{1,0:T(8,128)S(1)}, f32[1152,128]{1,0:T(8,128)S(1)}, u32[]{:S(2)}, u32[]{:S(2)}) %collective-permute-start.2) | collective-permute-done | bytes 589856 | tf_op jit(solution)/shard_map/ppermute | solution.py:615
  21.7 1.3 %collective-permute-start.10 = (f32[1152,128]{1,0:T(8,128)S(1)}, f32[1152,128]{1,0:T(8,128)S(1)}, u32[]{:S(2)}, u32[]{:S(2)}) collective-permute-start(f32[1152,128]{1,0:T(8,128)S(1)} %collective-permute-done.2), channel_id=1, source_target_pairs={{28,16},{0,12},{29,17},{1,13},{30,18},{2,14},{31,19},{3,15}} | collective-permute-start | bytes 1769480 | tf_op jit(solution)/shard_map/ppermute | solution.py:634
  23.0 0.0 collective-permute-done.4.beyond_first
  23.0 3.7 %collective-permute-start.7 = (f32[2,2688]{1,0:T(2,128)S(1)}, f32[2,2688]{1,0:T(2,128)S(1)}, u32[]{:S(2)}, u32[]{:S(2)}) collective-permute-start(f32[2,2688]{1,0:T(2,128)S(1)} %get-tuple-element.53.west), channel_id=1, source_target_pairs={{1,0},{2,1},{3,2},{0,3},{5,4},{6,5},{7,6},{4,7},{9,8},{10,9},{11,1... | collective-permute-start | bytes 64520 | tf_op jit(solution)/shard_map/ppermute | solution.py:637
  26.6 0.0 collective-permute-done.5.beyond_last
  26.6 0.0 copy-start.1
  26.6 0.0 collective-permute-start.6
  26.7 3.2 %base.1 = (f32[1152,128]{1,0:T(8,128)S(1)}, f32[1440,128]{1,0:T(8,128)S(1)}, f32[1728,128]{1,0:T(8,128)S(1)}, f32[2160,128]{1,0:T(8,128)S(1)}) custom-call(f32[32,128]{1,0:T(8,128)S(1)} %get-tuple-element.50.par, f32[2592,128]{1,0:T(8,128)S(1)} %bitcast.5, f32[1152,128]{1,0:T(8,128)S(1)} %collective-permute-done.4.beyond_first, ...), custom_call_target="tpu_custom_call" | custom-call | bytes 12000000 | tf_op jit(solution)/shard_map/base/pallas_call | solution.py:537
  29.9 0.0 collective-permute-done.7.from_east
  29.9 2.4 %collective-permute-done.6.from_west = f32[2,2688]{1,0:T(2,128)S(1)} collective-permute-done((f32[2,2688]{1,0:T(2,128)S(1)}, f32[2,2688]{1,0:T(2,128)S(1)}, u32[]{:S(2)}, u32[]{:S(2)}) %collective-permute-start.6) | collective-permute-done | bytes 21536 | tf_op jit(solution)/shard_map/ppermute | solution.py:636
  32.2 0.0 copy-done.1
  32.2 0.5 %fix.1 = f32[2688,128]{1,0:T(8,128)S(1)} custom-call(f32[2,2688]{1,0:T(2,128)S(1)} %copy-done.1, f32[32,128]{1,0:T(8,128)S(1)} %get-tuple-element.50.par, f32[2,2688]{1,0:T(2,128)S(1)} %get-tuple-element.53.west, f32[2,2688]{1,0:T(2,128)S(1)} %get-tuple-element.54.east, f32[2,2688]{1,0:T(2,128)S(1)} %collective-permute-done.6.from_west, ...), custom_call_target="tpu_custom_call" | custom-call | bytes 3000000 | tf_op jit(solution)/shard_map/fix/pallas_call | solution.py:537
  32.8 0.0 collective-permute-done.10.split
  32.8 0.0 collective-permute-done.8.straight
  32.8 0.5 %first_groups.1 = (f32[1152,128]{1,0:T(8,128)S(1)}, f32[16,128]{1,0:T(8,128)S(1)}) custom-call(f32[32,128]{1,0:T(8,128)S(1)} %get-tuple-element.50.par, f32[1152,128]{1,0:T(8,128)S(1)} %get-tuple-element.60.base, f32[1728,128]{1,0:T(8,128)S(1)} %get-tuple-element.61.gain, f32[2688,128]{1,0:T(8,128)S(1)} %fix.1, ...), custom_call_target="tpu_custom_call" | custom-call | bytes 3000000 | tf_op jit(solution)/shard_map/first_groups/pallas_call | solution.py:537
  33.3 0.0 collective-permute-done.9.split
  33.3 1.8 %last_groups.1 = f32[2592,128]{1,0:T(8,128)} custom-call(f32[32,128]{1,0:T(8,128)S(1)} %get-tuple-element.50.par, f32[1440,128]{1,0:T(8,128)S(1)} %get-tuple-element.51.base, f32[2160,128]{1,0:T(8,128)S(1)} %get-tuple-element.52.gain, f32[2688,128]{1,0:T(8,128)S(1)} %fix.1, f32[2592,128]{1,0:T(8,128)S(1)} %collective-permute-done.8.straight, ...), custom_call_target="tpu_custom_call" | custom-call | bytes 6000000 | tf_op jit(solution)/shard_map/last_groups/pallas_call | solution.py:537
  (3 shorter events, 0.0 us)
Async XLA Ops:
  0.0 7.7 %copy-start.3 = (s32[2,128]{1,0:T(2,128)S(1)}, s32[2,128]{1,0:T(2,128)}, u32[]{:S(2)}) copy-start(s32[2,128]{1,0:T(2,128)} %sea.2) | copy-start | bytes 3076
  0.0 5.3 %copy-start = (f32[1296,2,128]{2,1,0:T(2,128)S(1)}, f32[1296,2,128]{2,1,0:T(2,128)}, u32[]{:S(2)}) copy-start(f32[1296,2,128]{2,1,0:T(2,128)} %param.6) | copy-start | bytes 3981316
  1.0 5.1 %collective-permute-start = (f32[16,128]{1,0:T(8,128)S(1)}, f32[16,128]{1,0:T(8,128)S(1)}, u32[]{:S(2)}, u32[]{:S(2)}) collective-permute-start(f32[16,128]{1,0:T(8,128)S(1)} %pack_forcing.1.own), channel_id=1, source_target_pairs={{0,8},{4,12},{8,0},{12,4},{16,24},{20,28},{24,16},{28,20},{1,9},{5... | collective-permute-start | bytes 24584 | tf_op jit(solution)/shard_map/ppermute | solution.py:580
  4.0 9.4 %copy-start.2 = (f32[8,8]{1,0:T(8,128)S(1)}, f32[8,8]{1,0:T(8,128)}, u32[]{:S(2)}) copy-start(f32[8,8]{1,0:T(8,128)} %constant.4.clone.geometry) | copy-start | bytes 772
  5.3 27.5 %collective-permute-start.8 = (f32[2592,128]{1,0:T(8,128)S(1)}, f32[2592,128]{1,0:T(8,128)S(1)}, u32[]{:S(2)}, u32[]{:S(2)}) collective-permute-start(f32[2592,128]{1,0:T(8,128)S(1)} %bitcast.3), channel_id=1, source_target_pairs={{4,8},{20,24},{8,4},{24,20},{5,9},{21,25},{9,5},{25,21},{6,10},{22... | collective-permute-start | bytes 3981320 | tf_op jit(solution)/shard_map/ppermute | solution.py:596
  6.1 3.8 %collective-permute-start.1 = (f32[32,128]{1,0:T(8,128)S(1)}, f32[32,128]{1,0:T(8,128)S(1)}, u32[]{:S(2)}, u32[]{:S(2)}) collective-permute-start(f32[32,128]{1,0:T(8,128)S(1)} %pad_maximum_fusion.2), channel_id=1, source_target_pairs={{0,16},{4,20},{8,24},{12,28},{16,0},{20,4},{24,8},{28,12},{1,17},{... | collective-permute-start | bytes 49160 | tf_op jit(solution)/shard_map/ppermute | solution.py:580
  9.9 11.8 %collective-permute-start.2 = (f32[1152,128]{1,0:T(8,128)S(1)}, f32[1152,128]{1,0:T(8,128)S(1)}, u32[]{:S(2)}, u32[]{:S(2)}) collective-permute-start(f32[1152,128]{1,0:T(8,128)S(1)} %get-tuple-element.43), channel_id=1, source_target_pairs={{12,28},{16,0},{13,29},{17,1},{14,30},{18,2},{15,31},{19,3}} | collective-permute-start | bytes 1769480 | tf_op jit(solution)/shard_map/ppermute | solution.py:615
  11.2 1.3 %collective-permute-start.3 = (f32[64,128]{1,0:T(8,128)S(1)}, f32[64,128]{1,0:T(8,128)S(1)}, u32[]{:S(2)}, u32[]{:S(2)}) collective-permute-start(f32[64,128]{1,0:T(8,128)S(1)} %pad_maximum_fusion.1), channel_id=1, source_target_pairs={{0,4},{4,0},{8,12},{12,8},{16,20},{20,16},{24,28},{28,24},{1,5},{5... | collective-permute-start | bytes 98312 | tf_op jit(solution)/shard_map/ppermute | solution.py:580
  11.3 15.4 %collective-permute-start.5 = (f32[1440,128]{1,0:T(8,128)S(1)}, f32[1440,128]{1,0:T(8,128)S(1)}, u32[]{:S(2)}, u32[]{:S(2)}) collective-permute-start(f32[1440,128]{1,0:T(8,128)S(1)} %get-tuple-element.59), channel_id=1, source_target_pairs={{0,4},{8,12},{16,20},{24,28},{4,0},{12,8},{20,16},{28,24},{1,5},{9... | collective-permute-start | bytes 2211848 | tf_op jit(solution)/shard_map/ppermute | solution.py:618
  12.5 20.9 %collective-permute-start.9 = (f32[1440,128]{1,0:T(8,128)S(1)}, f32[1440,128]{1,0:T(8,128)S(1)}, u32[]{:S(2)}, u32[]{:S(2)}) collective-permute-start(f32[1440,128]{1,0:T(8,128)S(1)} %get-tuple-element.59), channel_id=1, source_target_pairs={{12,16},{16,12},{13,17},{17,13},{14,18},{18,14},{15,19},{19,15}} | collective-permute-start | bytes 2211848 | tf_op jit(solution)/shard_map/ppermute | solution.py:620
  13.2 9.8 %collective-permute-start.4 = (f32[1152,128]{1,0:T(8,128)S(1)}, f32[1152,128]{1,0:T(8,128)S(1)}, u32[]{:S(2)}, u32[]{:S(2)}) collective-permute-start(f32[1152,128]{1,0:T(8,128)S(1)} %get-tuple-element.43), channel_id=1, source_target_pairs={{0,4},{8,12},{16,20},{24,28},{4,0},{12,8},{20,16},{28,24},{1,5},{9... | collective-permute-start | bytes 1769480 | tf_op jit(solution)/shard_map/ppermute | solution.py:618
  21.7 11.1 %collective-permute-start.10 = (f32[1152,128]{1,0:T(8,128)S(1)}, f32[1152,128]{1,0:T(8,128)S(1)}, u32[]{:S(2)}, u32[]{:S(2)}) collective-permute-start(f32[1152,128]{1,0:T(8,128)S(1)} %collective-permute-done.2), channel_id=1, source_target_pairs={{28,16},{0,12},{29,17},{1,13},{30,18},{2,14},{31,19},{3,15}} | collective-permute-start | bytes 1769480 | tf_op jit(solution)/shard_map/ppermute | solution.py:634
  23.0 6.9 %collective-permute-start.7 = (f32[2,2688]{1,0:T(2,128)S(1)}, f32[2,2688]{1,0:T(2,128)S(1)}, u32[]{:S(2)}, u32[]{:S(2)}) collective-permute-start(f32[2,2688]{1,0:T(2,128)S(1)} %get-tuple-element.53.west), channel_id=1, source_target_pairs={{1,0},{2,1},{3,2},{0,3},{5,4},{6,5},{7,6},{4,7},{9,8},{10,9},{11,1... | collective-permute-start | bytes 64520 | tf_op jit(solution)/shard_map/ppermute | solution.py:637
  26.6 5.6 %copy-start.1 = (f32[2,2688]{1,0:T(2,128)S(1)}, f32[2,2688]{1,0:T(2,128)}, u32[]{:S(2)}) copy-start(f32[2,2688]{1,0:T(2,128)} %constant.5.clone.table) | copy-start | bytes 64516
  26.6 5.6 %collective-permute-start.6 = (f32[2,2688]{1,0:T(2,128)S(1)}, f32[2,2688]{1,0:T(2,128)S(1)}, u32[]{:S(2)}, u32[]{:S(2)}) collective-permute-start(f32[2,2688]{1,0:T(2,128)S(1)} %get-tuple-element.54.east), channel_id=1, source_target_pairs={{0,1},{1,2},{2,3},{3,0},{4,5},{5,6},{6,7},{7,4},{8,9},{9,10},{10,1... | collective-permute-start | bytes 64520 | tf_op jit(solution)/shard_map/ppermute | solution.py:636

commit v6 on v5

--- a/solution.py
+++ b/solution.py
@@ -532,7 +532,7 @@
 PARAMS = pltpu.CompilerParams(vmem_limit_bytes=40 * 1024 * 1024)
 
 
-def call(kernel, name, operands, specs, shapes, scratch, micros, outs_in=None):
+def call(kernel, name, operands, specs, shapes, scratch, micros, outs_in=None, flops=0):
     outs = [jax.ShapeDtypeStruct(s, jnp.float32) for s in shapes]
     return pl.pallas_call(
         kernel,
@@ -543,7 +543,7 @@
         scratch_shapes=scratch,
         compiler_params=PARAMS,
         cost_estimate=pl.CostEstimate(
-            flops=0, bytes_accessed=int(micros * 3.0e6), transcendentals=0
+            flops=flops, bytes_accessed=int(micros * 3.0e6), transcendentals=0
         ),
     )(*operands)
 
@@ -605,6 +605,8 @@
         [pltpu.VMEM((LANES, LANES), jnp.float32)],
         1.0,
     )
+    part_relayed, west, east = lax.optimization_barrier((part_relayed, west, east))
+    relay = lax.ppermute(part_relayed, "band", [(middle, bands - 1), (middle + 1, 0)])
     bit = 4
     while bit < bands:
         forcing = gathered(forcing, bit)
@@ -612,7 +614,6 @@
     part_relayed, part_direct, forcing, west, east = lax.optimization_barrier(
         (part_relayed, part_direct, forcing, west, east)
     )
-    relay = lax.ppermute(part_relayed, "band", [(middle, bands - 1), (middle + 1, 0)])
     pairs = [(b, b + 1) for b in range(0, bands, 2)]
     forcing = gathered(forcing, 1)
     beyond = [lax.ppermute(part, "band", swapped(pairs)) for part in (part_relayed, part_direct)]
@@ -629,6 +630,7 @@
         [(PAR_ROWS, LANES), (2, WIDE), (2, WIDE)],
         [pltpu.VMEM((8 * bands, LANES), jnp.float32)],
         0.3,
+        flops=4200000000,
     )
     relay, par = lax.optimization_barrier((relay, par))
     relayed = lax.ppermute(relay, "band", [(bands - 1, middle + 1), (0, middle)])

time: 35.4 us -> 33.6 us (0.949)
  waiting for transfers between devices: 12.2 us -> 10.1 us
    ppermute x3, waiting for transfers between devices: 2.49 us -> 0.83 us  [gathered(): other = lax.ppermute(values, 'band', [(b, b ^ bit) for b in range(bands)])]
    ppermute x3, starting transfers between devices: 4.66 us -> 5.13 us  [gathered(): other = lax.ppermute(values, 'band', [(b, b ^ bit) for b in range(bands)])]
    ppermute x1, waiting for transfers between devices: 7.31 us -> 6.91 us  [per_device(): lax.ppermute(part_relayed, 'band', [(middle, bands - 1), (middle + 1, 0)])]
  transfers between devices with their start and end apart: 11 -> 11, of which waited for: 4 -> 4; matrix products, arithmetic and copies ran while one was open for 0% -> 0% of each run, Pallas kernels for 20% -> 21%
where the time goes in v6:
time: 33.6 us; the launch traced here: 33.4 us
  starting transfers between devices  13.4 us (40%)
  waiting for transfers between devices  10.1 us (30%)
  Pallas kernels  9.77 us (29%)
    pallas_call x8, Pallas kernels, call(): pl.pallas_call(kernel, name=name, out_shape=outs, in_specs=specs, out_spe...  9.77 us
    ppermute x1, waiting for transfers between devices, per_device(): lax.ppermute(part_relayed, 'band', [(middle, bands - 1), (middle + 1, 0)])  6.91 us
    ppermute x3, starting transfers between devices, gathered(): other = lax.ppermute(values, 'band', [(b, b ^ bit) for b in range(bands)])  5.13 us
    ppermute x1, starting transfers between devices, per_device(): from_east = lax.ppermute(west, 'spec', [(t, s) for s, t in ring])  3.65 us
    ppermute x1, waiting for transfers between devices, per_device(): from_west = lax.ppermute(east, 'spec', ring)  2.35 us
    ppermute x1, starting transfers between devices, per_device(): lax.ppermute(relay, 'band', [(bands - 1, middle + 1), (0, middle)])  1.32 us
    ppermute x1, starting transfers between devices, per_device(): lax.ppermute(part_relayed, 'band', [(middle, bands - 1), (middle + 1, 0)])  1.3 us
    ppermute x3, waiting for transfers between devices, gathered(): other = lax.ppermute(values, 'band', [(b, b ^ bit) for b in range(bands)])  0.83 us
  transfers between devices with their start and end apart: 11, of which 4 were waited for; matrix products, arithmetic and copies ran while one was open for 0% of the time, Pallas kernels for 21%

profile of v6, /device:TPU:0, one launch (start us, length us, event | category | flops | bytes accessed | tf_op | source)
XLA Modules:
  0.0 33.4 jit_solution(10706724706255031187)
XLA Ops:
  0.0 0.0 copy-start.2
  0.0 0.0 copy-start
  0.0 0.9 %pack_forcing.1.own = f32[16,128]{1,0:T(8,128)S(1)} custom-call(f32[2,16,16]{2,1,0:T(8,128)} %wind.1, f32[2,16,16]{2,1,0:T(8,128)} %current.1, s32[2,128]{1,0:T(2,128)} %sea.2), custom_call_target="tpu_custom_call" | custom-call | bytes 900000 | tf_op jit(solution)/shard_map/pack_forcing/pallas_call | solution.py:537
  1.0 3.0 %collective-permute-start = (f32[16,128]{1,0:T(8,128)S(1)}, f32[16,128]{1,0:T(8,128)S(1)}, u32[]{:S(2)}, u32[]{:S(2)}) collective-permute-start(f32[16,128]{1,0:T(8,128)S(1)} %pack_forcing.1.own), channel_id=1, source_target_pairs={{0,8},{4,12},{8,0},{12,4},{16,24},{20,28},{24,16},{28,20},{1,9},{5... | collective-permute-start | bytes 24584 | tf_op jit(solution)/shard_map/ppermute | solution.py:580
  4.0 0.0 copy-start.3
  4.0 1.3 %split.1 = (f32[1152,128]{1,0:T(8,128)S(1)}, f32[1440,128]{1,0:T(8,128)S(1)}) custom-call(f32[2592,128]{1,0:T(8,128)} %bitcast.2, f32[16,128]{1,0:T(8,128)S(1)} %pack_forcing.1.own), custom_call_target="tpu_custom_call" | custom-call | bytes 3000000 | tf_op jit(solution)/shard_map/split/pallas_call | solution.py:537
  5.3 0.0 copy-done
  5.3 0.7 %collective-permute-start.8 = (f32[2592,128]{1,0:T(8,128)S(1)}, f32[2592,128]{1,0:T(8,128)S(1)}, u32[]{:S(2)}, u32[]{:S(2)}) collective-permute-start(f32[2592,128]{1,0:T(8,128)S(1)} %bitcast.3), channel_id=1, source_target_pairs={{4,8},{20,24},{8,4},{24,20},{5,9},{21,25},{9,5},{25,21},{6,10},{22... | collective-permute-start | bytes 3981320 | tf_op jit(solution)/shard_map/ppermute | solution.py:596
  6.1 0.0 collective-permute-done
  6.1 1.6 %collective-permute-start.2 = (f32[32,128]{1,0:T(8,128)S(1)}, f32[32,128]{1,0:T(8,128)S(1)}, u32[]{:S(2)}, u32[]{:S(2)}) collective-permute-start(f32[32,128]{1,0:T(8,128)S(1)} %pad_maximum_fusion.2), channel_id=1, source_target_pairs={{0,16},{4,20},{8,24},{12,28},{16,0},{20,4},{24,8},{28,12},{1,17},{... | collective-permute-start | bytes 49160 | tf_op jit(solution)/shard_map/ppermute | solution.py:580
  7.7 0.0 copy-done.2
  7.7 0.4 %ends.1 = (f32[2,2688]{1,0:T(2,128)S(1)}, f32[2,2688]{1,0:T(2,128)S(1)}) custom-call(f32[2592,128]{1,0:T(8,128)S(1)} %bitcast.4, s32[2,128]{1,0:T(2,128)S(1)} %copy-done.2), custom_call_target="tpu_custom_call" | custom-call | bytes 3000000 | tf_op jit(solution)/shard_map/ends/pallas_call | solution.py:537
  8.1 1.3 %collective-permute-start.1 = (f32[1152,128]{1,0:T(8,128)S(1)}, f32[1152,128]{1,0:T(8,128)S(1)}, u32[]{:S(2)}, u32[]{:S(2)}) collective-permute-start(f32[1152,128]{1,0:T(8,128)S(1)} %get-tuple-element.56), channel_id=1, source_target_pairs={{12,28},{16,0},{13,29},{17,1},{14,30},{18,2},{15,31},{19,3}} | collective-permute-start | bytes 1769480 | tf_op jit(solution)/shard_map/ppermute | solution.py:609
  9.4 0.5 %collective-permute-done.2 = f32[32,128]{1,0:T(8,128)S(1)} collective-permute-done((f32[32,128]{1,0:T(8,128)S(1)}, f32[32,128]{1,0:T(8,128)S(1)}, u32[]{:S(2)}, u32[]{:S(2)}) %collective-permute-start.2) | collective-permute-done | bytes 16416 | tf_op jit(solution)/shard_map/ppermute | solution.py:580
  9.9 0.5 %collective-permute-start.3 = (f32[64,128]{1,0:T(8,128)S(1)}, f32[64,128]{1,0:T(8,128)S(1)}, u32[]{:S(2)}, u32[]{:S(2)}) collective-permute-start(f32[64,128]{1,0:T(8,128)S(1)} %pad_maximum_fusion.1), channel_id=1, source_target_pairs={{0,4},{4,0},{8,12},{12,8},{16,20},{20,16},{24,28},{28,24},{1,5},{5... | collective-permute-start | bytes 98312 | tf_op jit(solution)/shard_map/ppermute | solution.py:580
  10.4 0.1 collective-permute-start.4
  10.5 0.4 %collective-permute-start.5 = (f32[1440,128]{1,0:T(8,128)S(1)}, f32[1440,128]{1,0:T(8,128)S(1)}, u32[]{:S(2)}, u32[]{:S(2)}) collective-permute-start(f32[1440,128]{1,0:T(8,128)S(1)} %get-tuple-element.65), channel_id=1, source_target_pairs={{0,4},{8,12},{16,20},{24,28},{4,0},{12,8},{20,16},{28,24},{1,5},{9... | collective-permute-start | bytes 2211848 | tf_op jit(solution)/shard_map/ppermute | solution.py:619
  10.9 0.3 %collective-permute-done.3 = f32[64,128]{1,0:T(8,128)S(1)} collective-permute-done((f32[64,128]{1,0:T(8,128)S(1)}, f32[64,128]{1,0:T(8,128)S(1)}, u32[]{:S(2)}, u32[]{:S(2)}) %collective-permute-start.3) | collective-permute-done | bytes 32800 | tf_op jit(solution)/shard_map/ppermute | solution.py:580
  11.3 0.7 %collective-permute-start.9 = (f32[1440,128]{1,0:T(8,128)S(1)}, f32[1440,128]{1,0:T(8,128)S(1)}, u32[]{:S(2)}, u32[]{:S(2)}) collective-permute-start(f32[1440,128]{1,0:T(8,128)S(1)} %get-tuple-element.65), channel_id=1, source_target_pairs={{12,16},{16,12},{13,17},{17,13},{14,18},{18,14},{15,19},{19,15}} | collective-permute-start | bytes 2211848 | tf_op jit(solution)/shard_map/ppermute | solution.py:621
  12.0 0.0 copy-done.3
  12.0 1.0 %tables.1 = (f32[32,128]{1,0:T(8,128)S(1)}, f32[2,2688]{1,0:T(2,128)S(1)}, f32[2,2688]{1,0:T(2,128)S(1)}) custom-call(f32[8,8]{1,0:T(8,128)S(1)} %copy-done.3, f32[128,128]{1,0:T(8,128)S(1)} %pad_maximum_fusion.slots, f32[2,2688]{1,0:T(2,128)S(1)} %get-tuple-element.52.west_in, f32[2,2688]{1,0:T(2,128)S(1)} %get-tuple-element.53.east_in), custom_call_target="tpu_custom_call" | custom-call | flops 4200000000 | bytes 900000 | tf_op jit(solution)/shard_map/tables/pallas_call | solution.py:537
  13.0 6.9 %collective-permute-done.1 = f32[1152,128]{1,0:T(8,128)S(1)} collective-permute-done((f32[1152,128]{1,0:T(8,128)S(1)}, f32[1152,128]{1,0:T(8,128)S(1)}, u32[]{:S(2)}, u32[]{:S(2)}) %collective-permute-start.1) | collective-permute-done | bytes 589856 | tf_op jit(solution)/shard_map/ppermute | solution.py:609
  19.9 1.3 %collective-permute-start.10 = (f32[1152,128]{1,0:T(8,128)S(1)}, f32[1152,128]{1,0:T(8,128)S(1)}, u32[]{:S(2)}, u32[]{:S(2)}) collective-permute-start(f32[1152,128]{1,0:T(8,128)S(1)} %collective-permute-done.1), channel_id=1, source_target_pairs={{28,16},{0,12},{29,17},{1,13},{30,18},{2,14},{31,19},{3,15}} | collective-permute-start | bytes 1769480 | tf_op jit(solution)/shard_map/ppermute | solution.py:636
  21.2 0.0 collective-permute-done.4.beyond_first
  21.2 3.7 %collective-permute-start.7 = (f32[2,2688]{1,0:T(2,128)S(1)}, f32[2,2688]{1,0:T(2,128)S(1)}, u32[]{:S(2)}, u32[]{:S(2)}) collective-permute-start(f32[2,2688]{1,0:T(2,128)S(1)} %get-tuple-element.59.west), channel_id=1, source_target_pairs={{1,0},{2,1},{3,2},{0,3},{5,4},{6,5},{7,6},{4,7},{9,8},{10,9},{11,1... | collective-permute-start | bytes 64520 | tf_op jit(solution)/shard_map/ppermute | solution.py:639
  24.9 0.0 collective-permute-done.5.beyond_last
  24.9 0.0 copy-start.1
  24.9 0.0 collective-permute-start.6
  24.9 3.2 %base.1 = (f32[1152,128]{1,0:T(8,128)S(1)}, f32[1440,128]{1,0:T(8,128)S(1)}, f32[1728,128]{1,0:T(8,128)S(1)}, f32[2160,128]{1,0:T(8,128)S(1)}) custom-call(f32[32,128]{1,0:T(8,128)S(1)} %get-tuple-element.55.par, f32[2592,128]{1,0:T(8,128)S(1)} %bitcast.5, f32[1152,128]{1,0:T(8,128)S(1)} %collective-permute-done.4.beyond_first, ...), custom_call_target="tpu_custom_call" | custom-call | bytes 12000000 | tf_op jit(solution)/shard_map/base/pallas_call | solution.py:537
  28.1 0.0 collective-permute-done.7.from_east
  28.1 2.4 %collective-permute-done.6.from_west = f32[2,2688]{1,0:T(2,128)S(1)} collective-permute-done((f32[2,2688]{1,0:T(2,128)S(1)}, f32[2,2688]{1,0:T(2,128)S(1)}, u32[]{:S(2)}, u32[]{:S(2)}) %collective-permute-start.6) | collective-permute-done | bytes 21536 | tf_op jit(solution)/shard_map/ppermute | solution.py:638
  30.5 0.0 copy-done.1
  30.5 0.5 %fix.1 = f32[2688,128]{1,0:T(8,128)S(1)} custom-call(f32[2,2688]{1,0:T(2,128)S(1)} %copy-done.1, f32[32,128]{1,0:T(8,128)S(1)} %get-tuple-element.55.par, f32[2,2688]{1,0:T(2,128)S(1)} %get-tuple-element.59.west, f32[2,2688]{1,0:T(2,128)S(1)} %get-tuple-element.60.east, f32[2,2688]{1,0:T(2,128)S(1)} %collective-permute-done.6.from_west, ...), custom_call_target="tpu_custom_call" | custom-call | bytes 3000000 | tf_op jit(solution)/shard_map/fix/pallas_call | solution.py:537
  31.0 0.0 collective-permute-done.10.split
  31.0 0.0 collective-permute-done.8.straight
  31.0 0.5 %first_groups.1 = (f32[1152,128]{1,0:T(8,128)S(1)}, f32[16,128]{1,0:T(8,128)S(1)}) custom-call(f32[32,128]{1,0:T(8,128)S(1)} %get-tuple-element.55.par, f32[1152,128]{1,0:T(8,128)S(1)} %get-tuple-element.66.base, f32[1728,128]{1,0:T(8,128)S(1)} %get-tuple-element.67.gain, f32[2688,128]{1,0:T(8,128)S(1)} %fix.1, ...), custom_call_target="tpu_custom_call" | custom-call | bytes 3000000 | tf_op jit(solution)/shard_map/first_groups/pallas_call | solution.py:537
  31.6 0.0 collective-permute-done.9.split
  31.6 1.8 %last_groups.1 = f32[2592,128]{1,0:T(8,128)} custom-call(f32[32,128]{1,0:T(8,128)S(1)} %get-tuple-element.55.par, f32[1440,128]{1,0:T(8,128)S(1)} %get-tuple-element.57.base, f32[2160,128]{1,0:T(8,128)S(1)} %get-tuple-element.58.gain, f32[2688,128]{1,0:T(8,128)S(1)} %fix.1, f32[2592,128]{1,0:T(8,128)S(1)} %collective-permute-done.8.straight, ...), custom_call_target="tpu_custom_call" | custom-call | bytes 6000000 | tf_op jit(solution)/shard_map/last_groups/pallas_call | solution.py:537
  (3 shorter events, 0.0 us)
Async XLA Ops:
  0.0 7.7 %copy-start.2 = (s32[2,128]{1,0:T(2,128)S(1)}, s32[2,128]{1,0:T(2,128)}, u32[]{:S(2)}) copy-start(s32[2,128]{1,0:T(2,128)} %sea.2) | copy-start | bytes 3076
  0.0 5.3 %copy-start = (f32[1296,2,128]{2,1,0:T(2,128)S(1)}, f32[1296,2,128]{2,1,0:T(2,128)}, u32[]{:S(2)}) copy-start(f32[1296,2,128]{2,1,0:T(2,128)} %param.6) | copy-start | bytes 3981316
  1.0 5.1 %collective-permute-start = (f32[16,128]{1,0:T(8,128)S(1)}, f32[16,128]{1,0:T(8,128)S(1)}, u32[]{:S(2)}, u32[]{:S(2)}) collective-permute-start(f32[16,128]{1,0:T(8,128)S(1)} %pack_forcing.1.own), channel_id=1, source_target_pairs={{0,8},{4,12},{8,0},{12,4},{16,24},{20,28},{24,16},{28,20},{1,9},{5... | collective-permute-start | bytes 24584 | tf_op jit(solution)/shard_map/ppermute | solution.py:580
  4.0 8.0 %copy-start.3 = (f32[8,8]{1,0:T(8,128)S(1)}, f32[8,8]{1,0:T(8,128)}, u32[]{:S(2)}) copy-start(f32[8,8]{1,0:T(8,128)} %constant.4.clone.geometry) | copy-start | bytes 772
  5.3 25.7 %collective-permute-start.8 = (f32[2592,128]{1,0:T(8,128)S(1)}, f32[2592,128]{1,0:T(8,128)S(1)}, u32[]{:S(2)}, u32[]{:S(2)}) collective-permute-start(f32[2592,128]{1,0:T(8,128)S(1)} %bitcast.3), channel_id=1, source_target_pairs={{4,8},{20,24},{8,4},{24,20},{5,9},{21,25},{9,5},{25,21},{6,10},{22... | collective-permute-start | bytes 3981320 | tf_op jit(solution)/shard_map/ppermute | solution.py:596
  6.1 3.8 %collective-permute-start.2 = (f32[32,128]{1,0:T(8,128)S(1)}, f32[32,128]{1,0:T(8,128)S(1)}, u32[]{:S(2)}, u32[]{:S(2)}) collective-permute-start(f32[32,128]{1,0:T(8,128)S(1)} %pad_maximum_fusion.2), channel_id=1, source_target_pairs={{0,16},{4,20},{8,24},{12,28},{16,0},{20,4},{24,8},{28,12},{1,17},{... | collective-permute-start | bytes 49160 | tf_op jit(solution)/shard_map/ppermute | solution.py:580
  8.1 11.8 %collective-permute-start.1 = (f32[1152,128]{1,0:T(8,128)S(1)}, f32[1152,128]{1,0:T(8,128)S(1)}, u32[]{:S(2)}, u32[]{:S(2)}) collective-permute-start(f32[1152,128]{1,0:T(8,128)S(1)} %get-tuple-element.56), channel_id=1, source_target_pairs={{12,28},{16,0},{13,29},{17,1},{14,30},{18,2},{15,31},{19,3}} | collective-permute-start | bytes 1769480 | tf_op jit(solution)/shard_map/ppermute | solution.py:609
  9.9 1.4 %collective-permute-start.3 = (f32[64,128]{1,0:T(8,128)S(1)}, f32[64,128]{1,0:T(8,128)S(1)}, u32[]{:S(2)}, u32[]{:S(2)}) collective-permute-start(f32[64,128]{1,0:T(8,128)S(1)} %pad_maximum_fusion.1), channel_id=1, source_target_pairs={{0,4},{4,0},{8,12},{12,8},{16,20},{20,16},{24,28},{28,24},{1,5},{5... | collective-permute-start | bytes 98312 | tf_op jit(solution)/shard_map/ppermute | solution.py:580
  10.4 10.8 %collective-permute-start.4 = (f32[1152,128]{1,0:T(8,128)S(1)}, f32[1152,128]{1,0:T(8,128)S(1)}, u32[]{:S(2)}, u32[]{:S(2)}) collective-permute-start(f32[1152,128]{1,0:T(8,128)S(1)} %get-tuple-element.56), channel_id=1, source_target_pairs={{0,4},{8,12},{16,20},{24,28},{4,0},{12,8},{20,16},{28,24},{1,5},{9... | collective-permute-start | bytes 1769480 | tf_op jit(solution)/shard_map/ppermute | solution.py:619
  10.5 14.4 %collective-permute-start.5 = (f32[1440,128]{1,0:T(8,128)S(1)}, f32[1440,128]{1,0:T(8,128)S(1)}, u32[]{:S(2)}, u32[]{:S(2)}) collective-permute-start(f32[1440,128]{1,0:T(8,128)S(1)} %get-tuple-element.65), channel_id=1, source_target_pairs={{0,4},{8,12},{16,20},{24,28},{4,0},{12,8},{20,16},{28,24},{1,5},{9... | collective-permute-start | bytes 2211848 | tf_op jit(solution)/shard_map/ppermute | solution.py:619
  11.3 20.3 %collective-permute-start.9 = (f32[1440,128]{1,0:T(8,128)S(1)}, f32[1440,128]{1,0:T(8,128)S(1)}, u32[]{:S(2)}, u32[]{:S(2)}) collective-permute-start(f32[1440,128]{1,0:T(8,128)S(1)} %get-tuple-element.65), channel_id=1, source_target_pairs={{12,16},{16,12},{13,17},{17,13},{14,18},{18,14},{15,19},{19,15}} | collective-permute-start | bytes 2211848 | tf_op jit(solution)/shard_map/ppermute | solution.py:621
  19.9 11.1 %collective-permute-start.10 = (f32[1152,128]{1,0:T(8,128)S(1)}, f32[1152,128]{1,0:T(8,128)S(1)}, u32[]{:S(2)}, u32[]{:S(2)}) collective-permute-start(f32[1152,128]{1,0:T(8,128)S(1)} %collective-permute-done.1), channel_id=1, source_target_pairs={{28,16},{0,12},{29,17},{1,13},{30,18},{2,14},{31,19},{3,15}} | collective-permute-start | bytes 1769480 | tf_op jit(solution)/shard_map/ppermute | solution.py:636
  21.2 6.9 %collective-permute-start.7 = (f32[2,2688]{1,0:T(2,128)S(1)}, f32[2,2688]{1,0:T(2,128)S(1)}, u32[]{:S(2)}, u32[]{:S(2)}) collective-permute-start(f32[2,2688]{1,0:T(2,128)S(1)} %get-tuple-element.59.west), channel_id=1, source_target_pairs={{1,0},{2,1},{3,2},{0,3},{5,4},{6,5},{7,6},{4,7},{9,8},{10,9},{11,1... | collective-permute-start | bytes 64520 | tf_op jit(solution)/shard_map/ppermute | solution.py:639
  24.9 5.6 %copy-start.1 = (f32[2,2688]{1,0:T(2,128)S(1)}, f32[2,2688]{1,0:T(2,128)}, u32[]{:S(2)}) copy-start(f32[2,2688]{1,0:T(2,128)} %constant.5.clone.table) | copy-start | bytes 64516
  24.9 5.6 %collective-permute-start.6 = (f32[2,2688]{1,0:T(2,128)S(1)}, f32[2,2688]{1,0:T(2,128)S(1)}, u32[]{:S(2)}, u32[]{:S(2)}) collective-permute-start(f32[2,2688]{1,0:T(2,128)S(1)} %get-tuple-element.60.east), channel_id=1, source_target_pairs={{0,1},{1,2},{2,3},{3,0},{4,5},{5,6},{6,7},{7,4},{8,9},{9,10},{10,1... | collective-permute-start | bytes 64520 | tf_op jit(solution)/shard_map/ppermute | solution.py:638

commit v7 on v6

--- a/solution.py
+++ b/solution.py
@@ -160,7 +160,7 @@
         east[:, at : at + LANES] = turned[LANES - 2 : LANES]
 
 
-def table_kernel(bands, order, geometry, slots, west_in, east_in, par, west, east, line):
+def table_kernel(bands, order, geometry, slots, west_in, east_in, par, first, second, line):
     me = lax.axis_index("band")
     is_even = lax.rem(me, 2) == 0
     rows = 2 * bands
@@ -239,18 +239,24 @@
     put(ICOS_1, icos[1])
     par[26:32, :] = jnp.zeros((6, LANES), jnp.float32)
 
-    west[...] = west_in[...]
-    east[...] = east_in[...]
-    for i in range(2):
-        west[:, ROWS + i : ROWS + i + 1] = jnp.concatenate(
-            [east_speed[i][:, j : j + 1] for j in range(2)], axis=0
-        )
-        east[:, ROWS + i : ROWS + i + 1] = jnp.concatenate(
-            [east_speed[i][:, j : j + 1] for j in (LANES - 2, LANES - 1)], axis=0
-        )
-
-
-def fix_kernel(table, par, west, east, from_west, from_east, fix, tall):
+    ends = []
+    for values, columns in ((west_in[...], (0, 1)), (east_in[...], (LANES - 2, LANES - 1))):
+        lane = lax.broadcasted_iota(jnp.int32, values.shape, 1)
+        for i in range(2):
+            pair = jnp.concatenate([east_speed[i][:, j : j + 1] for j in columns], axis=0)
+            values = jnp.where(lane == ROWS + i, pair, values)
+        ends.append(values)
+    even_spec = lax.rem(lax.axis_index("spec"), 2) == 0
+    first[...] = jnp.where(even_spec, ends[0], ends[1])
+    second[...] = jnp.where(even_spec, ends[1], ends[0])
+
+
+def fix_kernel(table, par, first_here, second_here, first_there, second_there, fix, tall):
+    even_spec = lax.rem(lax.axis_index("spec"), 2) == 0
+    west = jnp.where(even_spec, first_here[...], second_here[...])
+    east = jnp.where(even_spec, second_here[...], first_here[...])
+    from_west = jnp.where(even_spec, first_there[...], second_there[...])
+    from_east = jnp.where(even_spec, second_there[...], first_there[...])
     lane = lax.broadcasted_iota(jnp.int32, (1, WIDE), 1)
     even_row = lax.rem(lane, 2) == 0
     speed = table[0:1] * par[ICOS_0 : ICOS_0 + 1, 0:1] + table[1:2] * par[ICOS_1 : ICOS_1 + 1, 0:1]
@@ -591,10 +597,9 @@
         [pltpu.SemaphoreType.DMA((2,))],
         1.0,
     )
-    part_direct, rows_after = lax.optimization_barrier((part_direct, cells))
     part_relayed, forcing, ends_sea = lax.optimization_barrier((part_relayed, forcing, sea_mask))
     straight = lax.ppermute(
-        rows_after, "band", swapped([(b, b + 1) for b in range(1, bands - 1, 2) if b != middle])
+        cells, "band", swapped([(b, b + 1) for b in range(1, bands - 1, 2) if b != middle])
     )
     west, east = call(
         ends_kernel,
@@ -622,7 +627,7 @@
         part_direct, "band", [(middle, middle + 1), (middle + 1, middle)]
     )
 
-    par, west, east = call(
+    par, first_here, second_here = call(
         functools.partial(table_kernel, bands, tuple(order)),
         "tables",
         (jnp.asarray(geometry_table(bands)), forcing, west, east),
@@ -630,13 +635,13 @@
         [(PAR_ROWS, LANES), (2, WIDE), (2, WIDE)],
         [pltpu.VMEM((8 * bands, LANES), jnp.float32)],
         0.3,
-        flops=4200000000,
+        flops=4300000000,
     )
     relay, par = lax.optimization_barrier((relay, par))
     relayed = lax.ppermute(relay, "band", [(bands - 1, middle + 1), (0, middle)])
     ring = [(s, (s + 1) % spec_count) for s in range(spec_count)]
-    from_west = lax.ppermute(east, "spec", ring)
-    from_east = lax.ppermute(west, "spec", [(t, s) for s, t in ring])
+    first_there = lax.ppermute(first_here, "spec", swapped(ring[1::2]))
+    second_there = lax.ppermute(second_here, "spec", swapped(ring[0::2]))
     base_first, base_last, gain_first, gain_last = call(
         base_kernel,
         "base",
@@ -651,11 +656,13 @@
         [],
         4.0,
     )
-    base_first, from_west, from_east = lax.optimization_barrier((base_first, from_west, from_east))
+    base_first, first_there, second_there = lax.optimization_barrier(
+        (base_first, first_there, second_there)
+    )
     (fix,) = call(
         fix_kernel,
         "fix",
-        (jnp.asarray(speed_table()), par, west, east, from_west, from_east),
+        (jnp.asarray(speed_table()), par, first_here, second_here, first_there, second_there),
         [VMEM] * 6,
         [(WIDE, LANES)],
         [pltpu.VMEM((LANES, WIDE), jnp.float32)],

time: 33.6 us -> 32 us (0.952)
  waiting for transfers between devices: 10.1 us -> 8.31 us
    ppermute x3, waiting for transfers between devices: 2.36 us -> 0.56 us  [the longest x1 0.55 us: per_device(): second_there = lax.ppermute(second_here, 'spec', swapped(ring[0::2]))]
  transfers between devices with their start and end apart: 11 -> 11, of which waited for: 4 -> 4; matrix products, arithmetic and copies ran while one was open for 0% -> 0% of each run, Pallas kernels for 21% -> 22%
where the time goes in v7:
time: 32 us; the launch traced here: 31.7 us
  starting transfers between devices  13.5 us (42%)
  Pallas kernels  9.79 us (31%)
  waiting for transfers between devices  8.31 us (26%)
    pallas_call x8, Pallas kernels, call(): pl.pallas_call(kernel, name=name, out_shape=outs, in_specs=specs, out_spe...  9.79 us
    ppermute x1, waiting for transfers between devices, per_device(): lax.ppermute(part_relayed, 'band', [(middle, bands - 1), (middle + 1, 0)])  6.91 us
    ppermute x3, starting transfers between devices, gathered(): other = lax.ppermute(values, 'band', [(b, b ^ bit) for b in range(bands)])  5.13 us
    ppermute x1, starting transfers between devices, per_device(): first_there = lax.ppermute(first_here, 'spec', swapped(ring[1::2]))  3.67 us
    ppermute x1, starting transfers between devices, per_device(): lax.ppermute(relay, 'band', [(bands - 1, middle + 1), (0, middle)])  1.32 us
    ppermute x1, starting transfers between devices, per_device(): lax.ppermute(part_relayed, 'band', [(middle, bands - 1), (middle + 1, 0)])  1.3 us
    ppermute x1, starting transfers between devices, per_device(): lax.ppermute(cells, 'band', swapped([(b, b + 1) for b in range(1, bands -...  0.87 us
    ppermute x3, waiting for transfers between devices, gathered(): other = lax.ppermute(values, 'band', [(b, b ^ bit) for b in range(bands)])  0.83 us
  transfers between devices with their start and end apart: 11, of which 4 were waited for; matrix products, arithmetic and copies ran while one was open for 0% of the time, Pallas kernels for 22%

profile of v7, /device:TPU:0, one launch (start us, length us, event | category | flops | bytes accessed | tf_op | source)
XLA Modules:
  0.0 31.7 jit_solution(16751964016158663936)
XLA Ops:
  0.0 0.0 copy-start.2
  0.0 0.0 copy-start
  0.0 0.9 %pack_forcing.1.own = f32[16,128]{1,0:T(8,128)S(1)} custom-call(f32[2,16,16]{2,1,0:T(8,128)} %wind.1, f32[2,16,16]{2,1,0:T(8,128)} %current.1, s32[2,128]{1,0:T(2,128)} %sea.2), custom_call_target="tpu_custom_call" | custom-call | bytes 900000 | tf_op jit(solution)/shard_map/pack_forcing/pallas_call | solution.py:543
  1.0 3.0 %collective-permute-start = (f32[16,128]{1,0:T(8,128)S(1)}, f32[16,128]{1,0:T(8,128)S(1)}, u32[]{:S(2)}, u32[]{:S(2)}) collective-permute-start(f32[16,128]{1,0:T(8,128)S(1)} %pack_forcing.1.own), channel_id=1, source_target_pairs={{0,8},{4,12},{8,0},{12,4},{16,24},{20,28},{24,16},{28,20},{1,9},{5... | collective-permute-start | bytes 24584 | tf_op jit(solution)/shard_map/ppermute | solution.py:586
  4.0 0.0 copy-start.3
  4.0 0.9 %collective-permute-start.8 = (f32[2592,128]{1,0:T(8,128)}, f32[2592,128]{1,0:T(8,128)S(1)}, u32[]{:S(2)}, u32[]{:S(2)}) collective-permute-start(f32[2592,128]{1,0:T(8,128)} %bitcast.2), channel_id=1, source_target_pairs={{4,8},{20,24},{8,4},{24,20},{5,9},{21,25},{9,5},{25,21},{6,10},{22... | collective-permute-start | bytes 3981320 | tf_op jit(solution)/shard_map/ppermute | solution.py:601
  4.8 1.3 %split.1 = (f32[1152,128]{1,0:T(8,128)S(1)}, f32[1440,128]{1,0:T(8,128)S(1)}) custom-call(f32[2592,128]{1,0:T(8,128)} %bitcast.3, f32[16,128]{1,0:T(8,128)S(1)} %pack_forcing.1.own), custom_call_target="tpu_custom_call" | custom-call | bytes 3000000 | tf_op jit(solution)/shard_map/split/pallas_call | solution.py:543
  6.2 0.0 collective-permute-done
  6.2 1.6 %collective-permute-start.2 = (f32[32,128]{1,0:T(8,128)S(1)}, f32[32,128]{1,0:T(8,128)S(1)}, u32[]{:S(2)}, u32[]{:S(2)}) collective-permute-start(f32[32,128]{1,0:T(8,128)S(1)} %pad_maximum_fusion.2), channel_id=1, source_target_pairs={{0,16},{4,20},{8,24},{12,28},{16,0},{20,4},{24,8},{28,12},{1,17},{... | collective-permute-start | bytes 49160 | tf_op jit(solution)/shard_map/ppermute | solution.py:586
  7.8 0.0 copy-done.2
  7.8 0.0 copy-done
  7.8 0.4 %ends.1 = (f32[2,2688]{1,0:T(2,128)S(1)}, f32[2,2688]{1,0:T(2,128)S(1)}) custom-call(f32[2592,128]{1,0:T(8,128)S(1)} %bitcast.4, s32[2,128]{1,0:T(2,128)S(1)} %copy-done.2), custom_call_target="tpu_custom_call" | custom-call | bytes 3000000 | tf_op jit(solution)/shard_map/ends/pallas_call | solution.py:543
  8.2 1.3 %collective-permute-start.1 = (f32[1152,128]{1,0:T(8,128)S(1)}, f32[1152,128]{1,0:T(8,128)S(1)}, u32[]{:S(2)}, u32[]{:S(2)}) collective-permute-start(f32[1152,128]{1,0:T(8,128)S(1)} %get-tuple-element.53), channel_id=1, source_target_pairs={{12,28},{16,0},{13,29},{17,1},{14,30},{18,2},{15,31},{19,3}} | collective-permute-start | bytes 1769480 | tf_op jit(solution)/shard_map/ppermute | solution.py:614
  9.5 0.5 %collective-permute-done.2 = f32[32,128]{1,0:T(8,128)S(1)} collective-permute-done((f32[32,128]{1,0:T(8,128)S(1)}, f32[32,128]{1,0:T(8,128)S(1)}, u32[]{:S(2)}, u32[]{:S(2)}) %collective-permute-start.2) | collective-permute-done | bytes 16416 | tf_op jit(solution)/shard_map/ppermute | solution.py:586
  10.0 0.5 %collective-permute-start.3 = (f32[64,128]{1,0:T(8,128)S(1)}, f32[64,128]{1,0:T(8,128)S(1)}, u32[]{:S(2)}, u32[]{:S(2)}) collective-permute-start(f32[64,128]{1,0:T(8,128)S(1)} %pad_maximum_fusion.1), channel_id=1, source_target_pairs={{0,4},{4,0},{8,12},{12,8},{16,20},{20,16},{24,28},{28,24},{1,5},{5... | collective-permute-start | bytes 98312 | tf_op jit(solution)/shard_map/ppermute | solution.py:586
  10.5 0.1 collective-permute-start.4
  10.6 0.4 %collective-permute-start.5 = (f32[1440,128]{1,0:T(8,128)S(1)}, f32[1440,128]{1,0:T(8,128)S(1)}, u32[]{:S(2)}, u32[]{:S(2)}) collective-permute-start(f32[1440,128]{1,0:T(8,128)S(1)} %get-tuple-element.61), channel_id=1, source_target_pairs={{0,4},{8,12},{16,20},{24,28},{4,0},{12,8},{20,16},{28,24},{1,5},{9... | collective-permute-start | bytes 2211848 | tf_op jit(solution)/shard_map/ppermute | solution.py:624
  11.0 0.3 %collective-permute-done.3 = f32[64,128]{1,0:T(8,128)S(1)} collective-permute-done((f32[64,128]{1,0:T(8,128)S(1)}, f32[64,128]{1,0:T(8,128)S(1)}, u32[]{:S(2)}, u32[]{:S(2)}) %collective-permute-start.3) | collective-permute-done | bytes 32800 | tf_op jit(solution)/shard_map/ppermute | solution.py:586
  11.4 0.7 %collective-permute-start.9 = (f32[1440,128]{1,0:T(8,128)S(1)}, f32[1440,128]{1,0:T(8,128)S(1)}, u32[]{:S(2)}, u32[]{:S(2)}) collective-permute-start(f32[1440,128]{1,0:T(8,128)S(1)} %get-tuple-element.61), channel_id=1, source_target_pairs={{12,16},{16,12},{13,17},{17,13},{14,18},{18,14},{15,19},{19,15}} | collective-permute-start | bytes 2211848 | tf_op jit(solution)/shard_map/ppermute | solution.py:626
  12.1 0.0 copy-done.3
  12.1 1.0 %tables.1 = (f32[32,128]{1,0:T(8,128)S(1)}, f32[2,2688]{1,0:T(2,128)S(1)}, f32[2,2688]{1,0:T(2,128)S(1)}) custom-call(f32[8,8]{1,0:T(8,128)S(1)} %copy-done.3, f32[128,128]{1,0:T(8,128)S(1)} %pad_maximum_fusion.slots, f32[2,2688]{1,0:T(2,128)S(1)} %get-tuple-element.49.west_in, f32[2,2688]{1,0:T(2,128)S(1)} %get-tuple-element.50.east_in), custom_call_target="tpu_custom_call" | custom-call | flops 4300000256 | bytes 900000 | tf_op jit(solution)/shard_map/tables/pallas_call | solution.py:543
  13.1 6.9 %collective-permute-done.1 = f32[1152,128]{1,0:T(8,128)S(1)} collective-permute-done((f32[1152,128]{1,0:T(8,128)S(1)}, f32[1152,128]{1,0:T(8,128)S(1)}, u32[]{:S(2)}, u32[]{:S(2)}) %collective-permute-start.1) | collective-permute-done | bytes 589856 | tf_op jit(solution)/shard_map/ppermute | solution.py:614
  20.0 1.3 %collective-permute-start.10 = (f32[1152,128]{1,0:T(8,128)S(1)}, f32[1152,128]{1,0:T(8,128)S(1)}, u32[]{:S(2)}, u32[]{:S(2)}) collective-permute-start(f32[1152,128]{1,0:T(8,128)S(1)} %collective-permute-done.1), channel_id=1, source_target_pairs={{28,16},{0,12},{29,17},{1,13},{30,18},{2,14},{31,19},{3,15}} | collective-permute-start | bytes 1769480 | tf_op jit(solution)/shard_map/ppermute | solution.py:641
  21.3 0.0 collective-permute-done.4.beyond_first
  21.3 3.7 %collective-permute-start.6 = (f32[2,2688]{1,0:T(2,128)S(1)}, f32[2,2688]{1,0:T(2,128)S(1)}, u32[]{:S(2)}, u32[]{:S(2)}) collective-permute-start(f32[2,2688]{1,0:T(2,128)S(1)} %get-tuple-element.56.first_here), channel_id=1, source_target_pairs={{1,2},{3,0},{2,1},{0,3},{5,6},{7,4},{6,5},{4,7},{9,10},{11,8},{10,... | collective-permute-start | bytes 64520 | tf_op jit(solution)/shard_map/ppermute | solution.py:643
  25.0 0.0 collective-permute-done.5.beyond_last
  25.0 0.0 copy-start.1
  25.0 0.0 collective-permute-start.7
  25.0 3.2 %base.1 = (f32[1152,128]{1,0:T(8,128)S(1)}, f32[1440,128]{1,0:T(8,128)S(1)}, f32[1728,128]{1,0:T(8,128)S(1)}, f32[2160,128]{1,0:T(8,128)S(1)}) custom-call(f32[32,128]{1,0:T(8,128)S(1)} %get-tuple-element.52.par, f32[2592,128]{1,0:T(8,128)S(1)} %bitcast.5, f32[1152,128]{1,0:T(8,128)S(1)} %collective-permute-done.4.beyond_first, ...), custom_call_target="tpu_custom_call" | custom-call | bytes 12000000 | tf_op jit(solution)/shard_map/base/pallas_call | solution.py:543
  28.2 0.0 collective-permute-done.6.first_there
  28.2 0.6 %collective-permute-done.7.second_there = f32[2,2688]{1,0:T(2,128)S(1)} collective-permute-done((f32[2,2688]{1,0:T(2,128)S(1)}, f32[2,2688]{1,0:T(2,128)S(1)}, u32[]{:S(2)}, u32[]{:S(2)}) %collective-permute-start.7) | collective-permute-done | bytes 21536 | tf_op jit(solution)/shard_map/ppermute | solution.py:644
  28.8 0.0 copy-done.1
  28.8 0.6 %fix.1 = f32[2688,128]{1,0:T(8,128)S(1)} custom-call(f32[2,2688]{1,0:T(2,128)S(1)} %copy-done.1, f32[32,128]{1,0:T(8,128)S(1)} %get-tuple-element.52.par, f32[2,2688]{1,0:T(2,128)S(1)} %get-tuple-element.56.first_here, f32[2,2688]{1,0:T(2,128)S(1)} %get-tuple-element.57.second_here, f32[2,2688]{1,0:T(2,128)S(1)} %collective-permute-done.6.first_there, ...), custom_call_target="tpu_custom_call" | custom-call | bytes 3000000 | tf_op jit(solution)/shard_map/fix/pallas_call | solution.py:543
  29.3 0.0 collective-permute-done.10.split
  29.4 0.0 collective-permute-done.8.straight
  29.4 0.5 %first_groups.1 = (f32[1152,128]{1,0:T(8,128)S(1)}, f32[16,128]{1,0:T(8,128)S(1)}) custom-call(f32[32,128]{1,0:T(8,128)S(1)} %get-tuple-element.52.par, f32[1152,128]{1,0:T(8,128)S(1)} %get-tuple-element.62.base, f32[1728,128]{1,0:T(8,128)S(1)} %get-tuple-element.63.gain, f32[2688,128]{1,0:T(8,128)S(1)} %fix.1, ...), custom_call_target="tpu_custom_call" | custom-call | bytes 3000000 | tf_op jit(solution)/shard_map/first_groups/pallas_call | solution.py:543
  29.9 0.0 collective-permute-done.9.split
  29.9 1.8 %last_groups.1 = f32[2592,128]{1,0:T(8,128)} custom-call(f32[32,128]{1,0:T(8,128)S(1)} %get-tuple-element.52.par, f32[1440,128]{1,0:T(8,128)S(1)} %get-tuple-element.54.base, f32[2160,128]{1,0:T(8,128)S(1)} %get-tuple-element.55.gain, f32[2688,128]{1,0:T(8,128)S(1)} %fix.1, f32[2592,128]{1,0:T(8,128)S(1)} %collective-permute-done.8.straight, ...), custom_call_target="tpu_custom_call" | custom-call | bytes 6000000 | tf_op jit(solution)/shard_map/last_groups/pallas_call | solution.py:543
  (3 shorter events, 0.0 us)
Async XLA Ops:
  0.0 7.8 %copy-start.2 = (s32[2,128]{1,0:T(2,128)S(1)}, s32[2,128]{1,0:T(2,128)}, u32[]{:S(2)}) copy-start(s32[2,128]{1,0:T(2,128)} %sea.2) | copy-start | bytes 3076
  0.0 7.8 %copy-start = (f32[1296,2,128]{2,1,0:T(2,128)S(1)}, f32[1296,2,128]{2,1,0:T(2,128)}, u32[]{:S(2)}) copy-start(f32[1296,2,128]{2,1,0:T(2,128)} %param.6) | copy-start | bytes 3981316
  1.0 5.2 %collective-permute-start = (f32[16,128]{1,0:T(8,128)S(1)}, f32[16,128]{1,0:T(8,128)S(1)}, u32[]{:S(2)}, u32[]{:S(2)}) collective-permute-start(f32[16,128]{1,0:T(8,128)S(1)} %pack_forcing.1.own), channel_id=1, source_target_pairs={{0,8},{4,12},{8,0},{12,4},{16,24},{20,28},{24,16},{28,20},{1,9},{5... | collective-permute-start | bytes 24584 | tf_op jit(solution)/shard_map/ppermute | solution.py:586
  4.0 8.1 %copy-start.3 = (f32[8,8]{1,0:T(8,128)S(1)}, f32[8,8]{1,0:T(8,128)}, u32[]{:S(2)}) copy-start(f32[8,8]{1,0:T(8,128)} %constant.4.clone.geometry) | copy-start | bytes 772
  4.0 25.4 %collective-permute-start.8 = (f32[2592,128]{1,0:T(8,128)}, f32[2592,128]{1,0:T(8,128)S(1)}, u32[]{:S(2)}, u32[]{:S(2)}) collective-permute-start(f32[2592,128]{1,0:T(8,128)} %bitcast.2), channel_id=1, source_target_pairs={{4,8},{20,24},{8,4},{24,20},{5,9},{21,25},{9,5},{25,21},{6,10},{22... | collective-permute-start | bytes 3981320 | tf_op jit(solution)/shard_map/ppermute | solution.py:601
  6.2 3.8 %collective-permute-start.2 = (f32[32,128]{1,0:T(8,128)S(1)}, f32[32,128]{1,0:T(8,128)S(1)}, u32[]{:S(2)}, u32[]{:S(2)}) collective-permute-start(f32[32,128]{1,0:T(8,128)S(1)} %pad_maximum_fusion.2), channel_id=1, source_target_pairs={{0,16},{4,20},{8,24},{12,28},{16,0},{20,4},{24,8},{28,12},{1,17},{... | collective-permute-start | bytes 49160 | tf_op jit(solution)/shard_map/ppermute | solution.py:586
  8.2 11.8 %collective-permute-start.1 = (f32[1152,128]{1,0:T(8,128)S(1)}, f32[1152,128]{1,0:T(8,128)S(1)}, u32[]{:S(2)}, u32[]{:S(2)}) collective-permute-start(f32[1152,128]{1,0:T(8,128)S(1)} %get-tuple-element.53), channel_id=1, source_target_pairs={{12,28},{16,0},{13,29},{17,1},{14,30},{18,2},{15,31},{19,3}} | collective-permute-start | bytes 1769480 | tf_op jit(solution)/shard_map/ppermute | solution.py:614
  10.0 1.4 %collective-permute-start.3 = (f32[64,128]{1,0:T(8,128)S(1)}, f32[64,128]{1,0:T(8,128)S(1)}, u32[]{:S(2)}, u32[]{:S(2)}) collective-permute-start(f32[64,128]{1,0:T(8,128)S(1)} %pad_maximum_fusion.1), channel_id=1, source_target_pairs={{0,4},{4,0},{8,12},{12,8},{16,20},{20,16},{24,28},{28,24},{1,5},{5... | collective-permute-start | bytes 98312 | tf_op jit(solution)/shard_map/ppermute | solution.py:586
  10.5 10.8 %collective-permute-start.4 = (f32[1152,128]{1,0:T(8,128)S(1)}, f32[1152,128]{1,0:T(8,128)S(1)}, u32[]{:S(2)}, u32[]{:S(2)}) collective-permute-start(f32[1152,128]{1,0:T(8,128)S(1)} %get-tuple-element.53), channel_id=1, source_target_pairs={{0,4},{8,12},{16,20},{24,28},{4,0},{12,8},{20,16},{28,24},{1,5},{9... | collective-permute-start | bytes 1769480 | tf_op jit(solution)/shard_map/ppermute | solution.py:624
  10.6 14.4 %collective-permute-start.5 = (f32[1440,128]{1,0:T(8,128)S(1)}, f32[1440,128]{1,0:T(8,128)S(1)}, u32[]{:S(2)}, u32[]{:S(2)}) collective-permute-start(f32[1440,128]{1,0:T(8,128)S(1)} %get-tuple-element.61), channel_id=1, source_target_pairs={{0,4},{8,12},{16,20},{24,28},{4,0},{12,8},{20,16},{28,24},{1,5},{9... | collective-permute-start | bytes 2211848 | tf_op jit(solution)/shard_map/ppermute | solution.py:624
  11.4 18.5 %collective-permute-start.9 = (f32[1440,128]{1,0:T(8,128)S(1)}, f32[1440,128]{1,0:T(8,128)S(1)}, u32[]{:S(2)}, u32[]{:S(2)}) collective-permute-start(f32[1440,128]{1,0:T(8,128)S(1)} %get-tuple-element.61), channel_id=1, source_target_pairs={{12,16},{16,12},{13,17},{17,13},{14,18},{18,14},{15,19},{19,15}} | collective-permute-start | bytes 2211848 | tf_op jit(solution)/shard_map/ppermute | solution.py:626
  20.0 9.4 %collective-permute-start.10 = (f32[1152,128]{1,0:T(8,128)S(1)}, f32[1152,128]{1,0:T(8,128)S(1)}, u32[]{:S(2)}, u32[]{:S(2)}) collective-permute-start(f32[1152,128]{1,0:T(8,128)S(1)} %collective-permute-done.1), channel_id=1, source_target_pairs={{28,16},{0,12},{29,17},{1,13},{30,18},{2,14},{31,19},{3,15}} | collective-permute-start | bytes 1769480 | tf_op jit(solution)/shard_map/ppermute | solution.py:641
  21.3 6.9 %collective-permute-start.6 = (f32[2,2688]{1,0:T(2,128)S(1)}, f32[2,2688]{1,0:T(2,128)S(1)}, u32[]{:S(2)}, u32[]{:S(2)}) collective-permute-start(f32[2,2688]{1,0:T(2,128)S(1)} %get-tuple-element.56.first_here), channel_id=1, source_target_pairs={{1,2},{3,0},{2,1},{0,3},{5,6},{7,4},{6,5},{4,7},{9,10},{11,8},{10,... | collective-permute-start | bytes 64520 | tf_op jit(solution)/shard_map/ppermute | solution.py:643
  25.0 3.8 %copy-start.1 = (f32[2,2688]{1,0:T(2,128)S(1)}, f32[2,2688]{1,0:T(2,128)}, u32[]{:S(2)}) copy-start(f32[2,2688]{1,0:T(2,128)} %constant.5.clone.table) | copy-start | bytes 64516
  25.0 3.8 %collective-permute-start.7 = (f32[2,2688]{1,0:T(2,128)S(1)}, f32[2,2688]{1,0:T(2,128)S(1)}, u32[]{:S(2)}, u32[]{:S(2)}) collective-permute-start(f32[2,2688]{1,0:T(2,128)S(1)} %get-tuple-element.57.second_here), channel_id=1, source_target_pairs={{0,1},{2,3},{1,0},{3,2},{4,5},{6,7},{5,4},{7,6},{8,9},{10,11},{9,8... | collective-permute-start | bytes 64520 | tf_op jit(solution)/shard_map/ppermute | solution.py:644

commit v8 on v7

--- a/solution.py
+++ b/solution.py
@@ -124,17 +124,11 @@
     out[10:16, :] = jnp.zeros((6, LANES), jnp.float32)
 
 
-def split_kernel(source, own, relayed, direct, sems):
-    del own
-    first = relayed.shape[0]
-    parts = [
-        pltpu.make_async_copy(source.at[0:first], relayed, sems.at[0]),
-        pltpu.make_async_copy(source.at[first:ROWS], direct, sems.at[1]),
-    ]
-    for part in parts:
-        part.start()
-    for part in parts:
-        part.wait()
+def part_kernel(first, source, when, part, sem):
+    del when
+    copy = pltpu.make_async_copy(source.at[first : first + part.shape[0]], part, sem)
+    copy.start()
+    copy.wait()
 
 
 def ends_kernel(spectra, sea, west, east, line):
@@ -280,14 +274,16 @@
     second = jnp.where(c >= 0.0, -c * (1.0 - c * c) * (1.0 / 6.0), 0.0) * (xm1 - y1)
     c = speed + 0.5 * (d2 + dy1)
     before = jnp.where(c >= 0.0, 0.0, -c * (1.0 - c * c) * (1.0 / 6.0)) * (z0 - x0)
-    tall[...] = jnp.zeros((LANES, WIDE), jnp.float32)
-    tall[0:1, :] = first - second
-    tall[1:2, :] = second
-    tall[LANES - 2 : LANES - 1, :] = -before
-    tall[LANES - 1 : LANES, :] = before - last
+    tall[...] = jnp.zeros(tall.shape, jnp.float32)
     for block in range(WIDE // LANES):
         at = block * LANES
-        fix[at : at + LANES, :] = tall[:, at : at + LANES].T
+        piece = slice(at, at + LANES)
+        slot = block % tall.shape[0]
+        tall[slot, 0:1, :] = first[:, piece] - second[:, piece]
+        tall[slot, 1:2, :] = second[:, piece]
+        tall[slot, LANES - 2 : LANES - 1, :] = -before[:, piece]
+        tall[slot, LANES - 1 : LANES, :] = before[:, piece] - last[:, piece]
+        fix[piece, :] = tall[slot].T
 
 
 def base_kernel(par, spectra, beyond_first, beyond_last, base_first, base_last, gain_first, gain_last):
@@ -588,15 +584,19 @@
 
     forcing = gathered(own, 2)
 
-    part_relayed, part_direct = call(
-        split_kernel,
-        "split",
-        (pltpu.with_memory_space_constraint(cells, pltpu.HBM), own),
-        [HBM, VMEM],
-        [(first_rows, LANES), (last_rows, LANES)],
-        [pltpu.SemaphoreType.DMA((2,))],
-        1.0,
-    )
+    def part_of(first, rows, name, when):
+        (part,) = call(
+            functools.partial(part_kernel, first),
+            name,
+            (pltpu.with_memory_space_constraint(cells, pltpu.HBM), when),
+            [HBM, VMEM],
+            [(rows, LANES)],
+            [pltpu.SemaphoreType.DMA],
+            1.0,
+        )
+        return part
+
+    part_relayed = part_of(0, first_rows, "part_relayed", own)
     part_relayed, forcing, ends_sea = lax.optimization_barrier((part_relayed, forcing, sea_mask))
     straight = lax.ppermute(
         cells, "band", swapped([(b, b + 1) for b in range(1, bands - 1, 2) if b != middle])
@@ -616,6 +616,7 @@
     while bit < bands:
         forcing = gathered(forcing, bit)
         bit *= 2
+    part_direct = part_of(first_rows, last_rows, "part_direct", west)
     part_relayed, part_direct, forcing, west, east = lax.optimization_barrier(
         (part_relayed, part_direct, forcing, west, east)
     )
@@ -665,7 +666,7 @@
         (jnp.asarray(speed_table()), par, first_here, second_here, first_there, second_there),
         [VMEM] * 6,
         [(WIDE, LANES)],
-        [pltpu.VMEM((LANES, WIDE), jnp.float32)],
+        [pltpu.VMEM((4, LANES, LANES), jnp.float32)],
         1.0,
     )
     turned, total = call(

time: 32 us -> 32.1 us (level)
  waiting for transfers between devices: 8.31 us -> 6.79 us
  Pallas kernels: 9.79 us -> 10.7 us
  starting transfers between devices: 13.5 us -> 14.1 us
    ppermute x1, waiting for transfers between devices: 6.91 us -> 5.88 us  [per_device(): lax.ppermute(part_relayed, 'band', [(middle, bands - 1), (middle + 1, 0)])]
    pallas_call x8 -> x9, Pallas kernels: 9.79 us -> 10.7 us  [call(): pl.pallas_call(kernel, name=name, out_shape=outs, in_specs=specs, out_spe...]
    ppermute x3, waiting for transfers between devices: 0.83 us -> 0.35 us  [gathered(): other = lax.ppermute(values, 'band', [(b, b ^ bit) for b in range(bands)])]
    ppermute x3, starting transfers between devices: 5.13 us -> 5.6 us  [gathered(): other = lax.ppermute(values, 'band', [(b, b ^ bit) for b in range(bands)])]
  transfers between devices with their start and end apart: 11 -> 11, of which waited for: 4 -> 3; matrix products, arithmetic and copies ran while one was open for 0% -> 0% of each run, Pallas kernels for 22% -> 25%
where the time goes in v8:
time: 32.1 us; the launch traced here: 31.8 us
  starting transfers between devices  14.1 us (44%)
  Pallas kernels  10.7 us (33%)
  waiting for transfers between devices  6.79 us (21%)
    pallas_call x9, Pallas kernels, call(): pl.pallas_call(kernel, name=name, out_shape=outs, in_specs=specs, out_spe...  10.7 us
    ppermute x1, waiting for transfers between devices, per_device(): lax.ppermute(part_relayed, 'band', [(middle, bands - 1), (middle + 1, 0)])  5.88 us
    ppermute x3, starting transfers between devices, gathered(): other = lax.ppermute(values, 'band', [(b, b ^ bit) for b in range(bands)])  5.6 us
    ppermute x1, starting transfers between devices, per_device(): first_there = lax.ppermute(first_here, 'spec', swapped(ring[1::2]))  3.67 us
    ppermute x1, starting transfers between devices, per_device(): lax.ppermute(part_relayed, 'band', [(middle, bands - 1), (middle + 1, 0)])  1.42 us
    ppermute x1, starting transfers between devices, per_device(): lax.ppermute(relay, 'band', [(bands - 1, middle + 1), (0, middle)])  1.32 us
    ppermute x1, starting transfers between devices, per_device(): lax.ppermute(part_direct, 'band', [(middle, middle + 1), (middle + 1, mid...  0.83 us
    ppermute x1, starting transfers between devices, per_device(): lax.ppermute(cells, 'band', swapped([(b, b + 1) for b in range(1, bands -...  0.73 us
  transfers between devices with their start and end apart: 11, of which 3 were waited for; matrix products, arithmetic and copies ran while one was open for 0% of the time, Pallas kernels for 25%

profile of v8, /device:TPU:0, one launch (start us, length us, event | category | flops | bytes accessed | tf_op | source)
XLA Modules:
  0.0 31.8 jit_solution(17825071324627259287)
XLA Ops:
  0.0 0.0 copy-start.3
  0.0 0.0 copy-start
  0.0 0.9 %pack_forcing.1.when = f32[16,128]{1,0:T(8,128)S(1)} custom-call(f32[2,16,16]{2,1,0:T(8,128)} %wind.1, f32[2,16,16]{2,1,0:T(8,128)} %current.1, s32[2,128]{1,0:T(2,128)} %sea.2), custom_call_target="tpu_custom_call" | custom-call | bytes 900000 | tf_op jit(solution)/shard_map/pack_forcing/pallas_call | solution.py:539
  1.0 3.0 %collective-permute-start = (f32[16,128]{1,0:T(8,128)S(1)}, f32[16,128]{1,0:T(8,128)S(1)}, u32[]{:S(2)}, u32[]{:S(2)}) collective-permute-start(f32[16,128]{1,0:T(8,128)S(1)} %pack_forcing.1.when), channel_id=1, source_target_pairs={{0,8},{4,12},{8,0},{12,4},{16,24},{20,28},{24,16},{28,20},{1,9},{5... | collective-permute-start | bytes 24584 | tf_op jit(solution)/shard_map/ppermute | solution.py:582
  4.0 0.7 %collective-permute-start.8 = (f32[2592,128]{1,0:T(8,128)}, f32[2592,128]{1,0:T(8,128)S(1)}, u32[]{:S(2)}, u32[]{:S(2)}) collective-permute-start(f32[2592,128]{1,0:T(8,128)} %bitcast.2), channel_id=1, source_target_pairs={{4,8},{20,24},{8,4},{24,20},{5,9},{21,25},{9,5},{25,21},{6,10},{22... | collective-permute-start | bytes 3981320 | tf_op jit(solution)/shard_map/ppermute | solution.py:601
  4.7 1.1 %part_relayed.1 = f32[1152,128]{1,0:T(8,128)S(1)} custom-call(f32[2592,128]{1,0:T(8,128)} %bitcast.3, f32[16,128]{1,0:T(8,128)S(1)} %pack_forcing.1.when), custom_call_target="tpu_custom_call" | custom-call | bytes 3000000 | tf_op jit(solution)/shard_map/part_relayed/pallas_call | solution.py:539
  5.8 0.0 collective-permute-done
  5.8 1.8 %collective-permute-start.2 = (f32[32,128]{1,0:T(8,128)S(1)}, f32[32,128]{1,0:T(8,128)S(1)}, u32[]{:S(2)}, u32[]{:S(2)}) collective-permute-start(f32[32,128]{1,0:T(8,128)S(1)} %pad_maximum_fusion.2), channel_id=1, source_target_pairs={{0,16},{4,20},{8,24},{12,28},{16,0},{20,4},{24,8},{28,12},{1,17},{... | collective-permute-start | bytes 49160 | tf_op jit(solution)/shard_map/ppermute | solution.py:582
  7.6 0.0 copy-done.3
  7.6 0.0 copy-done
  7.6 0.4 %ends.1 = (f32[2,2688]{1,0:T(2,128)S(1)}, f32[2,2688]{1,0:T(2,128)S(1)}) custom-call(f32[2592,128]{1,0:T(8,128)S(1)} %bitcast.5, s32[2,128]{1,0:T(2,128)S(1)} %copy-done.3), custom_call_target="tpu_custom_call" | custom-call | bytes 3000000 | tf_op jit(solution)/shard_map/ends/pallas_call | solution.py:539
  8.1 0.0 copy-start.4
  8.1 1.4 %collective-permute-start.1 = (f32[1152,128]{1,0:T(8,128)S(1)}, f32[1152,128]{1,0:T(8,128)S(1)}, u32[]{:S(2)}, u32[]{:S(2)}) collective-permute-start(f32[1152,128]{1,0:T(8,128)S(1)} %part_relayed.1), channel_id=1, source_target_pairs={{12,28},{16,0},{13,29},{17,1},{14,30},{18,2},{15,31},{19,3}} | collective-permute-start | bytes 1769480 | tf_op jit(solution)/shard_map/ppermute | solution.py:614
  9.5 1.1 %part_direct.1 = f32[1440,128]{1,0:T(8,128)S(1)} custom-call(f32[2592,128]{1,0:T(8,128)} %bitcast.4, f32[2,2688]{1,0:T(2,128)S(1)} %get-tuple-element.45.when.west_in), custom_call_target="tpu_custom_call" | custom-call | bytes 3000000 | tf_op jit(solution)/shard_map/part_direct/pallas_call | solution.py:539
  10.7 0.0 collective-permute-done.2
  10.7 0.8 %collective-permute-start.3 = (f32[64,128]{1,0:T(8,128)S(1)}, f32[64,128]{1,0:T(8,128)S(1)}, u32[]{:S(2)}, u32[]{:S(2)}) collective-permute-start(f32[64,128]{1,0:T(8,128)S(1)} %pad_maximum_fusion.1), channel_id=1, source_target_pairs={{0,4},{4,0},{8,12},{12,8},{16,20},{20,16},{24,28},{28,24},{1,5},{5... | collective-permute-start | bytes 98312 | tf_op jit(solution)/shard_map/ppermute | solution.py:582
  11.4 0.1 collective-permute-start.4
  11.5 0.4 %collective-permute-start.5 = (f32[1440,128]{1,0:T(8,128)S(1)}, f32[1440,128]{1,0:T(8,128)S(1)}, u32[]{:S(2)}, u32[]{:S(2)}) collective-permute-start(f32[1440,128]{1,0:T(8,128)S(1)} %part_direct.1), channel_id=1, source_target_pairs={{0,4},{8,12},{16,20},{24,28},{4,0},{12,8},{20,16},{28,24},{1,5},{9... | collective-permute-start | bytes 2211848 | tf_op jit(solution)/shard_map/ppermute | solution.py:625
  12.0 0.3 %collective-permute-done.3 = f32[64,128]{1,0:T(8,128)S(1)} collective-permute-done((f32[64,128]{1,0:T(8,128)S(1)}, f32[64,128]{1,0:T(8,128)S(1)}, u32[]{:S(2)}, u32[]{:S(2)}) %collective-permute-start.3) | collective-permute-done | bytes 32800 | tf_op jit(solution)/shard_map/ppermute | solution.py:582
  12.3 0.0 copy-start.1
  12.3 0.8 %collective-permute-start.9 = (f32[1440,128]{1,0:T(8,128)S(1)}, f32[1440,128]{1,0:T(8,128)S(1)}, u32[]{:S(2)}, u32[]{:S(2)}) collective-permute-start(f32[1440,128]{1,0:T(8,128)S(1)} %part_direct.1), channel_id=1, source_target_pairs={{12,16},{16,12},{13,17},{17,13},{14,18},{18,14},{15,19},{19,15}} | collective-permute-start | bytes 2211848 | tf_op jit(solution)/shard_map/ppermute | solution.py:627
  13.1 0.0 copy-done.4
  13.2 1.0 %tables.1 = (f32[32,128]{1,0:T(8,128)S(1)}, f32[2,2688]{1,0:T(2,128)S(1)}, f32[2,2688]{1,0:T(2,128)S(1)}) custom-call(f32[8,8]{1,0:T(8,128)S(1)} %copy-done.4, f32[128,128]{1,0:T(8,128)S(1)} %pad_maximum_fusion.slots, f32[2,2688]{1,0:T(2,128)S(1)} %get-tuple-element.45.when.west_in, f32[2,2688]{1,0:T(2,128)S(1)} %get-tuple-element.46.east_in), custom_call_target="tpu_custom_call" | custom-call | flops 4300000256 | bytes 900000 | tf_op jit(solution)/shard_map/tables/pallas_call | solution.py:539
  14.1 5.9 %collective-permute-done.1 = f32[1152,128]{1,0:T(8,128)S(1)} collective-permute-done((f32[1152,128]{1,0:T(8,128)S(1)}, f32[1152,128]{1,0:T(8,128)S(1)}, u32[]{:S(2)}, u32[]{:S(2)}) %collective-permute-start.1) | collective-permute-done | bytes 589856 | tf_op jit(solution)/shard_map/ppermute | solution.py:614
  20.0 1.3 %collective-permute-start.10 = (f32[1152,128]{1,0:T(8,128)S(1)}, f32[1152,128]{1,0:T(8,128)S(1)}, u32[]{:S(2)}, u32[]{:S(2)}) collective-permute-start(f32[1152,128]{1,0:T(8,128)S(1)} %collective-permute-done.1), channel_id=1, source_target_pairs={{28,16},{0,12},{29,17},{1,13},{30,18},{2,14},{31,19},{3,15}} | collective-permute-start | bytes 1769480 | tf_op jit(solution)/shard_map/ppermute | solution.py:642
  21.3 0.0 collective-permute-done.4.beyond_first
  21.3 3.7 %collective-permute-start.6 = (f32[2,2688]{1,0:T(2,128)S(1)}, f32[2,2688]{1,0:T(2,128)S(1)}, u32[]{:S(2)}, u32[]{:S(2)}) collective-permute-start(f32[2,2688]{1,0:T(2,128)S(1)} %get-tuple-element.52.first_here), channel_id=1, source_target_pairs={{1,2},{3,0},{2,1},{0,3},{5,6},{7,4},{6,5},{4,7},{9,10},{11,8},{10,... | collective-permute-start | bytes 64520 | tf_op jit(solution)/shard_map/ppermute | solution.py:644
  25.0 0.0 collective-permute-done.5.beyond_last
  25.0 0.0 copy-start.2
  25.0 0.0 collective-permute-start.7
  25.0 0.0 copy-done.1
  25.0 3.2 %base.1 = (f32[1152,128]{1,0:T(8,128)S(1)}, f32[1440,128]{1,0:T(8,128)S(1)}, f32[1728,128]{1,0:T(8,128)S(1)}, f32[2160,128]{1,0:T(8,128)S(1)}) custom-call(f32[32,128]{1,0:T(8,128)S(1)} %get-tuple-element.48.par, f32[2592,128]{1,0:T(8,128)S(1)} %bitcast.6, f32[1152,128]{1,0:T(8,128)S(1)} %collective-permute-done.4.beyond_first, ...), custom_call_target="tpu_custom_call" | custom-call | bytes 12000000 | tf_op jit(solution)/shard_map/base/pallas_call | solution.py:539
  28.2 0.0 collective-permute-done.6.first_there
  28.3 0.5 %collective-permute-done.7.second_there = f32[2,2688]{1,0:T(2,128)S(1)} collective-permute-done((f32[2,2688]{1,0:T(2,128)S(1)}, f32[2,2688]{1,0:T(2,128)S(1)}, u32[]{:S(2)}, u32[]{:S(2)}) %collective-permute-start.7) | collective-permute-done | bytes 21536 | tf_op jit(solution)/shard_map/ppermute | solution.py:645
  28.8 0.0 copy-done.2
  28.8 0.6 %fix.1 = f32[2688,128]{1,0:T(8,128)S(1)} custom-call(f32[2,2688]{1,0:T(2,128)S(1)} %copy-done.2, f32[32,128]{1,0:T(8,128)S(1)} %get-tuple-element.48.par, f32[2,2688]{1,0:T(2,128)S(1)} %get-tuple-element.52.first_here, f32[2,2688]{1,0:T(2,128)S(1)} %get-tuple-element.53.second_here, f32[2,2688]{1,0:T(2,128)S(1)} %collective-permute-done.6.first_there, ...), custom_call_target="tpu_custom_call" | custom-call | bytes 3000000 | tf_op jit(solution)/shard_map/fix/pallas_call | solution.py:539
  29.4 0.0 collective-permute-done.10.split
  29.4 0.0 collective-permute-done.8.straight
  29.4 0.5 %first_groups.1 = (f32[1152,128]{1,0:T(8,128)S(1)}, f32[16,128]{1,0:T(8,128)S(1)}) custom-call(f32[32,128]{1,0:T(8,128)S(1)} %get-tuple-element.48.par, f32[1152,128]{1,0:T(8,128)S(1)} %get-tuple-element.58.base, f32[1728,128]{1,0:T(8,128)S(1)} %get-tuple-element.59.gain, f32[2688,128]{1,0:T(8,128)S(1)} %fix.1, ...), custom_call_target="tpu_custom_call" | custom-call | bytes 3000000 | tf_op jit(solution)/shard_map/first_groups/pallas_call | solution.py:539
  29.9 0.0 collective-permute-done.9.split
  29.9 1.8 %last_groups.1 = f32[2592,128]{1,0:T(8,128)} custom-call(f32[32,128]{1,0:T(8,128)S(1)} %get-tuple-element.48.par, f32[1440,128]{1,0:T(8,128)S(1)} %get-tuple-element.50.base, f32[2160,128]{1,0:T(8,128)S(1)} %get-tuple-element.51.gain, f32[2688,128]{1,0:T(8,128)S(1)} %fix.1, f32[2592,128]{1,0:T(8,128)S(1)} %collective-permute-done.8.straight, ...), custom_call_target="tpu_custom_call" | custom-call | bytes 6000000 | tf_op jit(solution)/shard_map/last_groups/pallas_call | solution.py:539
  (3 shorter events, 0.0 us)
Async XLA Ops:
  0.0 7.6 %copy-start.3 = (s32[2,128]{1,0:T(2,128)S(1)}, s32[2,128]{1,0:T(2,128)}, u32[]{:S(2)}) copy-start(s32[2,128]{1,0:T(2,128)} %sea.2) | copy-start | bytes 3076
  0.0 7.6 %copy-start = (f32[1296,2,128]{2,1,0:T(2,128)S(1)}, f32[1296,2,128]{2,1,0:T(2,128)}, u32[]{:S(2)}) copy-start(f32[1296,2,128]{2,1,0:T(2,128)} %param.6) | copy-start | bytes 3981316
  1.0 4.8 %collective-permute-start = (f32[16,128]{1,0:T(8,128)S(1)}, f32[16,128]{1,0:T(8,128)S(1)}, u32[]{:S(2)}, u32[]{:S(2)}) collective-permute-start(f32[16,128]{1,0:T(8,128)S(1)} %pack_forcing.1.when), channel_id=1, source_target_pairs={{0,8},{4,12},{8,0},{12,4},{16,24},{20,28},{24,16},{28,20},{1,9},{5... | collective-permute-start | bytes 24584 | tf_op jit(solution)/shard_map/ppermute | solution.py:582
  4.0 25.4 %collective-permute-start.8 = (f32[2592,128]{1,0:T(8,128)}, f32[2592,128]{1,0:T(8,128)S(1)}, u32[]{:S(2)}, u32[]{:S(2)}) collective-permute-start(f32[2592,128]{1,0:T(8,128)} %bitcast.2), channel_id=1, source_target_pairs={{4,8},{20,24},{8,4},{24,20},{5,9},{21,25},{9,5},{25,21},{6,10},{22... | collective-permute-start | bytes 3981320 | tf_op jit(solution)/shard_map/ppermute | solution.py:601
  5.8 4.9 %collective-permute-start.2 = (f32[32,128]{1,0:T(8,128)S(1)}, f32[32,128]{1,0:T(8,128)S(1)}, u32[]{:S(2)}, u32[]{:S(2)}) collective-permute-start(f32[32,128]{1,0:T(8,128)S(1)} %pad_maximum_fusion.2), channel_id=1, source_target_pairs={{0,16},{4,20},{8,24},{12,28},{16,0},{20,4},{24,8},{28,12},{1,17},{... | collective-permute-start | bytes 49160 | tf_op jit(solution)/shard_map/ppermute | solution.py:582
  8.1 5.1 %copy-start.4 = (f32[8,8]{1,0:T(8,128)S(1)}, f32[8,8]{1,0:T(8,128)}, u32[]{:S(2)}) copy-start(f32[8,8]{1,0:T(8,128)} %constant.4.clone.geometry) | copy-start | bytes 772
  8.1 11.9 %collective-permute-start.1 = (f32[1152,128]{1,0:T(8,128)S(1)}, f32[1152,128]{1,0:T(8,128)S(1)}, u32[]{:S(2)}, u32[]{:S(2)}) collective-permute-start(f32[1152,128]{1,0:T(8,128)S(1)} %part_relayed.1), channel_id=1, source_target_pairs={{12,28},{16,0},{13,29},{17,1},{14,30},{18,2},{15,31},{19,3}} | collective-permute-start | bytes 1769480 | tf_op jit(solution)/shard_map/ppermute | solution.py:614
  10.7 1.6 %collective-permute-start.3 = (f32[64,128]{1,0:T(8,128)S(1)}, f32[64,128]{1,0:T(8,128)S(1)}, u32[]{:S(2)}, u32[]{:S(2)}) collective-permute-start(f32[64,128]{1,0:T(8,128)S(1)} %pad_maximum_fusion.1), channel_id=1, source_target_pairs={{0,4},{4,0},{8,12},{12,8},{16,20},{20,16},{24,28},{28,24},{1,5},{5... | collective-permute-start | bytes 98312 | tf_op jit(solution)/shard_map/ppermute | solution.py:582
  11.4 9.9 %collective-permute-start.4 = (f32[1152,128]{1,0:T(8,128)S(1)}, f32[1152,128]{1,0:T(8,128)S(1)}, u32[]{:S(2)}, u32[]{:S(2)}) collective-permute-start(f32[1152,128]{1,0:T(8,128)S(1)} %part_relayed.1), channel_id=1, source_target_pairs={{0,4},{8,12},{16,20},{24,28},{4,0},{12,8},{20,16},{28,24},{1,5},{9... | collective-permute-start | bytes 1769480 | tf_op jit(solution)/shard_map/ppermute | solution.py:625
  11.5 13.5 %collective-permute-start.5 = (f32[1440,128]{1,0:T(8,128)S(1)}, f32[1440,128]{1,0:T(8,128)S(1)}, u32[]{:S(2)}, u32[]{:S(2)}) collective-permute-start(f32[1440,128]{1,0:T(8,128)S(1)} %part_direct.1), channel_id=1, source_target_pairs={{0,4},{8,12},{16,20},{24,28},{4,0},{12,8},{20,16},{28,24},{1,5},{9... | collective-permute-start | bytes 2211848 | tf_op jit(solution)/shard_map/ppermute | solution.py:625
  12.3 12.7 %copy-start.1 = (f32[1296,2,128]{2,1,0:T(2,128)S(1)}, f32[1296,2,128]{2,1,0:T(2,128)}, u32[]{:S(2)}) copy-start(f32[1296,2,128]{2,1,0:T(2,128)} %param.6) | copy-start | bytes 3981316
  12.3 17.6 %collective-permute-start.9 = (f32[1440,128]{1,0:T(8,128)S(1)}, f32[1440,128]{1,0:T(8,128)S(1)}, u32[]{:S(2)}, u32[]{:S(2)}) collective-permute-start(f32[1440,128]{1,0:T(8,128)S(1)} %part_direct.1), channel_id=1, source_target_pairs={{12,16},{16,12},{13,17},{17,13},{14,18},{18,14},{15,19},{19,15}} | collective-permute-start | bytes 2211848 | tf_op jit(solution)/shard_map/ppermute | solution.py:627
  20.0 9.4 %collective-permute-start.10 = (f32[1152,128]{1,0:T(8,128)S(1)}, f32[1152,128]{1,0:T(8,128)S(1)}, u32[]{:S(2)}, u32[]{:S(2)}) collective-permute-start(f32[1152,128]{1,0:T(8,128)S(1)} %collective-permute-done.1), channel_id=1, source_target_pairs={{28,16},{0,12},{29,17},{1,13},{30,18},{2,14},{31,19},{3,15}} | collective-permute-start | bytes 1769480 | tf_op jit(solution)/shard_map/ppermute | solution.py:642
  21.3 6.9 %collective-permute-start.6 = (f32[2,2688]{1,0:T(2,128)S(1)}, f32[2,2688]{1,0:T(2,128)S(1)}, u32[]{:S(2)}, u32[]{:S(2)}) collective-permute-start(f32[2,2688]{1,0:T(2,128)S(1)} %get-tuple-element.52.first_here), channel_id=1, source_target_pairs={{1,2},{3,0},{2,1},{0,3},{5,6},{7,4},{6,5},{4,7},{9,10},{11,8},{10,... | collective-permute-start | bytes 64520 | tf_op jit(solution)/shard_map/ppermute | solution.py:644
  25.0 3.8 %copy-start.2 = (f32[2,2688]{1,0:T(2,128)S(1)}, f32[2,2688]{1,0:T(2,128)}, u32[]{:S(2)}) copy-start(f32[2,2688]{1,0:T(2,128)} %constant.5.clone.table) | copy-start | bytes 64516
  25.0 3.8 %collective-permute-start.7 = (f32[2,2688]{1,0:T(2,128)S(1)}, f32[2,2688]{1,0:T(2,128)S(1)}, u32[]{:S(2)}, u32[]{:S(2)}) collective-permute-start(f32[2,2688]{1,0:T(2,128)S(1)} %get-tuple-element.53.second_here), channel_id=1, source_target_pairs={{0,1},{2,3},{1,0},{3,2},{4,5},{6,7},{5,4},{7,6},{8,9},{10,11},{9,8... | collective-permute-start | bytes 64520 | tf_op jit(solution)/shard_map/ppermute | solution.py:645

commit v9 on v7

--- a/solution.py
+++ b/solution.py
@@ -247,16 +247,16 @@
             values = jnp.where(lane == ROWS + i, pair, values)
         ends.append(values)
     even_spec = lax.rem(lax.axis_index("spec"), 2) == 0
-    first[...] = jnp.where(even_spec, ends[0], ends[1])
-    second[...] = jnp.where(even_spec, ends[1], ends[0])
+    first[...] = jnp.where(even_spec, ends[1], ends[0])
+    second[...] = jnp.where(even_spec, ends[0], ends[1])
 
 
 def fix_kernel(table, par, first_here, second_here, first_there, second_there, fix, tall):
     even_spec = lax.rem(lax.axis_index("spec"), 2) == 0
-    west = jnp.where(even_spec, first_here[...], second_here[...])
-    east = jnp.where(even_spec, second_here[...], first_here[...])
-    from_west = jnp.where(even_spec, first_there[...], second_there[...])
-    from_east = jnp.where(even_spec, second_there[...], first_there[...])
+    west = jnp.where(even_spec, second_here[...], first_here[...])
+    east = jnp.where(even_spec, first_here[...], second_here[...])
+    from_west = jnp.where(even_spec, second_there[...], first_there[...])
+    from_east = jnp.where(even_spec, first_there[...], second_there[...])
     lane = lax.broadcasted_iota(jnp.int32, (1, WIDE), 1)
     even_row = lax.rem(lane, 2) == 0
     speed = table[0:1] * par[ICOS_0 : ICOS_0 + 1, 0:1] + table[1:2] * par[ICOS_1 : ICOS_1 + 1, 0:1]
@@ -640,8 +640,8 @@
     relay, par = lax.optimization_barrier((relay, par))
     relayed = lax.ppermute(relay, "band", [(bands - 1, middle + 1), (0, middle)])
     ring = [(s, (s + 1) % spec_count) for s in range(spec_count)]
-    first_there = lax.ppermute(first_here, "spec", swapped(ring[1::2]))
-    second_there = lax.ppermute(second_here, "spec", swapped(ring[0::2]))
+    first_there = lax.ppermute(first_here, "spec", swapped(ring[0::2]))
+    second_there = lax.ppermute(second_here, "spec", swapped(ring[1::2]))
     base_first, base_last, gain_first, gain_last = call(
         base_kernel,
         "base",

time: 32 us -> 31.9 us (level)
  waiting for transfers between devices: 8.31 us -> 7.76 us
  starting transfers between devices: 13.5 us -> 13.9 us
    ppermute x2, waiting for transfers between devices: 0.56 us -> 0.01 us  [the longest x1 0.01 us: per_device(): second_there = lax.ppermute(second_here, 'spec', swapped(ring[1::2]))]
    ppermute x2, starting transfers between devices: 3.67 us -> 4.12 us  [the longest x1 2.48 us: per_device(): second_there = lax.ppermute(second_here, 'spec', swapped(ring[1::2]))]
  transfers between devices with their start and end apart: 11 -> 11, of which waited for: 4 -> 3; matrix products, arithmetic and copies ran while one was open for 0% -> 0% of each run, Pallas kernels for 22% -> 22%
where the time goes in v9:
time: 31.9 us; the launch traced here: 31.7 us
  starting transfers between devices  13.9 us (44%)
  Pallas kernels  9.78 us (31%)
  waiting for transfers between devices  7.76 us (24%)
    pallas_call x8, Pallas kernels, call(): pl.pallas_call(kernel, name=name, out_shape=outs, in_specs=specs, out_spe...  9.78 us
    ppermute x1, waiting for transfers between devices, per_device(): lax.ppermute(part_relayed, 'band', [(middle, bands - 1), (middle + 1, 0)])  6.91 us
    ppermute x3, starting transfers between devices, gathered(): other = lax.ppermute(values, 'band', [(b, b ^ bit) for b in range(bands)])  5.13 us
    ppermute x1, starting transfers between devices, per_device(): second_there = lax.ppermute(second_here, 'spec', swapped(ring[1::2]))  2.48 us
    ppermute x1, starting transfers between devices, per_device(): first_there = lax.ppermute(first_here, 'spec', swapped(ring[0::2]))  1.64 us
    ppermute x1, starting transfers between devices, per_device(): lax.ppermute(relay, 'band', [(bands - 1, middle + 1), (0, middle)])  1.32 us
    ppermute x1, starting transfers between devices, per_device(): lax.ppermute(part_relayed, 'band', [(middle, bands - 1), (middle + 1, 0)])  1.3 us
    ppermute x1, starting transfers between devices, per_device(): lax.ppermute(cells, 'band', swapped([(b, b + 1) for b in range(1, bands -...  0.87 us
  transfers between devices with their start and end apart: 11, of which 3 were waited for; matrix products, arithmetic and copies ran while one was open for 0% of the time, Pallas kernels for 22%

profile of v9, /device:TPU:0, one launch (start us, length us, event | category | flops | bytes accessed | tf_op | source)
XLA Modules:
  0.0 31.7 jit_solution(16940730700121425953)
XLA Ops:
  0.0 0.0 copy-start.2
  0.0 0.0 copy-start
  0.0 0.9 %pack_forcing.1.own = f32[16,128]{1,0:T(8,128)S(1)} custom-call(f32[2,16,16]{2,1,0:T(8,128)} %wind.1, f32[2,16,16]{2,1,0:T(8,128)} %current.1, s32[2,128]{1,0:T(2,128)} %sea.2), custom_call_target="tpu_custom_call" | custom-call | bytes 900000 | tf_op jit(solution)/shard_map/pack_forcing/pallas_call | solution.py:543
  1.0 3.0 %collective-permute-start = (f32[16,128]{1,0:T(8,128)S(1)}, f32[16,128]{1,0:T(8,128)S(1)}, u32[]{:S(2)}, u32[]{:S(2)}) collective-permute-start(f32[16,128]{1,0:T(8,128)S(1)} %pack_forcing.1.own), channel_id=1, source_target_pairs={{0,8},{4,12},{8,0},{12,4},{16,24},{20,28},{24,16},{28,20},{1,9},{5... | collective-permute-start | bytes 24584 | tf_op jit(solution)/shard_map/ppermute | solution.py:586
  4.0 0.0 copy-start.3
  4.0 0.9 %collective-permute-start.8 = (f32[2592,128]{1,0:T(8,128)}, f32[2592,128]{1,0:T(8,128)S(1)}, u32[]{:S(2)}, u32[]{:S(2)}) collective-permute-start(f32[2592,128]{1,0:T(8,128)} %bitcast.2), channel_id=1, source_target_pairs={{4,8},{20,24},{8,4},{24,20},{5,9},{21,25},{9,5},{25,21},{6,10},{22... | collective-permute-start | bytes 3981320 | tf_op jit(solution)/shard_map/ppermute | solution.py:601
  4.8 1.3 %split.1 = (f32[1152,128]{1,0:T(8,128)S(1)}, f32[1440,128]{1,0:T(8,128)S(1)}) custom-call(f32[2592,128]{1,0:T(8,128)} %bitcast.3, f32[16,128]{1,0:T(8,128)S(1)} %pack_forcing.1.own), custom_call_target="tpu_custom_call" | custom-call | bytes 3000000 | tf_op jit(solution)/shard_map/split/pallas_call | solution.py:543
  6.2 0.0 collective-permute-done
  6.2 1.6 %collective-permute-start.2 = (f32[32,128]{1,0:T(8,128)S(1)}, f32[32,128]{1,0:T(8,128)S(1)}, u32[]{:S(2)}, u32[]{:S(2)}) collective-permute-start(f32[32,128]{1,0:T(8,128)S(1)} %pad_maximum_fusion.2), channel_id=1, source_target_pairs={{0,16},{4,20},{8,24},{12,28},{16,0},{20,4},{24,8},{28,12},{1,17},{... | collective-permute-start | bytes 49160 | tf_op jit(solution)/shard_map/ppermute | solution.py:586
  7.8 0.0 copy-done.2
  7.8 0.0 copy-done
  7.8 0.4 %ends.1 = (f32[2,2688]{1,0:T(2,128)S(1)}, f32[2,2688]{1,0:T(2,128)S(1)}) custom-call(f32[2592,128]{1,0:T(8,128)S(1)} %bitcast.4, s32[2,128]{1,0:T(2,128)S(1)} %copy-done.2), custom_call_target="tpu_custom_call" | custom-call | bytes 3000000 | tf_op jit(solution)/shard_map/ends/pallas_call | solution.py:543
  8.2 1.3 %collective-permute-start.1 = (f32[1152,128]{1,0:T(8,128)S(1)}, f32[1152,128]{1,0:T(8,128)S(1)}, u32[]{:S(2)}, u32[]{:S(2)}) collective-permute-start(f32[1152,128]{1,0:T(8,128)S(1)} %get-tuple-element.53), channel_id=1, source_target_pairs={{12,28},{16,0},{13,29},{17,1},{14,30},{18,2},{15,31},{19,3}} | collective-permute-start | bytes 1769480 | tf_op jit(solution)/shard_map/ppermute | solution.py:614
  9.5 0.5 %collective-permute-done.2 = f32[32,128]{1,0:T(8,128)S(1)} collective-permute-done((f32[32,128]{1,0:T(8,128)S(1)}, f32[32,128]{1,0:T(8,128)S(1)}, u32[]{:S(2)}, u32[]{:S(2)}) %collective-permute-start.2) | collective-permute-done | bytes 16416 | tf_op jit(solution)/shard_map/ppermute | solution.py:586
  10.0 0.5 %collective-permute-start.3 = (f32[64,128]{1,0:T(8,128)S(1)}, f32[64,128]{1,0:T(8,128)S(1)}, u32[]{:S(2)}, u32[]{:S(2)}) collective-permute-start(f32[64,128]{1,0:T(8,128)S(1)} %pad_maximum_fusion.1), channel_id=1, source_target_pairs={{0,4},{4,0},{8,12},{12,8},{16,20},{20,16},{24,28},{28,24},{1,5},{5... | collective-permute-start | bytes 98312 | tf_op jit(solution)/shard_map/ppermute | solution.py:586
  10.5 0.1 collective-permute-start.4
  10.6 0.4 %collective-permute-start.5 = (f32[1440,128]{1,0:T(8,128)S(1)}, f32[1440,128]{1,0:T(8,128)S(1)}, u32[]{:S(2)}, u32[]{:S(2)}) collective-permute-start(f32[1440,128]{1,0:T(8,128)S(1)} %get-tuple-element.61), channel_id=1, source_target_pairs={{0,4},{8,12},{16,20},{24,28},{4,0},{12,8},{20,16},{28,24},{1,5},{9... | collective-permute-start | bytes 2211848 | tf_op jit(solution)/shard_map/ppermute | solution.py:624
  11.0 0.3 %collective-permute-done.3 = f32[64,128]{1,0:T(8,128)S(1)} collective-permute-done((f32[64,128]{1,0:T(8,128)S(1)}, f32[64,128]{1,0:T(8,128)S(1)}, u32[]{:S(2)}, u32[]{:S(2)}) %collective-permute-start.3) | collective-permute-done | bytes 32800 | tf_op jit(solution)/shard_map/ppermute | solution.py:586
  11.4 0.7 %collective-permute-start.9 = (f32[1440,128]{1,0:T(8,128)S(1)}, f32[1440,128]{1,0:T(8,128)S(1)}, u32[]{:S(2)}, u32[]{:S(2)}) collective-permute-start(f32[1440,128]{1,0:T(8,128)S(1)} %get-tuple-element.61), channel_id=1, source_target_pairs={{12,16},{16,12},{13,17},{17,13},{14,18},{18,14},{15,19},{19,15}} | collective-permute-start | bytes 2211848 | tf_op jit(solution)/shard_map/ppermute | solution.py:626
  12.1 0.0 copy-done.3
  12.1 1.0 %tables.1 = (f32[32,128]{1,0:T(8,128)S(1)}, f32[2,2688]{1,0:T(2,128)S(1)}, f32[2,2688]{1,0:T(2,128)S(1)}) custom-call(f32[8,8]{1,0:T(8,128)S(1)} %copy-done.3, f32[128,128]{1,0:T(8,128)S(1)} %pad_maximum_fusion.slots, f32[2,2688]{1,0:T(2,128)S(1)} %get-tuple-element.49.west_in, f32[2,2688]{1,0:T(2,128)S(1)} %get-tuple-element.50.east_in), custom_call_target="tpu_custom_call" | custom-call | flops 4300000256 | bytes 900000 | tf_op jit(solution)/shard_map/tables/pallas_call | solution.py:543
  13.1 6.9 %collective-permute-done.1 = f32[1152,128]{1,0:T(8,128)S(1)} collective-permute-done((f32[1152,128]{1,0:T(8,128)S(1)}, f32[1152,128]{1,0:T(8,128)S(1)}, u32[]{:S(2)}, u32[]{:S(2)}) %collective-permute-start.1) | collective-permute-done | bytes 589856 | tf_op jit(solution)/shard_map/ppermute | solution.py:614
  20.0 1.3 %collective-permute-start.10 = (f32[1152,128]{1,0:T(8,128)S(1)}, f32[1152,128]{1,0:T(8,128)S(1)}, u32[]{:S(2)}, u32[]{:S(2)}) collective-permute-start(f32[1152,128]{1,0:T(8,128)S(1)} %collective-permute-done.1), channel_id=1, source_target_pairs={{28,16},{0,12},{29,17},{1,13},{30,18},{2,14},{31,19},{3,15}} | collective-permute-start | bytes 1769480 | tf_op jit(solution)/shard_map/ppermute | solution.py:641
  21.3 0.0 collective-permute-done.4.beyond_first
  21.3 1.6 %collective-permute-start.6 = (f32[2,2688]{1,0:T(2,128)S(1)}, f32[2,2688]{1,0:T(2,128)S(1)}, u32[]{:S(2)}, u32[]{:S(2)}) collective-permute-start(f32[2,2688]{1,0:T(2,128)S(1)} %get-tuple-element.56.first_here), channel_id=1, source_target_pairs={{0,1},{2,3},{1,0},{3,2},{4,5},{6,7},{5,4},{7,6},{8,9},{10,11},{9,8... | collective-permute-start | bytes 64520 | tf_op jit(solution)/shard_map/ppermute | solution.py:643
  23.0 0.0 collective-permute-done.5.beyond_last
  23.0 0.0 copy-start.1
  23.0 2.5 %collective-permute-start.7 = (f32[2,2688]{1,0:T(2,128)S(1)}, f32[2,2688]{1,0:T(2,128)S(1)}, u32[]{:S(2)}, u32[]{:S(2)}) collective-permute-start(f32[2,2688]{1,0:T(2,128)S(1)} %get-tuple-element.57.second_here), channel_id=1, source_target_pairs={{1,2},{3,0},{2,1},{0,3},{5,6},{7,4},{6,5},{4,7},{9,10},{11,8},{10,... | collective-permute-start | bytes 64520 | tf_op jit(solution)/shard_map/ppermute | solution.py:644
  25.4 3.2 %base.1 = (f32[1152,128]{1,0:T(8,128)S(1)}, f32[1440,128]{1,0:T(8,128)S(1)}, f32[1728,128]{1,0:T(8,128)S(1)}, f32[2160,128]{1,0:T(8,128)S(1)}) custom-call(f32[32,128]{1,0:T(8,128)S(1)} %get-tuple-element.52.par, f32[2592,128]{1,0:T(8,128)S(1)} %bitcast.5, f32[1152,128]{1,0:T(8,128)S(1)} %collective-permute-done.4.beyond_first, ...), custom_call_target="tpu_custom_call" | custom-call | bytes 12000000 | tf_op jit(solution)/shard_map/base/pallas_call | solution.py:543
  28.7 0.0 collective-permute-done.6.first_there
  28.7 0.0 collective-permute-done.7.second_there
  28.7 0.0 copy-done.1
  28.7 0.6 %fix.1 = f32[2688,128]{1,0:T(8,128)S(1)} custom-call(f32[2,2688]{1,0:T(2,128)S(1)} %copy-done.1, f32[32,128]{1,0:T(8,128)S(1)} %get-tuple-element.52.par, f32[2,2688]{1,0:T(2,128)S(1)} %get-tuple-element.56.first_here, f32[2,2688]{1,0:T(2,128)S(1)} %get-tuple-element.57.second_here, f32[2,2688]{1,0:T(2,128)S(1)} %collective-permute-done.6.first_there, ...), custom_call_target="tpu_custom_call" | custom-call | bytes 3000000 | tf_op jit(solution)/shard_map/fix/pallas_call | solution.py:543
  29.3 0.0 collective-permute-done.10.split
  29.3 0.0 collective-permute-done.8.straight
  29.3 0.5 %first_groups.1 = (f32[1152,128]{1,0:T(8,128)S(1)}, f32[16,128]{1,0:T(8,128)S(1)}) custom-call(f32[32,128]{1,0:T(8,128)S(1)} %get-tuple-element.52.par, f32[1152,128]{1,0:T(8,128)S(1)} %get-tuple-element.62.base, f32[1728,128]{1,0:T(8,128)S(1)} %get-tuple-element.63.gain, f32[2688,128]{1,0:T(8,128)S(1)} %fix.1, ...), custom_call_target="tpu_custom_call" | custom-call | bytes 3000000 | tf_op jit(solution)/shard_map/first_groups/pallas_call | solution.py:543
  29.8 0.0 collective-permute-done.9.split
  29.8 1.8 %last_groups.1 = f32[2592,128]{1,0:T(8,128)} custom-call(f32[32,128]{1,0:T(8,128)S(1)} %get-tuple-element.52.par, f32[1440,128]{1,0:T(8,128)S(1)} %get-tuple-element.54.base, f32[2160,128]{1,0:T(8,128)S(1)} %get-tuple-element.55.gain, f32[2688,128]{1,0:T(8,128)S(1)} %fix.1, f32[2592,128]{1,0:T(8,128)S(1)} %collective-permute-done.8.straight, ...), custom_call_target="tpu_custom_call" | custom-call | bytes 6000000 | tf_op jit(solution)/shard_map/last_groups/pallas_call | solution.py:543
  (3 shorter events, 0.0 us)
Async XLA Ops:
  0.0 7.8 %copy-start.2 = (s32[2,128]{1,0:T(2,128)S(1)}, s32[2,128]{1,0:T(2,128)}, u32[]{:S(2)}) copy-start(s32[2,128]{1,0:T(2,128)} %sea.2) | copy-start | bytes 3076
  0.0 7.8 %copy-start = (f32[1296,2,128]{2,1,0:T(2,128)S(1)}, f32[1296,2,128]{2,1,0:T(2,128)}, u32[]{:S(2)}) copy-start(f32[1296,2,128]{2,1,0:T(2,128)} %param.6) | copy-start | bytes 3981316
  1.0 5.2 %collective-permute-start = (f32[16,128]{1,0:T(8,128)S(1)}, f32[16,128]{1,0:T(8,128)S(1)}, u32[]{:S(2)}, u32[]{:S(2)}) collective-permute-start(f32[16,128]{1,0:T(8,128)S(1)} %pack_forcing.1.own), channel_id=1, source_target_pairs={{0,8},{4,12},{8,0},{12,4},{16,24},{20,28},{24,16},{28,20},{1,9},{5... | collective-permute-start | bytes 24584 | tf_op jit(solution)/shard_map/ppermute | solution.py:586
  4.0 8.1 %copy-start.3 = (f32[8,8]{1,0:T(8,128)S(1)}, f32[8,8]{1,0:T(8,128)}, u32[]{:S(2)}) copy-start(f32[8,8]{1,0:T(8,128)} %constant.4.clone.geometry) | copy-start | bytes 772
  4.0 25.3 %collective-permute-start.8 = (f32[2592,128]{1,0:T(8,128)}, f32[2592,128]{1,0:T(8,128)S(1)}, u32[]{:S(2)}, u32[]{:S(2)}) collective-permute-start(f32[2592,128]{1,0:T(8,128)} %bitcast.2), channel_id=1, source_target_pairs={{4,8},{20,24},{8,4},{24,20},{5,9},{21,25},{9,5},{25,21},{6,10},{22... | collective-permute-start | bytes 3981320 | tf_op jit(solution)/shard_map/ppermute | solution.py:601
  6.2 3.8 %collective-permute-start.2 = (f32[32,128]{1,0:T(8,128)S(1)}, f32[32,128]{1,0:T(8,128)S(1)}, u32[]{:S(2)}, u32[]{:S(2)}) collective-permute-start(f32[32,128]{1,0:T(8,128)S(1)} %pad_maximum_fusion.2), channel_id=1, source_target_pairs={{0,16},{4,20},{8,24},{12,28},{16,0},{20,4},{24,8},{28,12},{1,17},{... | collective-permute-start | bytes 49160 | tf_op jit(solution)/shard_map/ppermute | solution.py:586
  8.2 11.8 %collective-permute-start.1 = (f32[1152,128]{1,0:T(8,128)S(1)}, f32[1152,128]{1,0:T(8,128)S(1)}, u32[]{:S(2)}, u32[]{:S(2)}) collective-permute-start(f32[1152,128]{1,0:T(8,128)S(1)} %get-tuple-element.53), channel_id=1, source_target_pairs={{12,28},{16,0},{13,29},{17,1},{14,30},{18,2},{15,31},{19,3}} | collective-permute-start | bytes 1769480 | tf_op jit(solution)/shard_map/ppermute | solution.py:614
  10.0 1.4 %collective-permute-start.3 = (f32[64,128]{1,0:T(8,128)S(1)}, f32[64,128]{1,0:T(8,128)S(1)}, u32[]{:S(2)}, u32[]{:S(2)}) collective-permute-start(f32[64,128]{1,0:T(8,128)S(1)} %pad_maximum_fusion.1), channel_id=1, source_target_pairs={{0,4},{4,0},{8,12},{12,8},{16,20},{20,16},{24,28},{28,24},{1,5},{5... | collective-permute-start | bytes 98312 | tf_op jit(solution)/shard_map/ppermute | solution.py:586
  10.5 10.8 %collective-permute-start.4 = (f32[1152,128]{1,0:T(8,128)S(1)}, f32[1152,128]{1,0:T(8,128)S(1)}, u32[]{:S(2)}, u32[]{:S(2)}) collective-permute-start(f32[1152,128]{1,0:T(8,128)S(1)} %get-tuple-element.53), channel_id=1, source_target_pairs={{0,4},{8,12},{16,20},{24,28},{4,0},{12,8},{20,16},{28,24},{1,5},{9... | collective-permute-start | bytes 1769480 | tf_op jit(solution)/shard_map/ppermute | solution.py:624
  10.6 12.3 %collective-permute-start.5 = (f32[1440,128]{1,0:T(8,128)S(1)}, f32[1440,128]{1,0:T(8,128)S(1)}, u32[]{:S(2)}, u32[]{:S(2)}) collective-permute-start(f32[1440,128]{1,0:T(8,128)S(1)} %get-tuple-element.61), channel_id=1, source_target_pairs={{0,4},{8,12},{16,20},{24,28},{4,0},{12,8},{20,16},{28,24},{1,5},{9... | collective-permute-start | bytes 2211848 | tf_op jit(solution)/shard_map/ppermute | solution.py:624
  11.4 18.4 %collective-permute-start.9 = (f32[1440,128]{1,0:T(8,128)S(1)}, f32[1440,128]{1,0:T(8,128)S(1)}, u32[]{:S(2)}, u32[]{:S(2)}) collective-permute-start(f32[1440,128]{1,0:T(8,128)S(1)} %get-tuple-element.61), channel_id=1, source_target_pairs={{12,16},{16,12},{13,17},{17,13},{14,18},{18,14},{15,19},{19,15}} | collective-permute-start | bytes 2211848 | tf_op jit(solution)/shard_map/ppermute | solution.py:626
  20.0 9.3 %collective-permute-start.10 = (f32[1152,128]{1,0:T(8,128)S(1)}, f32[1152,128]{1,0:T(8,128)S(1)}, u32[]{:S(2)}, u32[]{:S(2)}) collective-permute-start(f32[1152,128]{1,0:T(8,128)S(1)} %collective-permute-done.1), channel_id=1, source_target_pairs={{28,16},{0,12},{29,17},{1,13},{30,18},{2,14},{31,19},{3,15}} | collective-permute-start | bytes 1769480 | tf_op jit(solution)/shard_map/ppermute | solution.py:641
  21.3 7.3 %collective-permute-start.6 = (f32[2,2688]{1,0:T(2,128)S(1)}, f32[2,2688]{1,0:T(2,128)S(1)}, u32[]{:S(2)}, u32[]{:S(2)}) collective-permute-start(f32[2,2688]{1,0:T(2,128)S(1)} %get-tuple-element.56.first_here), channel_id=1, source_target_pairs={{0,1},{2,3},{1,0},{3,2},{4,5},{6,7},{5,4},{7,6},{8,9},{10,11},{9,8... | collective-permute-start | bytes 64520 | tf_op jit(solution)/shard_map/ppermute | solution.py:643
  23.0 5.7 %copy-start.1 = (f32[2,2688]{1,0:T(2,128)S(1)}, f32[2,2688]{1,0:T(2,128)}, u32[]{:S(2)}) copy-start(f32[2,2688]{1,0:T(2,128)} %constant.5.clone.table) | copy-start | bytes 64516
  23.0 5.7 %collective-permute-start.7 = (f32[2,2688]{1,0:T(2,128)S(1)}, f32[2,2688]{1,0:T(2,128)S(1)}, u32[]{:S(2)}, u32[]{:S(2)}) collective-permute-start(f32[2,2688]{1,0:T(2,128)S(1)} %get-tuple-element.57.second_here), channel_id=1, source_target_pairs={{1,2},{3,0},{2,1},{0,3},{5,6},{7,4},{6,5},{4,7},{9,10},{11,8},{10,... | collective-permute-start | bytes 64520 | tf_op jit(solution)/shard_map/ppermute | solution.py:644

commit v10 on v7

--- a/solution.py
+++ b/solution.py
@@ -622,7 +622,6 @@
     pairs = [(b, b + 1) for b in range(0, bands, 2)]
     forcing = gathered(forcing, 1)
     beyond = [lax.ppermute(part, "band", swapped(pairs)) for part in (part_relayed, part_direct)]
-    part_direct, forcing = lax.optimization_barrier((part_direct, forcing))
     direct = lax.ppermute(
         part_direct, "band", [(middle, middle + 1), (middle + 1, middle)]
     )

time: 32 us -> 32 us (level)
  no operation moved by 1% of the time
where the time goes in v10:
time: 32 us; the launch traced here: 31.7 us
  starting transfers between devices  13.5 us (42%)
  Pallas kernels  9.79 us (31%)
  waiting for transfers between devices  8.31 us (26%)
    pallas_call x8, Pallas kernels, call(): pl.pallas_call(kernel, name=name, out_shape=outs, in_specs=specs, out_spe...  9.79 us
    ppermute x1, waiting for transfers between devices, per_device(): lax.ppermute(part_relayed, 'band', [(middle, bands - 1), (middle + 1, 0)])  7.19 us
    ppermute x3, starting transfers between devices, gathered(): other = lax.ppermute(values, 'band', [(b, b ^ bit) for b in range(bands)])  5.13 us
    ppermute x1, starting transfers between devices, per_device(): first_there = lax.ppermute(first_here, 'spec', swapped(ring[1::2]))  3.67 us
    ppermute x1, starting transfers between devices, per_device(): lax.ppermute(relay, 'band', [(bands - 1, middle + 1), (0, middle)])  1.32 us
    ppermute x1, starting transfers between devices, per_device(): lax.ppermute(part_relayed, 'band', [(middle, bands - 1), (middle + 1, 0)])  1.3 us
    ppermute x1, starting transfers between devices, per_device(): lax.ppermute(cells, 'band', swapped([(b, b + 1) for b in range(1, bands -...  0.87 us
    ppermute x1, starting transfers between devices, per_device(): lax.ppermute(part_direct, 'band', [(middle, middle + 1), (middle + 1, mid...  0.7 us
  transfers between devices with their start and end apart: 11, of which 4 were waited for; matrix products, arithmetic and copies ran while one was open for 0% of the time, Pallas kernels for 22%

profile of v10, /device:TPU:0, one launch (start us, length us, event | category | flops | bytes accessed | tf_op | source)
XLA Modules:
  0.0 31.7 jit_solution(2988479591725707412)
XLA Ops:
  0.0 0.0 copy-start.2
  0.0 0.0 copy-start
  0.0 0.9 %pack_forcing.1.own = f32[16,128]{1,0:T(8,128)S(1)} custom-call(f32[2,16,16]{2,1,0:T(8,128)} %wind.1, f32[2,16,16]{2,1,0:T(8,128)} %current.1, s32[2,128]{1,0:T(2,128)} %sea.2), custom_call_target="tpu_custom_call" | custom-call | bytes 900000 | tf_op jit(solution)/shard_map/pack_forcing/pallas_call | solution.py:543
  1.0 3.0 %collective-permute-start = (f32[16,128]{1,0:T(8,128)S(1)}, f32[16,128]{1,0:T(8,128)S(1)}, u32[]{:S(2)}, u32[]{:S(2)}) collective-permute-start(f32[16,128]{1,0:T(8,128)S(1)} %pack_forcing.1.own), channel_id=1, source_target_pairs={{0,8},{4,12},{8,0},{12,4},{16,24},{20,28},{24,16},{28,20},{1,9},{5... | collective-permute-start | bytes 24584 | tf_op jit(solution)/shard_map/ppermute | solution.py:586
  4.0 0.0 copy-start.3
  4.0 0.9 %collective-permute-start.8 = (f32[2592,128]{1,0:T(8,128)}, f32[2592,128]{1,0:T(8,128)S(1)}, u32[]{:S(2)}, u32[]{:S(2)}) collective-permute-start(f32[2592,128]{1,0:T(8,128)} %bitcast.2), channel_id=1, source_target_pairs={{4,8},{20,24},{8,4},{24,20},{5,9},{21,25},{9,5},{25,21},{6,10},{22... | collective-permute-start | bytes 3981320 | tf_op jit(solution)/shard_map/ppermute | solution.py:601
  4.8 1.3 %split.1 = (f32[1152,128]{1,0:T(8,128)S(1)}, f32[1440,128]{1,0:T(8,128)S(1)}) custom-call(f32[2592,128]{1,0:T(8,128)} %bitcast.3, f32[16,128]{1,0:T(8,128)S(1)} %pack_forcing.1.own), custom_call_target="tpu_custom_call" | custom-call | bytes 3000000 | tf_op jit(solution)/shard_map/split/pallas_call | solution.py:543
  6.2 0.0 collective-permute-done
  6.2 1.6 %collective-permute-start.2 = (f32[32,128]{1,0:T(8,128)S(1)}, f32[32,128]{1,0:T(8,128)S(1)}, u32[]{:S(2)}, u32[]{:S(2)}) collective-permute-start(f32[32,128]{1,0:T(8,128)S(1)} %pad_maximum_fusion.2), channel_id=1, source_target_pairs={{0,16},{4,20},{8,24},{12,28},{16,0},{20,4},{24,8},{28,12},{1,17},{... | collective-permute-start | bytes 49160 | tf_op jit(solution)/shard_map/ppermute | solution.py:586
  7.8 0.0 copy-done.2
  7.8 0.0 copy-done
  7.8 0.4 %ends.1 = (f32[2,2688]{1,0:T(2,128)S(1)}, f32[2,2688]{1,0:T(2,128)S(1)}) custom-call(f32[2592,128]{1,0:T(8,128)S(1)} %bitcast.4, s32[2,128]{1,0:T(2,128)S(1)} %copy-done.2), custom_call_target="tpu_custom_call" | custom-call | bytes 3000000 | tf_op jit(solution)/shard_map/ends/pallas_call | solution.py:543
  8.2 1.3 %collective-permute-start.1 = (f32[1152,128]{1,0:T(8,128)S(1)}, f32[1152,128]{1,0:T(8,128)S(1)}, u32[]{:S(2)}, u32[]{:S(2)}) collective-permute-start(f32[1152,128]{1,0:T(8,128)S(1)} %get-tuple-element.49), channel_id=1, source_target_pairs={{12,28},{16,0},{13,29},{17,1},{14,30},{18,2},{15,31},{19,3}} | collective-permute-start | bytes 1769480 | tf_op jit(solution)/shard_map/ppermute | solution.py:614
  9.5 0.5 %collective-permute-done.2 = f32[32,128]{1,0:T(8,128)S(1)} collective-permute-done((f32[32,128]{1,0:T(8,128)S(1)}, f32[32,128]{1,0:T(8,128)S(1)}, u32[]{:S(2)}, u32[]{:S(2)}) %collective-permute-start.2) | collective-permute-done | bytes 16416 | tf_op jit(solution)/shard_map/ppermute | solution.py:586
  10.0 0.5 %collective-permute-start.3 = (f32[64,128]{1,0:T(8,128)S(1)}, f32[64,128]{1,0:T(8,128)S(1)}, u32[]{:S(2)}, u32[]{:S(2)}) collective-permute-start(f32[64,128]{1,0:T(8,128)S(1)} %pad_maximum_fusion.1), channel_id=1, source_target_pairs={{0,4},{4,0},{8,12},{12,8},{16,20},{20,16},{24,28},{28,24},{1,5},{5... | collective-permute-start | bytes 98312 | tf_op jit(solution)/shard_map/ppermute | solution.py:586
  10.5 0.7 %collective-permute-start.9 = (f32[1440,128]{1,0:T(8,128)S(1)}, f32[1440,128]{1,0:T(8,128)S(1)}, u32[]{:S(2)}, u32[]{:S(2)}) collective-permute-start(f32[1440,128]{1,0:T(8,128)S(1)} %get-tuple-element.50), channel_id=1, source_target_pairs={{12,16},{16,12},{13,17},{17,13},{14,18},{18,14},{15,19},{19,15}} | collective-permute-start | bytes 2211848 | tf_op jit(solution)/shard_map/ppermute | solution.py:625
  11.2 0.1 collective-permute-start.5
  11.3 0.1 collective-permute-done.3
  11.4 0.4 %collective-permute-start.4 = (f32[1152,128]{1,0:T(8,128)S(1)}, f32[1152,128]{1,0:T(8,128)S(1)}, u32[]{:S(2)}, u32[]{:S(2)}) collective-permute-start(f32[1152,128]{1,0:T(8,128)S(1)} %get-tuple-element.49), channel_id=1, source_target_pairs={{0,4},{8,12},{16,20},{24,28},{4,0},{12,8},{20,16},{28,24},{1,5},{9... | collective-permute-start | bytes 1769480 | tf_op jit(solution)/shard_map/ppermute | solution.py:624
  11.8 0.0 copy-done.3
  11.8 1.0 %tables.1 = (f32[32,128]{1,0:T(8,128)S(1)}, f32[2,2688]{1,0:T(2,128)S(1)}, f32[2,2688]{1,0:T(2,128)S(1)}) custom-call(f32[8,8]{1,0:T(8,128)S(1)} %copy-done.3, f32[128,128]{1,0:T(8,128)S(1)} %pad_maximum_fusion.slots, f32[2,2688]{1,0:T(2,128)S(1)} %get-tuple-element.45.west_in, f32[2,2688]{1,0:T(2,128)S(1)} %get-tuple-element.46.east_in), custom_call_target="tpu_custom_call" | custom-call | flops 4300000256 | bytes 900000 | tf_op jit(solution)/shard_map/tables/pallas_call | solution.py:543
  12.8 7.2 %collective-permute-done.1 = f32[1152,128]{1,0:T(8,128)S(1)} collective-permute-done((f32[1152,128]{1,0:T(8,128)S(1)}, f32[1152,128]{1,0:T(8,128)S(1)}, u32[]{:S(2)}, u32[]{:S(2)}) %collective-permute-start.1) | collective-permute-done | bytes 589856 | tf_op jit(solution)/shard_map/ppermute | solution.py:614
  20.0 1.3 %collective-permute-start.10 = (f32[1152,128]{1,0:T(8,128)S(1)}, f32[1152,128]{1,0:T(8,128)S(1)}, u32[]{:S(2)}, u32[]{:S(2)}) collective-permute-start(f32[1152,128]{1,0:T(8,128)S(1)} %collective-permute-done.1), channel_id=1, source_target_pairs={{28,16},{0,12},{29,17},{1,13},{30,18},{2,14},{31,19},{3,15}} | collective-permute-start | bytes 1769480 | tf_op jit(solution)/shard_map/ppermute | solution.py:640
  21.3 0.0 collective-permute-done.4.beyond_first
  21.3 3.7 %collective-permute-start.6 = (f32[2,2688]{1,0:T(2,128)S(1)}, f32[2,2688]{1,0:T(2,128)S(1)}, u32[]{:S(2)}, u32[]{:S(2)}) collective-permute-start(f32[2,2688]{1,0:T(2,128)S(1)} %get-tuple-element.53.first_here), channel_id=1, source_target_pairs={{1,2},{3,0},{2,1},{0,3},{5,6},{7,4},{6,5},{4,7},{9,10},{11,8},{10,... | collective-permute-start | bytes 64520 | tf_op jit(solution)/shard_map/ppermute | solution.py:642
  25.0 0.0 collective-permute-done.5.beyond_last
  25.0 0.0 copy-start.1
  25.0 0.0 collective-permute-start.7
  25.0 3.2 %base.1 = (f32[1152,128]{1,0:T(8,128)S(1)}, f32[1440,128]{1,0:T(8,128)S(1)}, f32[1728,128]{1,0:T(8,128)S(1)}, f32[2160,128]{1,0:T(8,128)S(1)}) custom-call(f32[32,128]{1,0:T(8,128)S(1)} %get-tuple-element.48.par, f32[2592,128]{1,0:T(8,128)S(1)} %bitcast.5, f32[1152,128]{1,0:T(8,128)S(1)} %collective-permute-done.4.beyond_first, ...), custom_call_target="tpu_custom_call" | custom-call | bytes 12000000 | tf_op jit(solution)/shard_map/base/pallas_call | solution.py:543
  28.2 0.0 collective-permute-done.6.first_there
  28.2 0.6 %collective-permute-done.7.second_there = f32[2,2688]{1,0:T(2,128)S(1)} collective-permute-done((f32[2,2688]{1,0:T(2,128)S(1)}, f32[2,2688]{1,0:T(2,128)S(1)}, u32[]{:S(2)}, u32[]{:S(2)}) %collective-permute-start.7) | collective-permute-done | bytes 21536 | tf_op jit(solution)/shard_map/ppermute | solution.py:643
  28.8 0.0 copy-done.1
  28.8 0.6 %fix.1 = f32[2688,128]{1,0:T(8,128)S(1)} custom-call(f32[2,2688]{1,0:T(2,128)S(1)} %copy-done.1, f32[32,128]{1,0:T(8,128)S(1)} %get-tuple-element.48.par, f32[2,2688]{1,0:T(2,128)S(1)} %get-tuple-element.53.first_here, f32[2,2688]{1,0:T(2,128)S(1)} %get-tuple-element.54.second_here, f32[2,2688]{1,0:T(2,128)S(1)} %collective-permute-done.6.first_there, ...), custom_call_target="tpu_custom_call" | custom-call | bytes 3000000 | tf_op jit(solution)/shard_map/fix/pallas_call | solution.py:543
  29.3 0.0 collective-permute-done.10.split
  29.4 0.0 collective-permute-done.8.straight
  29.4 0.5 %first_groups.1 = (f32[1152,128]{1,0:T(8,128)S(1)}, f32[16,128]{1,0:T(8,128)S(1)}) custom-call(f32[32,128]{1,0:T(8,128)S(1)} %get-tuple-element.48.par, f32[1152,128]{1,0:T(8,128)S(1)} %get-tuple-element.58.base, f32[1728,128]{1,0:T(8,128)S(1)} %get-tuple-element.59.gain, f32[2688,128]{1,0:T(8,128)S(1)} %fix.1, ...), custom_call_target="tpu_custom_call" | custom-call | bytes 3000000 | tf_op jit(solution)/shard_map/first_groups/pallas_call | solution.py:543
  29.9 0.0 collective-permute-done.9.split
  29.9 1.8 %last_groups.1 = f32[2592,128]{1,0:T(8,128)} custom-call(f32[32,128]{1,0:T(8,128)S(1)} %get-tuple-element.48.par, f32[1440,128]{1,0:T(8,128)S(1)} %get-tuple-element.51.base, f32[2160,128]{1,0:T(8,128)S(1)} %get-tuple-element.52.gain, f32[2688,128]{1,0:T(8,128)S(1)} %fix.1, f32[2592,128]{1,0:T(8,128)S(1)} %collective-permute-done.8.straight, ...), custom_call_target="tpu_custom_call" | custom-call | bytes 6000000 | tf_op jit(solution)/shard_map/last_groups/pallas_call | solution.py:543
  (3 shorter events, 0.0 us)
Async XLA Ops:
  0.0 7.8 %copy-start.2 = (s32[2,128]{1,0:T(2,128)S(1)}, s32[2,128]{1,0:T(2,128)}, u32[]{:S(2)}) copy-start(s32[2,128]{1,0:T(2,128)} %sea.2) | copy-start | bytes 3076
  0.0 7.8 %copy-start = (f32[1296,2,128]{2,1,0:T(2,128)S(1)}, f32[1296,2,128]{2,1,0:T(2,128)}, u32[]{:S(2)}) copy-start(f32[1296,2,128]{2,1,0:T(2,128)} %param.6) | copy-start | bytes 3981316
  1.0 5.2 %collective-permute-start = (f32[16,128]{1,0:T(8,128)S(1)}, f32[16,128]{1,0:T(8,128)S(1)}, u32[]{:S(2)}, u32[]{:S(2)}) collective-permute-start(f32[16,128]{1,0:T(8,128)S(1)} %pack_forcing.1.own), channel_id=1, source_target_pairs={{0,8},{4,12},{8,0},{12,4},{16,24},{20,28},{24,16},{28,20},{1,9},{5... | collective-permute-start | bytes 24584 | tf_op jit(solution)/shard_map/ppermute | solution.py:586
  4.0 7.9 %copy-start.3 = (f32[8,8]{1,0:T(8,128)S(1)}, f32[8,8]{1,0:T(8,128)}, u32[]{:S(2)}) copy-start(f32[8,8]{1,0:T(8,128)} %constant.4.clone.geometry) | copy-start | bytes 772
  4.0 25.4 %collective-permute-start.8 = (f32[2592,128]{1,0:T(8,128)}, f32[2592,128]{1,0:T(8,128)S(1)}, u32[]{:S(2)}, u32[]{:S(2)}) collective-permute-start(f32[2592,128]{1,0:T(8,128)} %bitcast.2), channel_id=1, source_target_pairs={{4,8},{20,24},{8,4},{24,20},{5,9},{21,25},{9,5},{25,21},{6,10},{22... | collective-permute-start | bytes 3981320 | tf_op jit(solution)/shard_map/ppermute | solution.py:601
  6.2 3.8 %collective-permute-start.2 = (f32[32,128]{1,0:T(8,128)S(1)}, f32[32,128]{1,0:T(8,128)S(1)}, u32[]{:S(2)}, u32[]{:S(2)}) collective-permute-start(f32[32,128]{1,0:T(8,128)S(1)} %pad_maximum_fusion.2), channel_id=1, source_target_pairs={{0,16},{4,20},{8,24},{12,28},{16,0},{20,4},{24,8},{28,12},{1,17},{... | collective-permute-start | bytes 49160 | tf_op jit(solution)/shard_map/ppermute | solution.py:586
  8.2 11.8 %collective-permute-start.1 = (f32[1152,128]{1,0:T(8,128)S(1)}, f32[1152,128]{1,0:T(8,128)S(1)}, u32[]{:S(2)}, u32[]{:S(2)}) collective-permute-start(f32[1152,128]{1,0:T(8,128)S(1)} %get-tuple-element.49), channel_id=1, source_target_pairs={{12,28},{16,0},{13,29},{17,1},{14,30},{18,2},{15,31},{19,3}} | collective-permute-start | bytes 1769480 | tf_op jit(solution)/shard_map/ppermute | solution.py:614
  10.0 1.4 %collective-permute-start.3 = (f32[64,128]{1,0:T(8,128)S(1)}, f32[64,128]{1,0:T(8,128)S(1)}, u32[]{:S(2)}, u32[]{:S(2)}) collective-permute-start(f32[64,128]{1,0:T(8,128)S(1)} %pad_maximum_fusion.1), channel_id=1, source_target_pairs={{0,4},{4,0},{8,12},{12,8},{16,20},{20,16},{24,28},{28,24},{1,5},{5... | collective-permute-start | bytes 98312 | tf_op jit(solution)/shard_map/ppermute | solution.py:586
  10.5 19.4 %collective-permute-start.9 = (f32[1440,128]{1,0:T(8,128)S(1)}, f32[1440,128]{1,0:T(8,128)S(1)}, u32[]{:S(2)}, u32[]{:S(2)}) collective-permute-start(f32[1440,128]{1,0:T(8,128)S(1)} %get-tuple-element.50), channel_id=1, source_target_pairs={{12,16},{16,12},{13,17},{17,13},{14,18},{18,14},{15,19},{19,15}} | collective-permute-start | bytes 2211848 | tf_op jit(solution)/shard_map/ppermute | solution.py:625
  11.2 13.7 %collective-permute-start.5 = (f32[1440,128]{1,0:T(8,128)S(1)}, f32[1440,128]{1,0:T(8,128)S(1)}, u32[]{:S(2)}, u32[]{:S(2)}) collective-permute-start(f32[1440,128]{1,0:T(8,128)S(1)} %get-tuple-element.50), channel_id=1, source_target_pairs={{0,4},{8,12},{16,20},{24,28},{4,0},{12,8},{20,16},{28,24},{1,5},{9... | collective-permute-start | bytes 2211848 | tf_op jit(solution)/shard_map/ppermute | solution.py:624
  11.4 9.9 %collective-permute-start.4 = (f32[1152,128]{1,0:T(8,128)S(1)}, f32[1152,128]{1,0:T(8,128)S(1)}, u32[]{:S(2)}, u32[]{:S(2)}) collective-permute-start(f32[1152,128]{1,0:T(8,128)S(1)} %get-tuple-element.49), channel_id=1, source_target_pairs={{0,4},{8,12},{16,20},{24,28},{4,0},{12,8},{20,16},{28,24},{1,5},{9... | collective-permute-start | bytes 1769480 | tf_op jit(solution)/shard_map/ppermute | solution.py:624
  20.0 9.4 %collective-permute-start.10 = (f32[1152,128]{1,0:T(8,128)S(1)}, f32[1152,128]{1,0:T(8,128)S(1)}, u32[]{:S(2)}, u32[]{:S(2)}) collective-permute-start(f32[1152,128]{1,0:T(8,128)S(1)} %collective-permute-done.1), channel_id=1, source_target_pairs={{28,16},{0,12},{29,17},{1,13},{30,18},{2,14},{31,19},{3,15}} | collective-permute-start | bytes 1769480 | tf_op jit(solution)/shard_map/ppermute | solution.py:640
  21.3 6.9 %collective-permute-start.6 = (f32[2,2688]{1,0:T(2,128)S(1)}, f32[2,2688]{1,0:T(2,128)S(1)}, u32[]{:S(2)}, u32[]{:S(2)}) collective-permute-start(f32[2,2688]{1,0:T(2,128)S(1)} %get-tuple-element.53.first_here), channel_id=1, source_target_pairs={{1,2},{3,0},{2,1},{0,3},{5,6},{7,4},{6,5},{4,7},{9,10},{11,8},{10,... | collective-permute-start | bytes 64520 | tf_op jit(solution)/shard_map/ppermute | solution.py:642
  25.0 3.8 %copy-start.1 = (f32[2,2688]{1,0:T(2,128)S(1)}, f32[2,2688]{1,0:T(2,128)}, u32[]{:S(2)}) copy-start(f32[2,2688]{1,0:T(2,128)} %constant.5.clone.table) | copy-start | bytes 64516
  25.0 3.8 %collective-permute-start.7 = (f32[2,2688]{1,0:T(2,128)S(1)}, f32[2,2688]{1,0:T(2,128)S(1)}, u32[]{:S(2)}, u32[]{:S(2)}) collective-permute-start(f32[2,2688]{1,0:T(2,128)S(1)} %get-tuple-element.54.second_here), channel_id=1, source_target_pairs={{0,1},{2,3},{1,0},{3,2},{4,5},{6,7},{5,4},{7,6},{8,9},{10,11},{9,8... | collective-permute-start | bytes 64520 | tf_op jit(solution)/shard_map/ppermute | solution.py:643
